TPU v7x, 256 devices: a whole 4x4x8 slice. The times are simulated.
256 devices in a mesh: grp: 8 (over x, core), dev: 32 (over z, y).
Axes of the slice: x: 4, y: 4, z: 8, core: 2. Of those that a mesh axis runs over, the one named last changes fastest.
Arguments:
- inputs: bfloat16 [512, 8, 8, 512], P(('grp', 'dev')), may hold values from -6 to 6
- occupancy: int32 [512, 8, 64], P(('grp', 'dev')), may hold values 0 or 1
- neighbours: int32 [512, 26], P(('grp', 'dev')), may hold values from -1 to 511, as said below
- first_kernel: bfloat16 [1728, 64], replicated, may hold values from -0.15625 to 0.15625
- second_kernel: bfloat16 [1728, 64], replicated, may hold values from -0.15625 to 0.15625
- out_grads: bfloat16 [512, 8, 8, 512], P(('grp', 'dev')), may hold values from -6 to 6
Outputs:
- input_grads: bfloat16 [512, 8, 8, 512], P(('grp', 'dev'))
- first_kernel_grads: float32 [1728, 64], replicated
- second_kernel_grads: float32 [1728, 64], replicated
Inputs may be any that keep to these rules, and one draw needn't show every extreme that they name: `neighbours`: column d names the brick beside brick k in direction d, the 26 directions (d_x, d_y, d_z) in the finite set (-1,0,1)^3 without (0,0,0) in lexicographic order, or -1 where there is no brick; the relation is symmetric and geometric. Brick k lies on device k // 2 of grp+dev, and a named brick lies on a device at most 4 away from brick k's device; that distance occurs in every draw.
All inputs are finite; a program needn't handle non-finite values. No bound on the sum of `occupancy` on one device may be relied on, other than what follows from the above.
Results may differ from a plain program's by a relative error of at most 0.005.
Values may be sent and summed in bfloat16 or wider, within the bound.
No kernel may reach another device: no remote copies, remote signals or barrier semaphores. Data moves between devices by JAX's collectives and lax.ppermute only.
A program may use at most 128 MiB of HBM per device.

v0:
```python
import math

import jax
import jax.numpy as jnp
from jax import lax
from jax.sharding import PartitionSpec as P


def shifted(value, axis, by):
    devices = lax.axis_size(axis)
    pairs = [(i, i + by) for i in range(devices) if 0 <= i + by < devices]
    return lax.ppermute(value, axis, pairs)


def directions():
    result = []
    for along_x in (-1, 0, 1):
        for along_y in (-1, 0, 1):
            for along_z in (-1, 0, 1):
                if along_x != 0 or along_y != 0 or along_z != 0:
                    result.append((along_x, along_y, along_z))
    return result


def source_range(offset, halo_depth, extent):
    if offset > 0:
        return slice(0, halo_depth)
    if offset < 0:
        return slice(extent - halo_depth, extent)
    return slice(0, extent)


def target_range(offset, halo_depth, extent):
    if offset < 0:
        return slice(0, halo_depth)
    if offset > 0:
        return slice(halo_depth + extent, 2 * halo_depth + extent)
    return slice(halo_depth, halo_depth + extent)


def columns(padded, shift_x, extent):
    channels = padded.shape[3]
    pieces = []
    for shift_y in range(3):
        for shift_z in range(3):
            pieces.append(
                padded[
                    shift_x : shift_x + extent,
                    shift_y : shift_y + extent,
                    shift_z : shift_z + extent,
                    :,
                ]
            )
    return jnp.concatenate(pieces, axis=3).reshape(extent * extent * extent, 9 * channels)


def convolve(padded, kernel):
    extent = padded.shape[0] - 2
    block_rows = kernel.shape[0] // 3
    accumulated = jnp.zeros((extent**3, kernel.shape[1]), jnp.float32)
    for shift_x in range(3):
        accumulated = accumulated + jnp.dot(
            columns(padded, shift_x, extent),
            kernel[shift_x * block_rows : (shift_x + 1) * block_rows],
            preferred_element_type=jnp.float32,
        )
    return accumulated


def kernel_grad(padded, gradients):
    extent = padded.shape[0] - 2
    blocks = []
    for shift_x in range(3):
        blocks.append(
            lax.dot_general(
                columns(padded, shift_x, extent),
                gradients,
                (((0,), (0,)), ((), ())),
                preferred_element_type=jnp.float32,
            )
        )
    return jnp.concatenate(blocks, axis=0)


def flipped(kernel):
    channels = kernel.shape[1]
    return jnp.transpose(kernel.reshape(27, channels, channels)[::-1], (0, 2, 1)).reshape(
        27 * channels, channels
    )


def silu_slope(pre_act):
    logistic = jax.nn.sigmoid(pre_act)
    return logistic * (1.0 + pre_act * (1.0 - logistic))


def faces(source_field, halo_depth, upper_side):
    local_bricks = source_field.shape[0]
    extent = source_field.shape[1]
    if upper_side:
        layers = slice(extent - halo_depth, extent)
    else:
        layers = slice(0, halo_depth)
    along_first = source_field[:, layers]
    along_second = jnp.transpose(source_field[:, :, layers], (0, 2, 1, 3, 4))
    along_third = jnp.transpose(source_field[:, :, :, layers], (0, 3, 1, 2, 4))
    return jnp.stack([along_first, along_second, along_third], axis=1).reshape(local_bricks, 3, -1)


def single_shift(highs, lows, distance):
    from_lower = shifted(highs[0], ("grp", "dev"), distance)
    from_upper = shifted(lows[0], ("grp", "dev"), -distance)
    return ((from_lower,), (from_upper,))


def pair_shift(highs, lows, distance):
    from_lower = shifted((highs[0], highs[1]), ("grp", "dev"), distance)
    from_upper = shifted((lows[0], lows[1]), ("grp", "dev"), -distance)
    return (from_lower, from_upper)


def assemble(source_field, high_table, low_table, neighbours, halo_depth, my_device):
    local_bricks = source_field.shape[0]
    extent = source_field.shape[1]
    depth_channels = source_field.shape[4]
    reach_devices = (local_bricks + 6) // local_bricks
    padded_extent = extent + 2 * halo_depth
    padded = jnp.zeros(
        (local_bricks, padded_extent, padded_extent, padded_extent, depth_channels),
        source_field.dtype,
    )
    inner = slice(halo_depth, halo_depth + extent)
    padded = padded.at[:, inner, inner, inner].set(source_field)
    for number, (along_x, along_y, along_z) in enumerate(directions()):
        source = neighbours[:, number]
        present = source >= 0
        owner_device = jnp.maximum(source, 0) // local_bricks
        owner_slot = jnp.maximum(source, 0) - owner_device * local_bricks
        relative = owner_device - my_device
        if along_x != 0:
            face_axis = 0
            leading = along_x
        elif along_y != 0:
            face_axis = 1
            leading = along_y
        else:
            face_axis = 2
            leading = along_z
        if leading < 0:
            table_row = (relative + reach_devices) * local_bricks + owner_slot
            chosen = high_table[:, face_axis]
        else:
            table_row = relative * local_bricks + owner_slot
            chosen = low_table[:, face_axis]
        table_row = jnp.clip(table_row, 0, chosen.shape[0] - 1)
        face_piece = jnp.take(chosen, table_row, axis=0).reshape(
            local_bricks, halo_depth, extent, extent, depth_channels
        )
        if face_axis == 0:
            region = face_piece[
                :,
                :,
                source_range(along_y, halo_depth, extent),
                source_range(along_z, halo_depth, extent),
            ]
        elif face_axis == 1:
            region = jnp.transpose(
                face_piece[:, :, :, source_range(along_z, halo_depth, extent)], (0, 2, 1, 3, 4)
            )
        else:
            region = jnp.transpose(face_piece, (0, 2, 3, 1, 4))
        region = jnp.where(present[:, None, None, None, None], region, jnp.zeros_like(region))
        padded = padded.at[
            :,
            target_range(along_x, halo_depth, extent),
            target_range(along_y, halo_depth, extent),
            target_range(along_z, halo_depth, extent),
        ].set(region)
    return padded


def halo_fields(fields, neighbours, halo_depth, my_device, mover):
    local_bricks = fields[0].shape[0]
    reach_devices = (local_bricks + 6) // local_bricks
    highs = []
    lows = []
    for source_field in fields:
        highs.append(faces(source_field, halo_depth, True))
        lows.append(faces(source_field, halo_depth, False))
    lower_data = []
    upper_data = []
    for distance in range(1, reach_devices + 1):
        from_lower, from_upper = mover(tuple(highs), tuple(lows), distance)
        lower_data.append(from_lower)
        upper_data.append(from_upper)
    results = []
    for member in range(len(fields)):
        high_list = []
        for distance in range(reach_devices, 0, -1):
            high_list.append(lower_data[distance - 1][member])
        high_list.append(highs[member])
        low_list = [lows[member]]
        for distance in range(1, reach_devices + 1):
            low_list.append(upper_data[distance - 1][member])
        high_table = jnp.concatenate(high_list, axis=0)
        low_table = jnp.concatenate(low_list, axis=0)
        results.append(
            assemble(fields[member], high_table, low_table, neighbours, halo_depth, my_device)
        )
    return results


def per_device(inputs, occupancy, neighbours, first_kernel, second_kernel, out_grads):
    local_bricks = inputs.shape[0]
    extent = inputs.shape[1]
    channels = first_kernel.shape[1]
    my_device = lax.axis_index("grp") * lax.axis_size("dev") + lax.axis_index("dev")
    scaling = 1.0 / math.sqrt(
        local_bricks * lax.axis_size("grp") * lax.axis_size("dev") * extent**3
    )
    features = inputs.reshape(local_bricks, extent, extent, extent, channels)
    occupied_cells = occupancy.reshape(local_bricks, extent, extent, extent, 1).astype(jnp.bfloat16)
    masked = out_grads.reshape(local_bricks, extent, extent, extent, channels) * occupied_cells
    occupied = occupancy.reshape(local_bricks, extent**3, 1).astype(jnp.float32)
    first_flip = flipped(first_kernel)
    second_flip = flipped(second_kernel)
    first_sum = jnp.zeros((27 * channels, channels), jnp.float32)
    second_sum = jnp.zeros((27 * channels, channels), jnp.float32)
    grads_list = []
    feature_pad, masked_pad = halo_fields((features, masked), neighbours, 1, my_device, pair_shift)
    pre_list = []
    hidden_list = []
    for brick_slot in range(local_bricks):
        pre_act = convolve(feature_pad[brick_slot], first_kernel)
        pre_list.append(pre_act)
        hidden_list.append((jax.nn.silu(pre_act) * occupied[brick_slot]).astype(jnp.bfloat16))
    hidden = jnp.stack(hidden_list).reshape(local_bricks, extent, extent, extent, channels)
    hidden_pad = halo_fields((hidden,), neighbours, 1, my_device, single_shift)[0]
    pre_grads = []
    for brick_slot in range(local_bricks):
        second_sum = second_sum + kernel_grad(
            hidden_pad[brick_slot], masked[brick_slot].reshape(extent**3, channels)
        )
        hidden_grad = convolve(masked_pad[brick_slot], second_flip)
        pre_grads.append(
            (hidden_grad * silu_slope(pre_list[brick_slot]) * occupied[brick_slot]).astype(
                jnp.bfloat16
            )
        )
    pre_field = jnp.stack(pre_grads).reshape(local_bricks, extent, extent, extent, channels)
    pre_pad = halo_fields((pre_field,), neighbours, 1, my_device, single_shift)[0]
    for brick_slot in range(local_bricks):
        first_sum = first_sum + kernel_grad(feature_pad[brick_slot], pre_grads[brick_slot])
        grads_list.append(
            (convolve(pre_pad[brick_slot], first_flip) * occupied[brick_slot]).astype(jnp.bfloat16)
        )
    first_total, second_total = lax.psum((first_sum, second_sum), ("grp", "dev"))
    input_grads = jnp.stack(grads_list).reshape(local_bricks, extent, extent, extent * channels)
    return (input_grads, first_total * scaling, second_total * scaling)


def solution(mesh):
    in_specs = (
        P(("grp", "dev"), None, None, None),
        P(("grp", "dev"), None, None),
        P(("grp", "dev"), None),
        P(),
        P(),
        P(("grp", "dev"), None, None, None),
    )
    out_specs = (P(("grp", "dev"), None, None, None), P(), P())
    return jax.shard_map(
        per_device, mesh=mesh, in_specs=in_specs, out_specs=out_specs, check_vma=False
    )
```

profile of v0, /device:TPU:1, one launch (start us, length us, event | category | flops | bytes accessed | tf_op | source)
XLA Modules:
  0.0 786.7 jit_solution(12698136321828117083)
XLA Ops:
  9.1 4.4 collective-permute-start.8
  13.5 4.6 collective-permute-start.9
  18.1 3.6 collective-permute-start.10
  21.8 2.6 collective-permute-start.11
  25.7 3.5 collective-permute-start
  73.1 6.4 collective-permute-start.1
  79.6 3.3 collective-permute-start.2
  84.8 7.0 collective-permute-start.12
  93.7 2.8 collective-permute-start.13
  100.4 4.7 collective-permute-start.4
  107.0 4.9 collective-permute-start.5
  113.9 5.3 collective-permute-start.7
  145.0 3.2 concatenate.392
  258.7 2.2 multiply_convert_fusion
  268.2 4.8 collective-permute-start.25
  274.9 2.5 collective-permute-start.27
  284.3 2.2 concatenate.403
  293.2 2.1 concatenate.394
  297.5 2.1 concatenate.395
  310.6 2.3 collective-permute-start.16
  321.8 5.0 collective-permute-start.17
  326.7 2.7 collective-permute-start.18
  331.4 7.0 collective-permute-start.28
  338.4 3.2 concatenate.417
  341.7 3.4 collective-permute-start.29
  345.1 2.6 collective-permute-start.30
  347.8 4.2 collective-permute-start.31
  352.0 5.1 collective-permute-start.20
  358.9 4.9 collective-permute-start.21
  365.8 5.1 collective-permute-start.23
  394.3 3.2 concatenate.408
  525.9 251.1 %all-reduce.7.cloned.1.call-done = (f32[1728,64]{0,1:T(8,128)}, f32[1728,64]{0,1:T(8,128)}) async-done(((f32[1728,64]{0,1:T(8,128)}, f32[1728,64]{0,1:T(8,128)}), (f32[1728,64]{0,1:T(8,128)}, f32[1728,64]{0,1:T(8,128)})) %all-reduce.7.cloned.1.call-update) | async-done | bytes 884752 | tf_op jit(solution)/shard_map/psum | solution.py:257
  (1217 shorter events, 396.1 us)
Async XLA Ops:
  7.2 769.8 %all-reduce.7.cloned.1.call-start = ((), (), s32[]{:S(2)}) async-start(), calls=%async_computation | async-start | bytes 1835008 | tf_op jit(solution)/shard_map/psum | solution.py:257
  9.1 64.0 %collective-permute-start.8 = (bf16[2,3,4096]{2,0,1:T(2,128)(2,1)S(1)}, bf16[2,3,4096]{2,0,1:T(2,128)(2,1)S(1)}, u32[]{:S(2)}, u32[]{:S(2)}) collective-permute-start(bf16[2,3,4096]{2,0,1:T(2,128)(2,1)S(1)} %constant_dynamic-update-slice_fusion.6), channel_id=1, source_target_pairs={{0,4},{1,5},{2,6},{3,7},{4,8},{5,9},{6,10},{7,11},{8,12},{9,13},{1... | collective-permute-start | bytes 147464 | tf_op jit(solution)/shard_map/ppermute | solution.py:12
  13.5 66.1 %collective-permute-start.9 = (bf16[2,3,4096]{2,0,1:T(2,128)(2,1)S(1)}, bf16[2,3,4096]{2,0,1:T(2,128)(2,1)S(1)}, u32[]{:S(2)}, u32[]{:S(2)}) collective-permute-start(bf16[2,3,4096]{2,0,1:T(2,128)(2,1)S(1)} %constant_dynamic-update-slice_fusion.6), channel_id=1, source_target_pairs={{0,3},{1,4},{2,5},{3,6},{4,7},{5,8},{6,9},{7,10},{8,11},{9,12},{10... | collective-permute-start | bytes 147464 | tf_op jit(solution)/shard_map/ppermute | solution.py:12
  18.1 64.8 %collective-permute-start.10 = (bf16[2,3,4096]{2,0,1:T(2,128)(2,1)S(1)}, bf16[2,3,4096]{2,0,1:T(2,128)(2,1)}, u32[]{:S(2)}, u32[]{:S(2)}) collective-permute-start(bf16[2,3,4096]{2,0,1:T(2,128)(2,1)S(1)} %constant_dynamic-update-slice_fusion.6), channel_id=1, source_target_pairs={{0,2},{1,3},{2,4},{3,5},{4,6},{5,7},{6,8},{7,9},{8,10},{9,11},{10,... | collective-permute-start | bytes 147464 | tf_op jit(solution)/shard_map/ppermute | solution.py:12
  21.8 63.1 %collective-permute-start.11 = (bf16[2,3,4096]{2,0,1:T(2,128)(2,1)S(1)}, bf16[2,3,4096]{2,0,1:T(2,128)(2,1)}, u32[]{:S(2)}, u32[]{:S(2)}) collective-permute-start(bf16[2,3,4096]{2,0,1:T(2,128)(2,1)S(1)} %constant_dynamic-update-slice_fusion.6), channel_id=1, source_target_pairs={{0,1},{1,2},{2,3},{3,4},{4,5},{5,6},{6,7},{7,8},{8,9},{9,10},{10,1... | collective-permute-start | bytes 147464 | tf_op jit(solution)/shard_map/ppermute | solution.py:12
  25.7 68.0 %collective-permute-start = (bf16[2,3,4096]{2,0,1:T(2,128)(2,1)S(1)}, bf16[2,3,4096]{2,0,1:T(2,128)(2,1)}, u32[]{:S(2)}, u32[]{:S(2)}) collective-permute-start(bf16[2,3,4096]{2,0,1:T(2,128)(2,1)S(1)} %constant_dynamic-update-slice_fusion), channel_id=1, source_target_pairs={{0,4},{1,5},{2,6},{3,7},{4,8},{5,9},{6,10},{7,11},{8,12},{9,13},{1... | collective-permute-start | bytes 147464 | tf_op jit(solution)/shard_map/ppermute | solution.py:12
  73.1 23.4 %collective-permute-start.1 = (bf16[2,3,4096]{2,0,1:T(2,128)(2,1)S(1)}, bf16[2,3,4096]{2,0,1:T(2,128)(2,1)S(1)}, u32[]{:S(2)}, u32[]{:S(2)}) collective-permute-start(bf16[2,3,4096]{2,0,1:T(2,128)(2,1)S(1)} %constant_dynamic-update-slice_fusion), channel_id=1, source_target_pairs={{0,3},{1,4},{2,5},{3,6},{4,7},{5,8},{6,9},{7,10},{8,11},{9,12},{10... | collective-permute-start | bytes 147464 | tf_op jit(solution)/shard_map/ppermute | solution.py:12
  79.6 18.9 %collective-permute-start.2 = (bf16[2,3,4096]{2,0,1:T(2,128)(2,1)S(1)}, bf16[2,3,4096]{2,0,1:T(2,128)(2,1)S(1)}, u32[]{:S(2)}, u32[]{:S(2)}) collective-permute-start(bf16[2,3,4096]{2,0,1:T(2,128)(2,1)S(1)} %constant_dynamic-update-slice_fusion), channel_id=1, source_target_pairs={{0,2},{1,3},{2,4},{3,5},{4,6},{5,7},{6,8},{7,9},{8,10},{9,11},{10,... | collective-permute-start | bytes 147464 | tf_op jit(solution)/shard_map/ppermute | solution.py:12
  82.9 17.5 %collective-permute-start.3 = (bf16[2,3,4096]{2,0,1:T(2,128)(2,1)S(1)}, bf16[2,3,4096]{2,0,1:T(2,128)(2,1)S(1)}, u32[]{:S(2)}, u32[]{:S(2)}) collective-permute-start(bf16[2,3,4096]{2,0,1:T(2,128)(2,1)S(1)} %constant_dynamic-update-slice_fusion), channel_id=1, source_target_pairs={{0,1},{1,2},{2,3},{3,4},{4,5},{5,6},{6,7},{7,8},{8,9},{9,10},{10,1... | collective-permute-start | bytes 147464 | tf_op jit(solution)/shard_map/ppermute | solution.py:12
  84.8 22.1 %collective-permute-start.12 = (bf16[2,3,4096]{2,0,1:T(2,128)(2,1)S(1)}, bf16[2,3,4096]{2,0,1:T(2,128)(2,1)S(1)}, u32[]{:S(2)}, u32[]{:S(2)}) collective-permute-start(bf16[2,3,4096]{2,0,1:T(2,128)(2,1)S(1)} %constant_dynamic-update-slice_fusion.9), channel_id=1, source_target_pairs={{1,0},{2,1},{3,2},{4,3},{5,4},{6,5},{7,6},{8,7},{9,8},{10,9},{11,1... | collective-permute-start | bytes 147464 | tf_op jit(solution)/shard_map/ppermute | solution.py:12
  93.7 18.2 %collective-permute-start.13 = (bf16[2,3,4096]{2,0,1:T(2,128)(2,1)S(1)}, bf16[2,3,4096]{2,0,1:T(2,128)(2,1)S(1)}, u32[]{:S(2)}, u32[]{:S(2)}) collective-permute-start(bf16[2,3,4096]{2,0,1:T(2,128)(2,1)S(1)} %constant_dynamic-update-slice_fusion.9), channel_id=1, source_target_pairs={{2,0},{3,1},{4,2},{5,3},{6,4},{7,5},{8,6},{9,7},{10,8},{11,9},{12,... | collective-permute-start | bytes 147464 | tf_op jit(solution)/shard_map/ppermute | solution.py:12
  98.5 20.7 %collective-permute-start.15 = (bf16[2,3,4096]{2,0,1:T(2,128)(2,1)S(1)}, bf16[2,3,4096]{2,0,1:T(2,128)(2,1)}, u32[]{:S(2)}, u32[]{:S(2)}) collective-permute-start(bf16[2,3,4096]{2,0,1:T(2,128)(2,1)S(1)} %constant_dynamic-update-slice_fusion.9), channel_id=1, source_target_pairs={{4,0},{5,1},{6,2},{7,3},{8,4},{9,5},{10,6},{11,7},{12,8},{13,9},{1... | collective-permute-start | bytes 147464 | tf_op jit(solution)/shard_map/ppermute | solution.py:12
  100.4 44.6 %collective-permute-start.4 = (bf16[2,3,4096]{2,0,1:T(2,128)(2,1)S(1)}, bf16[2,3,4096]{2,0,1:T(2,128)(2,1)}, u32[]{:S(2)}, u32[]{:S(2)}) collective-permute-start(bf16[2,3,4096]{2,0,1:T(2,128)(2,1)S(1)} %constant_dynamic-update-slice_fusion.3), channel_id=1, source_target_pairs={{1,0},{2,1},{3,2},{4,3},{5,4},{6,5},{7,6},{8,7},{9,8},{10,9},{11,1... | collective-permute-start | bytes 147464 | tf_op jit(solution)/shard_map/ppermute | solution.py:12
  107.0 38.0 %collective-permute-start.5 = (bf16[2,3,4096]{2,0,1:T(2,128)(2,1)S(1)}, bf16[2,3,4096]{2,0,1:T(2,128)(2,1)}, u32[]{:S(2)}, u32[]{:S(2)}) collective-permute-start(bf16[2,3,4096]{2,0,1:T(2,128)(2,1)S(1)} %constant_dynamic-update-slice_fusion.3), channel_id=1, source_target_pairs={{2,0},{3,1},{4,2},{5,3},{6,4},{7,5},{8,6},{9,7},{10,8},{11,9},{12,... | collective-permute-start | bytes 147464 | tf_op jit(solution)/shard_map/ppermute | solution.py:12
  111.9 33.1 %collective-permute-start.6 = (bf16[2,3,4096]{2,0,1:T(2,128)(2,1)S(1)}, bf16[2,3,4096]{2,0,1:T(2,128)(2,1)}, u32[]{:S(2)}, u32[]{:S(2)}) collective-permute-start(bf16[2,3,4096]{2,0,1:T(2,128)(2,1)S(1)} %constant_dynamic-update-slice_fusion.3), channel_id=1, source_target_pairs={{3,0},{4,1},{5,2},{6,3},{7,4},{8,5},{9,6},{10,7},{11,8},{12,9},{13... | collective-permute-start | bytes 147464 | tf_op jit(solution)/shard_map/ppermute | solution.py:12
  113.9 31.1 %collective-permute-start.7 = (bf16[2,3,4096]{2,0,1:T(2,128)(2,1)S(1)}, bf16[2,3,4096]{2,0,1:T(2,128)(2,1)}, u32[]{:S(2)}, u32[]{:S(2)}) collective-permute-start(bf16[2,3,4096]{2,0,1:T(2,128)(2,1)S(1)} %constant_dynamic-update-slice_fusion.3), channel_id=1, source_target_pairs={{4,0},{5,1},{6,2},{7,3},{8,4},{9,5},{10,6},{11,7},{12,8},{13,9},{1... | collective-permute-start | bytes 147464 | tf_op jit(solution)/shard_map/ppermute | solution.py:12
  266.2 55.5 %collective-permute-start.24 = (bf16[2,3,4096]{2,0,1:T(2,128)(2,1)}, bf16[2,3,4096]{2,0,1:T(2,128)(2,1)}, u32[]{:S(2)}, u32[]{:S(2)}) collective-permute-start(bf16[2,3,4096]{2,0,1:T(2,128)(2,1)} %constant_dynamic-update-slice_fusion.18), channel_id=1, source_target_pairs={{0,4},{1,5},{2,6},{3,7},{4,8},{5,9},{6,10},{7,11},{8,12},{9,13},{1... | collective-permute-start | bytes 147464 | tf_op jit(solution)/shard_map/ppermute | solution.py:12
  268.2 58.6 %collective-permute-start.25 = (bf16[2,3,4096]{2,0,1:T(2,128)(2,1)}, bf16[2,3,4096]{2,0,1:T(2,128)(2,1)}, u32[]{:S(2)}, u32[]{:S(2)}) collective-permute-start(bf16[2,3,4096]{2,0,1:T(2,128)(2,1)} %constant_dynamic-update-slice_fusion.18), channel_id=1, source_target_pairs={{0,3},{1,4},{2,5},{3,6},{4,7},{5,8},{6,9},{7,10},{8,11},{9,12},{10... | collective-permute-start | bytes 147464 | tf_op jit(solution)/shard_map/ppermute | solution.py:12
  273.0 56.5 %collective-permute-start.26 = (bf16[2,3,4096]{2,0,1:T(2,128)(2,1)}, bf16[2,3,4096]{2,0,1:T(2,128)(2,1)}, u32[]{:S(2)}, u32[]{:S(2)}) collective-permute-start(bf16[2,3,4096]{2,0,1:T(2,128)(2,1)} %constant_dynamic-update-slice_fusion.18), channel_id=1, source_target_pairs={{0,2},{1,3},{2,4},{3,5},{4,6},{5,7},{6,8},{7,9},{8,10},{9,11},{10,... | collective-permute-start | bytes 147464 | tf_op jit(solution)/shard_map/ppermute | solution.py:12
  274.9 56.5 %collective-permute-start.27 = (bf16[2,3,4096]{2,0,1:T(2,128)(2,1)}, bf16[2,3,4096]{2,0,1:T(2,128)(2,1)}, u32[]{:S(2)}, u32[]{:S(2)}) collective-permute-start(bf16[2,3,4096]{2,0,1:T(2,128)(2,1)} %constant_dynamic-update-slice_fusion.18), channel_id=1, source_target_pairs={{0,1},{1,2},{2,3},{3,4},{4,5},{5,6},{6,7},{7,8},{8,9},{9,10},{10,1... | collective-permute-start | bytes 147464 | tf_op jit(solution)/shard_map/ppermute | solution.py:12
  310.6 31.1 %collective-permute-start.16 = (bf16[2,3,4096]{2,0,1:T(2,128)(2,1)S(1)}, bf16[2,3,4096]{2,0,1:T(2,128)(2,1)}, u32[]{:S(2)}, u32[]{:S(2)}) collective-permute-start(bf16[2,3,4096]{2,0,1:T(2,128)(2,1)S(1)} %constant_dynamic-update-slice_fusion.12), channel_id=1, source_target_pairs={{0,4},{1,5},{2,6},{3,7},{4,8},{5,9},{6,10},{7,11},{8,12},{9,13},{1... | collective-permute-start | bytes 147464 | tf_op jit(solution)/shard_map/ppermute | solution.py:12
  321.8 23.4 %collective-permute-start.17 = (bf16[2,3,4096]{2,0,1:T(2,128)(2,1)S(1)}, bf16[2,3,4096]{2,0,1:T(2,128)(2,1)S(1)}, u32[]{:S(2)}, u32[]{:S(2)}) collective-permute-start(bf16[2,3,4096]{2,0,1:T(2,128)(2,1)S(1)} %constant_dynamic-update-slice_fusion.12), channel_id=1, source_target_pairs={{0,3},{1,4},{2,5},{3,6},{4,7},{5,8},{6,9},{7,10},{8,11},{9,12},{10... | collective-permute-start | bytes 147464 | tf_op jit(solution)/shard_map/ppermute | solution.py:12
  326.7 21.0 %collective-permute-start.18 = (bf16[2,3,4096]{2,0,1:T(2,128)(2,1)S(1)}, bf16[2,3,4096]{2,0,1:T(2,128)(2,1)S(1)}, u32[]{:S(2)}, u32[]{:S(2)}) collective-permute-start(bf16[2,3,4096]{2,0,1:T(2,128)(2,1)S(1)} %constant_dynamic-update-slice_fusion.12), channel_id=1, source_target_pairs={{0,2},{1,3},{2,4},{3,5},{4,6},{5,7},{6,8},{7,9},{8,10},{9,11},{10,... | collective-permute-start | bytes 147464 | tf_op jit(solution)/shard_map/ppermute | solution.py:12
  329.5 22.5 %collective-permute-start.19 = (bf16[2,3,4096]{2,0,1:T(2,128)(2,1)S(1)}, bf16[2,3,4096]{2,0,1:T(2,128)(2,1)S(1)}, u32[]{:S(2)}, u32[]{:S(2)}) collective-permute-start(bf16[2,3,4096]{2,0,1:T(2,128)(2,1)S(1)} %constant_dynamic-update-slice_fusion.12), channel_id=1, source_target_pairs={{0,1},{1,2},{2,3},{3,4},{4,5},{5,6},{6,7},{7,8},{8,9},{9,10},{10,1... | collective-permute-start | bytes 147464 | tf_op jit(solution)/shard_map/ppermute | solution.py:12
  331.4 27.5 %collective-permute-start.28 = (bf16[2,3,4096]{2,0,1:T(2,128)(2,1)}, bf16[2,3,4096]{2,0,1:T(2,128)(2,1)S(1)}, u32[]{:S(2)}, u32[]{:S(2)}) collective-permute-start(bf16[2,3,4096]{2,0,1:T(2,128)(2,1)} %constant_dynamic-update-slice_fusion.21), channel_id=1, source_target_pairs={{1,0},{2,1},{3,2},{4,3},{5,4},{6,5},{7,6},{8,7},{9,8},{10,9},{11,1... | collective-permute-start | bytes 147464 | tf_op jit(solution)/shard_map/ppermute | solution.py:12
  341.7 22.1 %collective-permute-start.29 = (bf16[2,3,4096]{2,0,1:T(2,128)(2,1)}, bf16[2,3,4096]{2,0,1:T(2,128)(2,1)S(1)}, u32[]{:S(2)}, u32[]{:S(2)}) collective-permute-start(bf16[2,3,4096]{2,0,1:T(2,128)(2,1)} %constant_dynamic-update-slice_fusion.21), channel_id=1, source_target_pairs={{2,0},{3,1},{4,2},{5,3},{6,4},{7,5},{8,6},{9,7},{10,8},{11,9},{12,... | collective-permute-start | bytes 147464 | tf_op jit(solution)/shard_map/ppermute | solution.py:12
  345.1 20.7 %collective-permute-start.30 = (bf16[2,3,4096]{2,0,1:T(2,128)(2,1)}, bf16[2,3,4096]{2,0,1:T(2,128)(2,1)S(1)}, u32[]{:S(2)}, u32[]{:S(2)}) collective-permute-start(bf16[2,3,4096]{2,0,1:T(2,128)(2,1)} %constant_dynamic-update-slice_fusion.21), channel_id=1, source_target_pairs={{3,0},{4,1},{5,2},{6,3},{7,4},{8,5},{9,6},{10,7},{11,8},{12,9},{13... | collective-permute-start | bytes 147464 | tf_op jit(solution)/shard_map/ppermute | solution.py:12
  347.8 23.2 %collective-permute-start.31 = (bf16[2,3,4096]{2,0,1:T(2,128)(2,1)}, bf16[2,3,4096]{2,0,1:T(2,128)(2,1)S(1)}, u32[]{:S(2)}, u32[]{:S(2)}) collective-permute-start(bf16[2,3,4096]{2,0,1:T(2,128)(2,1)} %constant_dynamic-update-slice_fusion.21), channel_id=1, source_target_pairs={{4,0},{5,1},{6,2},{7,3},{8,4},{9,5},{10,6},{11,7},{12,8},{13,9},{1... | collective-permute-start | bytes 147464 | tf_op jit(solution)/shard_map/ppermute | solution.py:12
  352.0 41.0 %collective-permute-start.20 = (bf16[2,3,4096]{2,0,1:T(2,128)(2,1)}, bf16[2,3,4096]{2,0,1:T(2,128)(2,1)S(1)}, u32[]{:S(2)}, u32[]{:S(2)}) collective-permute-start(bf16[2,3,4096]{2,0,1:T(2,128)(2,1)} %constant_dynamic-update-slice_fusion.15), channel_id=1, source_target_pairs={{1,0},{2,1},{3,2},{4,3},{5,4},{6,5},{7,6},{8,7},{9,8},{10,9},{11,1... | collective-permute-start | bytes 147464 | tf_op jit(solution)/shard_map/ppermute | solution.py:12
  358.9 34.1 %collective-permute-start.21 = (bf16[2,3,4096]{2,0,1:T(2,128)(2,1)}, bf16[2,3,4096]{2,0,1:T(2,128)(2,1)S(1)}, u32[]{:S(2)}, u32[]{:S(2)}) collective-permute-start(bf16[2,3,4096]{2,0,1:T(2,128)(2,1)} %constant_dynamic-update-slice_fusion.15), channel_id=1, source_target_pairs={{2,0},{3,1},{4,2},{5,3},{6,4},{7,5},{8,6},{9,7},{10,8},{11,9},{12,... | collective-permute-start | bytes 147464 | tf_op jit(solution)/shard_map/ppermute | solution.py:12
  363.9 29.2 %collective-permute-start.22 = (bf16[2,3,4096]{2,0,1:T(2,128)(2,1)}, bf16[2,3,4096]{2,0,1:T(2,128)(2,1)S(1)}, u32[]{:S(2)}, u32[]{:S(2)}) collective-permute-start(bf16[2,3,4096]{2,0,1:T(2,128)(2,1)} %constant_dynamic-update-slice_fusion.15), channel_id=1, source_target_pairs={{3,0},{4,1},{5,2},{6,3},{7,4},{8,5},{9,6},{10,7},{11,8},{12,9},{13... | collective-permute-start | bytes 147464 | tf_op jit(solution)/shard_map/ppermute | solution.py:12
  365.8 28.5 %collective-permute-start.23 = (bf16[2,3,4096]{2,0,1:T(2,128)(2,1)}, bf16[2,3,4096]{2,0,1:T(2,128)(2,1)}, u32[]{:S(2)}, u32[]{:S(2)}) collective-permute-start(bf16[2,3,4096]{2,0,1:T(2,128)(2,1)} %constant_dynamic-update-slice_fusion.15), channel_id=1, source_target_pairs={{4,0},{5,1},{6,2},{7,3},{8,4},{9,5},{10,6},{11,7},{12,8},{13,9},{1... | collective-permute-start | bytes 147464 | tf_op jit(solution)/shard_map/ppermute | solution.py:12
  (249 other events, 296.6 us)
Sparse Core Ops, SparseCore 0:
  521.2 255.7 all-reduce.6
where the time goes:
time: 800 us; the launch traced here: 787 us
  local copies, waits for them, and re-layouts  301 us (38%)
  waiting for transfers between devices  251 us (31%)
  starting transfers between devices  118 us (15%)
  other arithmetic  64.7 us (8%)
  matrix products  33.1 us (4%)
  between operations  18.1 us (2%)
    psum x1, waiting for transfers between devices, per_device(): lax.psum((first_sum, second_sum), ('grp', 'dev'))  251 us
    ppermute x32, starting transfers between devices, shifted(): return lax.ppermute(value, axis, pairs)  118 us
    gather x104, local copies, waits for them, and re-layouts, assemble(): jnp.take(chosen, table_row, axis=0)  87.7 us
    unnamed x512, local copies, waits for them, and re-layouts  76.6 us
    concatenate x24, local copies, waits for them, and re-layouts, columns(): jnp.concatenate(pieces, axis=3)  33.2 us
    dot_general x18, matrix products, convolve(): jnp.dot(columns(padded, shift_x, extent), kernel[shift_x * block_rows:(sh...  27.4 us
    scatter x104, local copies, waits for them, and re-layouts, assemble(): padded = padded.at[:, target_range(along_x, halo_depth, extent), target_r...  26 us
    slice x16, local copies, waits for them, and re-layouts, columns(): padded[shift_x:shift_x + extent, shift_y:shift_y + extent, shift_z:shift_...  19.6 us
  transfers between devices with their start and end apart: 33, of which 1 were waited for; matrix products, arithmetic and copies ran while one was open for 18% of the time, Pallas kernels for 0%

commit v1 on v0

v1 whole, which is shorter than its diff:
```python
import functools
import math

import jax
import jax.numpy as jnp
from jax import lax
from jax.experimental import pallas as pl
from jax.experimental.pallas import tpu as pltpu
from jax.sharding import PartitionSpec as P

AXES = ("grp", "dev")
GROUP = 8
EDGE = 8
WIDE = 512
PADDED = 640
ROWS = 24
PACKED = 2048
BF16 = jnp.bfloat16
F32 = jnp.float32


def directions():
    result = []
    for along_x in (-1, 0, 1):
        for along_y in (-1, 0, 1):
            for along_z in (-1, 0, 1):
                if along_x != 0 or along_y != 0 or along_z != 0:
                    result.append((along_x, along_y, along_z))
    return result


DIRECTIONS = directions()
NUMBER = {offset: number for number, offset in enumerate(DIRECTIONS)}


def locate(nb_ref, me, brick, number):
    other = nb_ref[brick, number]
    present = other >= 0
    owner = jnp.maximum(other, 0) >> 1
    same = (owner >> 3) == (me >> 3)
    box = jnp.where(same, owner & 7, 8 + ((owner + 4) & 7))
    return present, box, other & 1


def send_place(nb_ref, me, brick, number):
    present, box, slot = locate(nb_ref, me, brick, number)
    unused = (8 + ((me + 4) & 7)) * 4
    return jnp.where(present, box * 4 + brick * 2 + slot, unused)


def face_kind(offset):
    for axis in range(3):
        if offset[axis] != 0:
            return axis, 1 if offset[axis] > 0 else 0


def face_values(wide, index):
    faces = {}
    for side, at in ((0, 0), (1, EDGE - 1)):
        faces[0, side] = wide[index, at * EDGE : (at + 1) * EDGE, :]
        faces[1, side] = jnp.concatenate(
            [wide[index, x * EDGE + at : x * EDGE + at + 1, :] for x in range(EDGE)], axis=0
        )
        faces[2, side] = jnp.concatenate(
            [
                wide[index, x * EDGE : (x + 1) * EDGE, at * 64 : (at + 1) * 64]
                for x in range(EDGE)
            ],
            axis=1,
        )
    return faces


def spread(occ_ref):
    rows = []
    for x in range(EDGE):
        for brick in range(2):
            rows.append(jnp.broadcast_to(occ_ref[brick, x : x + 1, :].astype(F32), (EDGE, 64)))
    stacked = jnp.concatenate(rows, axis=0)
    row = lax.broadcasted_iota(jnp.int32, stacked.shape, 0)
    lane = lax.broadcasted_iota(jnp.int32, stacked.shape, 1)
    own = jnp.where((row & 7) == (lane >> 3), stacked, 0.0).astype(BF16)
    source = lax.broadcasted_iota(jnp.int32, (64, WIDE), 0)
    target = lax.broadcasted_iota(jnp.int32, (64, WIDE), 1)
    select = jnp.where((source & 7) == (target >> 6), 1.0, 0.0).astype(BF16)
    return jnp.dot(own, select, preferred_element_type=F32)


def pack_kernel(
    me_ref, nb_ref, x_ref, g_ref, occ_ref, even_ref, odd_ref, masked_ref, wide, boxes
):
    me = me_ref[0]
    occupied = spread(occ_ref)
    for x in range(EDGE):
        both = []
        for brick in range(2):
            wide[brick, x * EDGE : (x + 1) * EDGE, :] = x_ref[brick, x].astype(F32)
            at = (2 * x + brick) * EDGE
            piece = g_ref[brick, x].astype(F32) * occupied[at : at + EDGE]
            wide[2 + brick, x * EDGE : (x + 1) * EDGE, :] = piece
            both.append(piece)
        masked_ref[x] = jnp.concatenate(both, axis=0).astype(BF16)
    for brick in range(2):
        first = face_values(wide, brick)
        second = face_values(wide, 2 + brick)
        packets = {}
        for key in first:
            packets[key] = jnp.concatenate([first[key], second[key]], axis=0).astype(BF16)
        for number, offset in enumerate(DIRECTIONS):
            boxes[send_place(nb_ref, me, brick, number)] = packets[face_kind(offset)]
    even_ref[...] = boxes[0:32].reshape(8, 4, 16, WIDE)
    odd_ref[...] = boxes[32:64].reshape(8, 4, 16, WIDE)


def beside(low, middle, high):
    return jnp.concatenate([low, middle, high], axis=1)


def fill_padded(padded, own, pick):
    def planes(along_x, along_y):
        return (
            pick((along_x, along_y, -1))[:, WIDE - 64 :],
            pick((along_x, along_y, 0)),
            pick((along_x, along_y, 1))[:, :64],
        )

    below, above = pick((0, 0, -1)), pick((0, 0, 1))
    for x in range(EDGE):
        lanes = slice(x * 64, (x + 1) * 64)
        start = (x + 1) * ROWS + 8
        padded[start : start + EDGE, :] = beside(below[:, lanes], own(x), above[:, lanes])
    for along_y, row in ((-1, 7), (1, 16)):
        value = beside(*planes(0, along_y))
        for x in range(EDGE):
            start = (x + 1) * ROWS + row
            padded[start : start + 1, :] = value[x : x + 1]
    for along_x, at in ((-1, 0), (1, 9)):
        start = at * ROWS + 8
        padded[start : start + EDGE, :] = beside(*planes(along_x, 0))
        for along_y, row, source in ((-1, 7, 7), (1, 16, 0)):
            value = beside(*planes(along_x, along_y))
            padded[at * ROWS + row : at * ROWS + row + 1, :] = value[source : source + 1]


def fill_windows(first, second, shifted, windows):
    for along_y in range(3):
        for x in range(10):
            start = x * ROWS + 7 + along_y
            shifted[along_y, x] = jnp.concatenate(
                [first[start : start + EDGE, :], second[start : start + EDGE, :]], axis=0
            ).astype(BF16)
    for pair in range(4):
        for along_x in range(3):
            for along_y in range(3):
                place = (3 * along_x + along_y) * 256
                windows[pair * 128 : (pair + 1) * 128, place : place + 256] = shifted[
                    along_y, along_x : along_x + EDGE, :, pair * 128 : pair * 128 + 256
                ].reshape(128, 256)


def fill_direct(kernel_ref, direct):
    for group in range(9):
        block = kernel_ref[group * 192 : (group + 1) * 192, :]
        none = jnp.zeros((64, 64), BF16)
        direct[group * 256 : (group + 1) * 256, :] = jnp.concatenate(
            [
                jnp.concatenate([block, none], axis=0),
                jnp.concatenate([none, block], axis=0),
            ],
            axis=1,
        )


def fill_flipped(kernel_ref, flipped):
    none = jnp.zeros((64, 64), BF16)
    for group in range(9):
        base = 3 * (8 - group)
        blocks = [kernel_ref[(base + z) * 64 : (base + z + 1) * 64, :] for z in (2, 1, 0)]
        lanes = slice(group * 256, (group + 1) * 256)
        flipped[0:64, lanes] = jnp.concatenate(blocks + [none], axis=1)
        flipped[64:128, lanes] = jnp.concatenate([none] + blocks, axis=1)


def times_flipped(windows, flipped):
    return lax.dot_general(
        windows, flipped, (((1,), (1,)), ((), ())), preferred_element_type=F32
    )


def paired(natural):
    return jnp.concatenate([natural[:, p * 128 : (p + 1) * 128] for p in range(4)], axis=0)


def unpaired(value):
    return jnp.concatenate([value[p * 128 : (p + 1) * 128] for p in range(4)], axis=1)


def gather_blocks(product):
    pieces = []
    for group in range(9):
        at = group * 256
        pieces.append(product[0:64, at : at + 192] + product[64:128, at + 64 : at + 256])
    pieces.append(jnp.zeros((64, PACKED - 27 * 64), F32))
    return jnp.concatenate(pieces, axis=1)


def main_kernel(
    me_ref,
    nb_ref,
    x_ref,
    masked_ref,
    occ_ref,
    even_in,
    odd_in,
    first_ref,
    second_ref,
    grads_ref,
    even_ref,
    odd_ref,
    padded,
    shifted,
    windows,
    direct,
    flipped,
    product,
    wide,
    boxes,
):
    me = me_ref[0]
    for brick in range(2):
        values = {}
        for number, offset in enumerate(DIRECTIONS):
            present, box, slot = locate(nb_ref, me, brick, number)
            place = slot * 2 + brick
            low = even_in[box & 7, place].astype(F32)
            high = odd_in[box & 7, place].astype(F32)
            values[offset] = jnp.where(present, jnp.where(box < 8, low, high), 0.0)

        def own_first(x):
            return x_ref[brick, x].astype(F32)

        def own_second(x):
            return masked_ref[x].astype(F32)[brick * EDGE : (brick + 1) * EDGE]

        fill_padded(padded.at[0, brick], own_first, lambda offset: values[offset][0:8])
        fill_padded(padded.at[1, brick], own_second, lambda offset: values[offset][8:16])
    for field in range(2):
        fill_windows(padded.at[field, 0], padded.at[field, 1], shifted.at[field], windows.at[field])
    fill_direct(first_ref, direct)
    fill_flipped(second_ref, flipped)
    occupied = paired(spread(occ_ref))
    pre_act = jnp.dot(windows[0], direct[...], preferred_element_type=F32)
    logistic = 1.0 / (1.0 + jnp.exp(-pre_act))
    hidden = (pre_act * logistic * occupied).astype(BF16)
    slope = logistic * (1.0 + pre_act * (1.0 - logistic))
    hidden_grad = times_flipped(windows[1], flipped[...])
    pre_grads = (hidden_grad * slope * occupied).astype(BF16)

    natural = unpaired(pre_grads.astype(F32))
    for x in range(EDGE):
        grads_ref[x] = natural[16 * x : 16 * x + 16].astype(BF16)
        for brick in range(2):
            at = 16 * x + EDGE * brick
            wide[brick, x * EDGE : (x + 1) * EDGE, :] = natural[at : at + EDGE]
    for brick in range(2):
        faces = face_values(wide, brick)
        for number, offset in enumerate(DIRECTIONS):
            boxes[send_place(nb_ref, me, brick, number)] = faces[face_kind(offset)]
    for box in range(8):
        even_ref[box, 0:32, :] = boxes[4 * box : 4 * box + 4].reshape(32, WIDE).astype(BF16)
        odd_ref[box] = boxes[32 + 4 * box : 36 + 4 * box].reshape(32, WIDE).astype(BF16)

    for half, own, field in ((0, hidden, 1), (1, pre_grads, 0)):
        turned = own.astype(F32).T.astype(BF16)
        product[...] = jnp.dot(turned, windows[field], preferred_element_type=F32)
        packed = gather_blocks(product).astype(BF16)
        for chunk in range(4):
            for part in range(4):
                at = 32 + 16 * part
                even_ref[4 * half + chunk, at : at + 16, :] = packed[
                    16 * chunk : 16 * chunk + 16, part * WIDE : (part + 1) * WIDE
                ]


def first_sum_kernel(parts_ref, tiles_ref):
    total = parts_ref[0, 32:96, :].astype(F32)
    for member in range(1, GROUP):
        total = total + parts_ref[member, 32:96, :].astype(F32)
    for down in range(8):
        for along in range(4):
            tiles_ref[4 * down + along] = total[
                8 * down : 8 * down + 8, 128 * along : 128 * along + 128
            ]


def second_sum_kernel(scaling, parts_ref, tiles_ref):
    members = parts_ref.shape[0]
    total = parts_ref[0]
    for member in range(1, members):
        total = total + parts_ref[member]
    total = total * scaling
    for member in range(members):
        tiles_ref[member] = total


def share_kernel(tiles_ref, odd_ref, out_ref):
    rows = []
    for down in range(8):
        rows.append(
            jnp.concatenate([tiles_ref[4 * down + along] for along in range(4)], axis=1)
        )
    chunk = jnp.concatenate(rows, axis=0).astype(BF16)
    for member in range(GROUP):
        out_ref[member, 0:32, :] = odd_ref[member]
        out_ref[member, 32:96, :] = chunk


def last_kernel(
    me_ref,
    nb_ref,
    grads_ref,
    occ_ref,
    even_in,
    odd_in,
    first_ref,
    out_ref,
    first_out,
    second_out,
    padded,
    shifted,
    windows,
    flipped,
    boxes,
):
    me = me_ref[0]
    for box in range(8):
        boxes[4 * box : 4 * box + 4] = (
            even_in[box, 0:32, :].astype(F32).reshape(4, EDGE, WIDE)
        )
        boxes[32 + 4 * box : 36 + 4 * box] = (
            odd_in[box, 0:32, :].astype(F32).reshape(4, EDGE, WIDE)
        )
    for brick in range(2):
        values = {}
        for number, offset in enumerate(DIRECTIONS):
            present, box, slot = locate(nb_ref, me, brick, number)
            values[offset] = jnp.where(present, boxes[4 * box + slot * 2 + brick], 0.0)

        def own(x):
            return grads_ref[x].astype(F32)[brick * EDGE : (brick + 1) * EDGE]

        fill_padded(padded.at[brick], own, lambda offset: values[offset])
    fill_windows(padded.at[0], padded.at[1], shifted, windows)
    fill_flipped(first_ref, flipped)
    result = unpaired(times_flipped(windows[...], flipped[...])) * spread(occ_ref)
    for x in range(EDGE):
        for brick in range(2):
            at = 16 * x + EDGE * brick
            out_ref[brick, x] = result[at : at + EDGE].astype(BF16)

    halves = []
    for half in range(2):
        rows = []
        for chunk in range(4 * half, 4 * half + 4):
            slot = (chunk + 4) & 7
            rows.append(
                jnp.concatenate(
                    [odd_in[slot, 32 + 16 * part : 48 + 16 * part, :] for part in range(4)],
                    axis=1,
                )
            )
        halves.append(jnp.concatenate(rows, axis=0).astype(F32))
    for block in range(27):
        at = (26 - block) * 64
        second_out[at : at + 64, :] = halves[0][:, block * 64 : block * 64 + 64]
    for pair in range(14):
        turned = halves[1][:, pair * 128 : pair * 128 + 128].T
        count = min(128, 27 * 64 - pair * 128)
        first_out[pair * 128 : pair * 128 + count, :] = turned[:count]


def call(kernel, shapes, scratch, arguments, scalars=0, flops=0):
    specs = [pl.BlockSpec(memory_space=pltpu.SMEM)] * scalars
    specs += [pl.BlockSpec(memory_space=pltpu.VMEM)] * (len(arguments) - scalars)
    return pl.pallas_call(
        kernel,
        out_shape=[jax.ShapeDtypeStruct(shape, kind) for shape, kind in shapes],
        in_specs=specs,
        out_specs=[pl.BlockSpec(memory_space=pltpu.VMEM)] * len(shapes),
        scratch_shapes=[pltpu.VMEM(shape, kind) for shape, kind in scratch],
        compiler_params=pltpu.CompilerParams(vmem_limit_bytes=40 * 1024 * 1024),
    )(*arguments)


def per_device(inputs, occupancy, neighbours, first_kernel, second_kernel, out_grads):
    devices = lax.axis_size("grp") * lax.axis_size("dev")
    members = devices // GROUP
    scaling = 1.0 / math.sqrt(inputs.shape[0] * devices * EDGE**3)
    even = [[GROUP * k + j for j in range(GROUP)] for k in range(members)]
    odd = [[(GROUP * k + 4 + j) % devices for j in range(GROUP)] for k in range(members)]
    across = [[GROUP * j + k for j in range(members)] for k in range(GROUP)]
    me = (lax.axis_index("grp") * lax.axis_size("dev") + lax.axis_index("dev")).reshape(1)

    def swap(value, groups):
        return lax.all_to_all(value, AXES, 0, 0, axis_index_groups=groups, tiled=True)

    halo = ((GROUP, 4, 16, WIDE), BF16)
    even_out, odd_out, masked = call(
        pack_kernel,
        [halo, halo, ((EDGE, 16, WIDE), BF16)],
        [((4, 64, WIDE), F32), ((64, 16, WIDE), BF16)],
        [me, neighbours, inputs, out_grads, occupancy],
        scalars=2,
    )
    even_in = swap(even_out, even)
    odd_in = swap(odd_out, odd)
    pre_grads, even_out, odd_out = call(
        main_kernel,
        [
            ((EDGE, 16, WIDE), BF16),
            ((GROUP, 96, WIDE), BF16),
            ((GROUP, 32, WIDE), BF16),
        ],
        [
            ((2, 2, 10 * ROWS, PADDED), F32),
            ((2, 3, 10, 16, PADDED), BF16),
            ((2, 512, 2304), BF16),
            ((2304, 128), BF16),
            ((128, 2304), BF16),
            ((128, 2304), F32),
            ((2, 64, WIDE), F32),
            ((64, EDGE, WIDE), F32),
        ],
        [me, neighbours, inputs, masked, occupancy, even_in, odd_in, first_kernel, second_kernel],
        scalars=2,
    )
    even_in = swap(even_out, even)
    (tiles,) = call(first_sum_kernel, [((32, 8, 128), F32)], [], [even_in])
    across_shape = (members, 32 // members, 8, 128)
    tiles = swap(tiles.reshape(across_shape), across)
    (tiles,) = call(
        functools.partial(second_sum_kernel, scaling), [(across_shape, F32)], [], [tiles]
    )
    tiles = swap(tiles, across).reshape(32, 8, 128)
    (odd_out,) = call(share_kernel, [((GROUP, 96, WIDE), BF16)], [], [tiles, odd_out])
    odd_in = swap(odd_out, odd)
    return tuple(
        call(
            last_kernel,
            [
                ((2, EDGE, EDGE, WIDE), BF16),
                ((27 * 64, 64), F32),
                ((27 * 64, 64), F32),
            ],
            [
                ((2, 10 * ROWS, PADDED), F32),
                ((3, 10, 16, PADDED), BF16),
                ((512, 2304), BF16),
                ((128, 2304), BF16),
                ((64, EDGE, WIDE), F32),
            ],
            [me, neighbours, pre_grads, occupancy, even_in, odd_in, first_kernel],
            scalars=2,
        )
    )


def solution(mesh):
    in_specs = (
        P(("grp", "dev"), None, None, None),
        P(("grp", "dev"), None, None),
        P(("grp", "dev"), None),
        P(),
        P(),
        P(("grp", "dev"), None, None, None),
    )
    out_specs = (P(("grp", "dev"), None, None, None), P(), P())
    return jax.shard_map(
        per_device, mesh=mesh, in_specs=in_specs, out_specs=out_specs, check_vma=False
    )
```

time: 800 us -> 111 us (0.14); the launches traced: 787 us -> 110 us
  local copies, waits for them, and re-layouts: 301 us -> 5.81 us
  waiting for transfers between devices: 251 us -> 7.88 us
  starting transfers between devices: 118 us -> 10.1 us
  blocking collectives: 0 us -> 78 us
  other arithmetic: 64.7 us -> 0 us
  matrix products: 33.1 us -> 0 us
  between operations: 18.1 us -> 0.68 us
    psum x1 -> x0, waiting for transfers between devices: 251 us -> none  [per_device(): lax.psum((first_sum, second_sum), ('grp', 'dev'))]
    ppermute x32 -> x0, starting transfers between devices: 118 us -> none  [shifted(): return lax.ppermute(value, axis, pairs)]
    gather x104 -> x0, local copies, waits for them, and re-layouts: 87.7 us -> none  [assemble(): jnp.take(chosen, table_row, axis=0)]
    all_to_all x0 -> x5, blocking collectives: none -> 78 us  [swap(): lax.all_to_all(value, AXES, 0, 0, axis_index_groups=groups, tiled=True)]
    unnamed x512 -> x16, local copies, waits for them, and re-layouts: 76.6 us -> 3.7 us
    concatenate x36 -> x0, local copies, waits for them, and re-layouts: 53.3 us -> none  [the longest x24 33.2 us: columns(): jnp.concatenate(pieces, axis=3)]
    dot_general x30 -> x0, matrix products: 33.1 us -> none  [the longest x18 27.4 us: convolve(): jnp.dot(columns(padded, shift_x, extent), kernel[shift_x * block_rows:(sh...]
    scatter x108 -> x0, local copies, waits for them, and re-layouts: 26.6 us -> none  [the longest x104 26 us: assemble(): padded = padded.at[:, target_range(along_x, halo_depth, extent), target_r...]
  transfers between devices with their start and end apart: 33 -> 1, of which waited for: 1 -> 1; matrix products, arithmetic and copies ran while one was open for 18% -> 0% of each run, Pallas kernels for 0% -> 0%
where the time goes in v1:
time: 111 us; the launch traced here: 110 us
  blocking collectives  78 us (70%)
  starting transfers between devices  10.1 us (9%)
  waiting for transfers between devices  7.88 us (7%)
  Pallas kernels  7.76 us (7%)
  local copies, waits for them, and re-layouts  5.81 us (5%)
    all_to_all x5, blocking collectives, swap(): lax.all_to_all(value, AXES, 0, 0, axis_index_groups=groups, tiled=True)  78 us
    all_to_all x1, starting transfers between devices, swap(): lax.all_to_all(value, AXES, 0, 0, axis_index_groups=groups, tiled=True)  10.1 us
    all_to_all x1, waiting for transfers between devices, swap(): lax.all_to_all(value, AXES, 0, 0, axis_index_groups=groups, tiled=True)  7.88 us
    pallas_call x6, Pallas kernels, call(): pl.pallas_call(kernel, out_shape=[jax.ShapeDtypeStruct(shape, kind) for s...  7.76 us
    unnamed x16, local copies, waits for them, and re-layouts  3.7 us
  transfers between devices with their start and end apart: 1, of which 1 were waited for; matrix products, arithmetic and copies ran while one was open for 0% of the time, Pallas kernels for 0%

profile of v1, /device:TPU:1, one launch (start us, length us, event | category | flops | bytes accessed | tf_op | source)
XLA Modules:
  0.0 110.2 jit_solution(7837036560810658935)
XLA Ops:
  0.6 0.0 copy-start.3
  0.6 0.0 copy-start.4
  0.7 0.7 copy-done.3
  1.3 0.0 copy-done.4
  1.3 0.0 copy-start
  1.3 0.9 copy-done
  2.2 0.0 copy-start.2
  2.2 0.9 copy-done.2
  3.1 1.8 %shard_map.85 = (bf16[8,4,16,512]{3,2,1,0:T(8,128)(2,1)S(1)}, bf16[8,4,16,512]{3,2,1,0:T(8,128)(2,1)}, bf16[8,16,512]{2,1,0:T(8,128)(2,1)S(1)}) custom-call(s32[1]{0:T(128)} %bitcast.me_ref, s32[2,26]{1,0:T(2,128)S(1)} %copy-done.4, bf16[2,8,8,512]{3,2,1,0:T(8,128)(2,1)S(1)} %copy-done, bf16[2,8,8,512]{3,2,1,0:T(8,128)(2,1)S(1)} %copy-done.2, ...), custom_call_target="tpu_custom_call" | custom-call | tf_op jit(solution)/shard_map/pallas_call | solution.py:385
  5.0 14.8 %all_to_all.30.even_in = bf16[8,4,16,512]{3,2,1,0:T(8,128)(2,1)S(1)} all-to-all(bf16[8,4,16,512]{3,2,1,0:T(8,128)(2,1)S(1)} %get-tuple-element.10), channel_id=1, replica_groups={{0,1,2,3,4,5,6,7},{8,9,10,11,12,13,14,15},{16,17,18,19,20,21,22,23},{24..., dimensions={0} | all-to-all | bytes 1048576 | tf_op jit(solution)/shard_map/all_to_all | solution.py:405
  19.7 0.0 copy-start.5
  19.7 10.1 %all-to-all-start.1 = ((bf16[8,4,16,512]{3,2,1,0:T(8,128)(2,1)}), bf16[8,4,16,512]{3,2,1,0:T(8,128)(2,1)S(1)}, u32[]{:S(2)}, u32[]{:S(2)}) async-start(bf16[8,4,16,512]{3,2,1,0:T(8,128)(2,1)} %get-tuple-element.11), calls=%async_computation.1 | async-start | bytes 1048576 | tf_op jit(solution)/shard_map/all_to_all | solution.py:405
  29.8 0.0 copy-done.5
  29.8 0.0 copy-start.6
  29.8 0.3 copy.15.first_ref
  30.1 0.7 copy-done.6
  30.8 0.0 copy-start.1
  30.8 0.3 copy.16.second_ref
  31.0 7.9 %all-to-all-done.1.odd_in = bf16[8,4,16,512]{3,2,1,0:T(8,128)(2,1)S(1)} async-done(((bf16[8,4,16,512]{3,2,1,0:T(8,128)(2,1)}), bf16[8,4,16,512]{3,2,1,0:T(8,128)(2,1)S(1)}, u32[]{:S(2)}, u32[]{:S(2)}) %all-to-all-start.1) | async-done | bytes 524320 | tf_op jit(solution)/shard_map/all_to_all | solution.py:405
  38.9 0.0 copy-done.1
  38.9 3.5 %shard_map.86 = (bf16[8,16,512]{2,1,0:T(8,128)(2,1)S(1)}, bf16[8,96,512]{2,1,0:T(8,128)(2,1)S(1)}, bf16[8,32,512]{2,1,0:T(8,128)(2,1)S(1)}) custom-call(s32[1]{0:T(128)} %bitcast.me_ref, s32[2,26]{1,0:T(2,128)S(1)} %copy-done.4, bf16[2,8,8,512]{3,2,1,0:T(8,128)(2,1)S(1)} %copy-done.1, bf16[8,16,512]{2,1,0:T(8,128)(2,1)S(1)} %get-tuple-element.9.masked_ref, ...), custom_call_target="tpu_custom_call" | custom-call | tf_op jit(solution)/shard_map/pallas_call | solution.py:385
  42.4 14.0 %all_to_all.31.parts_ref.even_in = bf16[8,96,512]{2,1,0:T(8,128)(2,1)S(1)} all-to-all(bf16[8,96,512]{2,1,0:T(8,128)(2,1)S(1)} %get-tuple-element.13), channel_id=1, replica_groups={{0,1,2,3,4,5,6,7},{8,9,10,11,12,13,14,15},{16,17,18,19,20,21,22,23},{24..., dimensions={0} | all-to-all | bytes 1572864 | tf_op jit(solution)/shard_map/all_to_all | solution.py:405
  56.4 0.1 shard_map.87
  56.5 19.2 %all_to_all.32.parts_ref = f32[32,1,8,128]{3,2,1,0:T(8,128)S(1)} all-to-all(f32[32,1,8,128]{3,2,1,0:T(8,128)S(1)} %bitcast.4), channel_id=1, replica_groups={{0,8,16,24,32,40,48,56,64,72,80,88,96,104,112,120,128,136,144,152,160,1..., dimensions={0} | all-to-all | bytes 262144 | tf_op jit(solution)/shard_map/all_to_all | solution.py:405
  75.7 14.2 %all_to_all.33 = f32[32,1,8,128]{3,2,1,0:T(8,128)S(1)} all-to-all(f32[32,1,8,128]{3,2,1,0:T(8,128)S(1)} %shard_map.88), channel_id=1, replica_groups={{0,8,16,24,32,40,48,56,64,72,80,88,96,104,112,120,128,136,144,152,160,1..., dimensions={0} | all-to-all | bytes 262144 | tf_op jit(solution)/shard_map/all_to_all | solution.py:405
  89.9 0.1 shard_map.89
  89.9 15.9 %all_to_all.34.odd_in = bf16[8,96,512]{2,1,0:T(8,128)(2,1)S(1)} all-to-all(bf16[8,96,512]{2,1,0:T(8,128)(2,1)S(1)} %shard_map.89), channel_id=1, replica_groups={{4,5,6,7,8,9,10,11},{12,13,14,15,16,17,18,19},{20,21,22,23,24,25,26,27}..., dimensions={0} | all-to-all | bytes 1572864 | tf_op jit(solution)/shard_map/all_to_all | solution.py:405
  105.8 2.3 %shard_map.90 = (bf16[2,8,8,512]{3,2,1,0:T(8,128)(2,1)}, f32[1728,64]{1,0:T(8,128)S(1)}, f32[1728,64]{1,0:T(8,128)S(1)}) custom-call(s32[1]{0:T(128)} %bitcast.me_ref, s32[2,26]{1,0:T(2,128)S(1)} %copy-done.4, bf16[8,16,512]{2,1,0:T(8,128)(2,1)S(1)} %get-tuple-element.12.grads_ref, s32[2,8,64]{2,1,0:T(8,128)S(1)} %copy-done.3, ...), custom_call_target="tpu_custom_call" | custom-call | tf_op jit(solution)/shard_map/pallas_call | solution.py:385
  108.1 1.1 copy.18
  109.2 1.1 copy.19
  (1 shorter events, 0.0 us)
Async XLA Ops:
  0.6 0.7 copy-start.3
  0.6 0.7 copy-start.4
  1.3 0.9 copy-start
  2.2 0.9 copy-start.2
  19.7 10.1 %copy-start.5 = (bf16[1728,64]{0,1:T(8,128)(2,1)S(1)}, bf16[1728,64]{0,1:T(8,128)(2,1)}, u32[]{:S(2)}) copy-start(bf16[1728,64]{0,1:T(8,128)(2,1)} %param.9) | copy-start | bytes 663556
  19.7 19.2 %all-to-all-start.1 = ((bf16[8,4,16,512]{3,2,1,0:T(8,128)(2,1)}), bf16[8,4,16,512]{3,2,1,0:T(8,128)(2,1)S(1)}, u32[]{:S(2)}, u32[]{:S(2)}) async-start(bf16[8,4,16,512]{3,2,1,0:T(8,128)(2,1)} %get-tuple-element.11), calls=%async_computation.1 | async-start | bytes 1048576 | tf_op jit(solution)/shard_map/all_to_all | solution.py:405
  29.8 0.9 copy-start.6
  30.8 8.2 %copy-start.1 = (bf16[2,8,8,512]{3,2,1,0:T(8,128)(2,1)S(1)}, bf16[2,8,8,512]{3,2,1,0:T(8,128)(2,1)}, u32[]{:S(2)}) copy-start(bf16[2,8,8,512]{3,2,1,0:T(8,128)(2,1)} %x_ref.3) | copy-start | bytes 393220

commit v2 on v1

--- a/solution.py
+++ b/solution.py
@@ -87,10 +87,34 @@
 
 
 def pack_kernel(
-    me_ref, nb_ref, x_ref, g_ref, occ_ref, even_ref, odd_ref, masked_ref, wide, boxes
+    me_ref,
+    nb_ref,
+    x_hbm,
+    g_hbm,
+    occ_hbm,
+    even_ref,
+    odd_ref,
+    masked_ref,
+    x_ref,
+    g_ref,
+    occ_ref,
+    wide,
+    boxes,
+    sems,
 ):
+    copies = [
+        pltpu.make_async_copy(source, target, sems.at[number])
+        for number, (source, target) in enumerate(
+            ((occ_hbm, occ_ref), (g_hbm, g_ref), (x_hbm, x_ref))
+        )
+    ]
+    for copy in copies:
+        copy.start()
     me = me_ref[0]
+    copies[0].wait()
     occupied = spread(occ_ref)
+    copies[1].wait()
+    copies[2].wait()
     for x in range(EDGE):
         both = []
         for brick in range(2):
@@ -282,33 +306,29 @@
                 ]
 
 
-def first_sum_kernel(parts_ref, tiles_ref):
+def first_sum_kernel(parts_ref, pieces_ref):
     total = parts_ref[0, 32:96, :].astype(F32)
     for member in range(1, GROUP):
         total = total + parts_ref[member, 32:96, :].astype(F32)
-    for down in range(8):
-        for along in range(4):
-            tiles_ref[4 * down + along] = total[
-                8 * down : 8 * down + 8, 128 * along : 128 * along + 128
-            ]
-
-
-def second_sum_kernel(scaling, parts_ref, tiles_ref):
-    members = parts_ref.shape[0]
-    total = parts_ref[0]
-    for member in range(1, members):
-        total = total + parts_ref[member]
+    for member in range(GROUP):
+        rows = total[EDGE * member : EDGE * member + EDGE]
+        pieces_ref[member] = jnp.concatenate([rows[:, :256], rows[:, 256:]], axis=0).astype(BF16)
+
+
+def next_sum_kernel(scaling, parts_ref, copies_ref):
+    total = parts_ref[0].astype(F32)
+    for member in range(1, parts_ref.shape[0]):
+        total = total + parts_ref[member].astype(F32)
     total = total * scaling
-    for member in range(members):
-        tiles_ref[member] = total
-
-
-def share_kernel(tiles_ref, odd_ref, out_ref):
+    for member in range(copies_ref.shape[0]):
+        copies_ref[member] = total.astype(copies_ref.dtype)
+
+
+def share_kernel(pieces_ref, odd_ref, out_ref):
     rows = []
-    for down in range(8):
-        rows.append(
-            jnp.concatenate([tiles_ref[4 * down + along] for along in range(4)], axis=1)
-        )
+    for member in range(GROUP):
+        piece = pieces_ref[member].astype(F32)
+        rows.append(jnp.concatenate([piece[:EDGE], piece[EDGE:]], axis=1))
     chunk = jnp.concatenate(rows, axis=0).astype(BF16)
     for member in range(GROUP):
         out_ref[member, 0:32, :] = odd_ref[member]
@@ -370,25 +390,25 @@
                 )
             )
         halves.append(jnp.concatenate(rows, axis=0).astype(F32))
-    for block in range(27):
-        at = (26 - block) * 64
-        second_out[at : at + 64, :] = halves[0][:, block * 64 : block * 64 + 64]
+    first_out[...] = halves[1][:, : 27 * 64]
+    blocks = []
     for pair in range(14):
-        turned = halves[1][:, pair * 128 : pair * 128 + 128].T
-        count = min(128, 27 * 64 - pair * 128)
-        first_out[pair * 128 : pair * 128 + count, :] = turned[:count]
-
-
-def call(kernel, shapes, scratch, arguments, scalars=0, flops=0):
+        turned = halves[0][:, pair * 128 : pair * 128 + 128].T
+        blocks += [turned[0:64], turned[64:128]]
+    second_out[...] = jnp.concatenate(blocks[26::-1], axis=1)
+
+
+def call(kernel, shapes, scratch, arguments, scalars=0, outside=0, megabytes=40):
     specs = [pl.BlockSpec(memory_space=pltpu.SMEM)] * scalars
-    specs += [pl.BlockSpec(memory_space=pltpu.VMEM)] * (len(arguments) - scalars)
+    specs += [pl.BlockSpec(memory_space=pl.ANY)] * outside
+    specs += [pl.BlockSpec(memory_space=pltpu.VMEM)] * (len(arguments) - len(specs))
     return pl.pallas_call(
         kernel,
         out_shape=[jax.ShapeDtypeStruct(shape, kind) for shape, kind in shapes],
         in_specs=specs,
         out_specs=[pl.BlockSpec(memory_space=pltpu.VMEM)] * len(shapes),
-        scratch_shapes=[pltpu.VMEM(shape, kind) for shape, kind in scratch],
-        compiler_params=pltpu.CompilerParams(vmem_limit_bytes=40 * 1024 * 1024),
+        scratch_shapes=scratch,
+        compiler_params=pltpu.CompilerParams(vmem_limit_bytes=megabytes * 2**20),
     )(*arguments)
 
 
@@ -398,19 +418,34 @@
     scaling = 1.0 / math.sqrt(inputs.shape[0] * devices * EDGE**3)
     even = [[GROUP * k + j for j in range(GROUP)] for k in range(members)]
     odd = [[(GROUP * k + 4 + j) % devices for j in range(GROUP)] for k in range(members)]
-    across = [[GROUP * j + k for j in range(members)] for k in range(GROUP)]
+    quarters = lax.axis_size("dev") // GROUP
+    strided = [
+        [lax.axis_size("dev") * grp + GROUP * quarter + member for quarter in range(quarters)]
+        for grp in range(lax.axis_size("grp"))
+        for member in range(GROUP)
+    ]
     me = (lax.axis_index("grp") * lax.axis_size("dev") + lax.axis_index("dev")).reshape(1)
 
     def swap(value, groups):
         return lax.all_to_all(value, AXES, 0, 0, axis_index_groups=groups, tiled=True)
 
+    vmem = pltpu.VMEM
     halo = ((GROUP, 4, 16, WIDE), BF16)
     even_out, odd_out, masked = call(
         pack_kernel,
         [halo, halo, ((EDGE, 16, WIDE), BF16)],
-        [((4, 64, WIDE), F32), ((64, 16, WIDE), BF16)],
+        [
+            vmem((2, EDGE, EDGE, WIDE), BF16),
+            vmem((2, EDGE, EDGE, WIDE), BF16),
+            vmem((2, EDGE, 64), jnp.int32),
+            vmem((4, 64, WIDE), F32),
+            vmem((64, 16, WIDE), BF16),
+            pltpu.SemaphoreType.DMA((3,)),
+        ],
         [me, neighbours, inputs, out_grads, occupancy],
         scalars=2,
+        outside=3,
+        megabytes=60,
     )
     even_in = swap(even_out, even)
     odd_in = swap(odd_out, odd)
@@ -422,47 +457,50 @@
             ((GROUP, 32, WIDE), BF16),
         ],
         [
-            ((2, 2, 10 * ROWS, PADDED), F32),
-            ((2, 3, 10, 16, PADDED), BF16),
-            ((2, 512, 2304), BF16),
-            ((2304, 128), BF16),
-            ((128, 2304), BF16),
-            ((128, 2304), F32),
-            ((2, 64, WIDE), F32),
-            ((64, EDGE, WIDE), F32),
+            vmem((2, 2, 10 * ROWS, PADDED), F32),
+            vmem((2, 3, 10, 16, PADDED), BF16),
+            vmem((2, 512, 2304), BF16),
+            vmem((2304, 128), BF16),
+            vmem((128, 2304), BF16),
+            vmem((128, 2304), F32),
+            vmem((2, 64, WIDE), F32),
+            vmem((64, EDGE, WIDE), F32),
         ],
         [me, neighbours, inputs, masked, occupancy, even_in, odd_in, first_kernel, second_kernel],
         scalars=2,
     )
     even_in = swap(even_out, even)
-    (tiles,) = call(first_sum_kernel, [((32, 8, 128), F32)], [], [even_in])
-    across_shape = (members, 32 // members, 8, 128)
-    tiles = swap(tiles.reshape(across_shape), across)
-    (tiles,) = call(
-        functools.partial(second_sum_kernel, scaling), [(across_shape, F32)], [], [tiles]
-    )
-    tiles = swap(tiles, across).reshape(32, 8, 128)
-    (odd_out,) = call(share_kernel, [((GROUP, 96, WIDE), BF16)], [], [tiles, odd_out])
+    piece = (16, 256)
+    (pieces,) = call(first_sum_kernel, [((GROUP,) + piece, BF16)], [], [even_in])
+    pieces = lax.all_to_all(pieces, "grp", 0, 0, tiled=True)
+    (pieces,) = call(
+        functools.partial(next_sum_kernel, 1.0), [((quarters,) + piece, BF16)], [], [pieces]
+    )
+    pieces = swap(pieces, strided)
+    (pieces,) = call(
+        functools.partial(next_sum_kernel, scaling), [((GROUP,) + piece, BF16)], [], [pieces]
+    )
+    pieces = lax.all_to_all(pieces, "grp", 0, 0, tiled=True)
+    (odd_out,) = call(share_kernel, [((GROUP, 96, WIDE), BF16)], [], [pieces, odd_out])
     odd_in = swap(odd_out, odd)
-    return tuple(
-        call(
-            last_kernel,
-            [
-                ((2, EDGE, EDGE, WIDE), BF16),
-                ((27 * 64, 64), F32),
-                ((27 * 64, 64), F32),
-            ],
-            [
-                ((2, 10 * ROWS, PADDED), F32),
-                ((3, 10, 16, PADDED), BF16),
-                ((512, 2304), BF16),
-                ((128, 2304), BF16),
-                ((64, EDGE, WIDE), F32),
-            ],
-            [me, neighbours, pre_grads, occupancy, even_in, odd_in, first_kernel],
-            scalars=2,
-        )
-    )
+    input_grads, first_grads, second_grads = call(
+        last_kernel,
+        [
+            ((2, EDGE, EDGE, WIDE), BF16),
+            ((64, 27 * 64), F32),
+            ((64, 27 * 64), F32),
+        ],
+        [
+            vmem((2, 10 * ROWS, PADDED), F32),
+            vmem((3, 10, 16, PADDED), BF16),
+            vmem((512, 2304), BF16),
+            vmem((128, 2304), BF16),
+            vmem((64, EDGE, WIDE), F32),
+        ],
+        [me, neighbours, pre_grads, occupancy, even_in, odd_in, first_kernel],
+        scalars=2,
+    )
+    return input_grads, first_grads.T, second_grads.T
 
 
 def solution(mesh):

time: 111 us -> 106 us (0.955)
  local copies, waits for them, and re-layouts: 5.81 us -> 1.22 us
  blocking collectives: 78 us -> 76.2 us
  Pallas kernels: 7.76 us -> 9.26 us
    all_to_all x5 -> x4, blocking collectives: 78 us -> 56.8 us  [swap(): lax.all_to_all(value, AXES, 0, 0, axis_index_groups=groups, tiled=True)]
    all_to_all x0 -> x2, blocking collectives: none -> 19.3 us  [per_device(): pieces = lax.all_to_all(pieces, 'grp', 0, 0, tiled=True)]
    unnamed x16 -> x14, local copies, waits for them, and re-layouts: 3.7 us -> 1.22 us
    pallas_call x2 -> x0, local copies, waits for them, and re-layouts: 2.1 us -> none  [call(): pl.pallas_call(kernel, out_shape=[jax.ShapeDtypeStruct(shape, kind) for s...]
    pallas_call x6 -> x7, Pallas kernels: 7.76 us -> 9.26 us  [call(): pl.pallas_call(kernel, out_shape=[jax.ShapeDtypeStruct(shape, kind) for s...]
  transfers between devices with their start and end apart: 1 -> 1, of which waited for: 1 -> 1; matrix products, arithmetic and copies ran while one was open for 0% -> 1% of each run, Pallas kernels for 0% -> 0%
where the time goes in v2:
time: 106 us; the launch traced here: 105 us
  blocking collectives  76.2 us (72%)
  starting transfers between devices  10.1 us (10%)
  Pallas kernels  9.26 us (9%)
  waiting for transfers between devices  7.87 us (7%)
  local copies, waits for them, and re-layouts  1.22 us (1%)
    all_to_all x4, blocking collectives, swap(): lax.all_to_all(value, AXES, 0, 0, axis_index_groups=groups, tiled=True)  56.8 us
    all_to_all x2, blocking collectives, per_device(): pieces = lax.all_to_all(pieces, 'grp', 0, 0, tiled=True)  19.3 us
    all_to_all x1, starting transfers between devices, swap(): lax.all_to_all(value, AXES, 0, 0, axis_index_groups=groups, tiled=True)  10.1 us
    pallas_call x7, Pallas kernels, call(): pl.pallas_call(kernel, out_shape=[jax.ShapeDtypeStruct(shape, kind) for s...  9.26 us
    all_to_all x1, waiting for transfers between devices, swap(): lax.all_to_all(value, AXES, 0, 0, axis_index_groups=groups, tiled=True)  7.87 us
  transfers between devices with their start and end apart: 1, of which 1 were waited for; matrix products, arithmetic and copies ran while one was open for 1% of the time, Pallas kernels for 0%

profile of v2, /device:TPU:1, one launch (start us, length us, event | category | flops | bytes accessed | tf_op | source)
XLA Modules:
  0.0 105.3 jit_solution(3618865618003524628)
XLA Ops:
  0.6 3.0 %shard_map.85 = (bf16[8,4,16,512]{3,2,1,0:T(8,128)(2,1)}, bf16[8,4,16,512]{3,2,1,0:T(8,128)(2,1)}, bf16[8,16,512]{2,1,0:T(8,128)(2,1)}) custom-call(s32[1]{0:T(128)} %bitcast.me_ref, s32[2,26]{1,0:T(2,128)} %nb_ref.5, bf16[2,8,8,512]{3,2,1,0:T(8,128)(2,1)} %x_ref.1, bf16[2,8,8,512]{3,2,1,0:T(8,128)(2,1)} %g_hbm.1, s32[2,8,64]{2,1,0:T(8,128)} %occ_ref.3), custom_call_target="tpu_custom_call" | custom-call | tf_op jit(solution)/shard_map/pallas_call | solution.py:405
  3.7 15.0 %all_to_all.35.even_in = bf16[8,4,16,512]{3,2,1,0:T(8,128)(2,1)S(1)} all-to-all(bf16[8,4,16,512]{3,2,1,0:T(8,128)(2,1)} %get-tuple-element.13), channel_id=1, replica_groups={{0,1,2,3,4,5,6,7},{8,9,10,11,12,13,14,15},{16,17,18,19,20,21,22,23},{24..., dimensions={0} | all-to-all | bytes 1048576 | tf_op jit(solution)/shard_map/all_to_all | solution.py:430
  18.7 0.0 copy-start.4
  18.7 10.1 %all-to-all-start.1 = ((bf16[8,4,16,512]{3,2,1,0:T(8,128)(2,1)}), bf16[8,4,16,512]{3,2,1,0:T(8,128)(2,1)S(1)}, u32[]{:S(2)}, u32[]{:S(2)}) async-start(bf16[8,4,16,512]{3,2,1,0:T(8,128)(2,1)} %get-tuple-element.14), calls=%async_computation.1 | async-start | bytes 1048576 | tf_op jit(solution)/shard_map/all_to_all | solution.py:430
  28.8 0.0 copy-done.4
  28.8 0.0 copy-start.5
  28.8 0.3 copy.9.first_ref
  29.1 0.7 copy-done.5
  29.7 0.0 copy-start
  29.7 0.0 copy-start.1
  29.7 0.0 copy-start.2
  29.7 0.3 copy.10.second_ref
  30.0 0.0 copy-start.3
  30.0 7.9 %all-to-all-done.1.odd_in = bf16[8,4,16,512]{3,2,1,0:T(8,128)(2,1)S(1)} async-done(((bf16[8,4,16,512]{3,2,1,0:T(8,128)(2,1)}), bf16[8,4,16,512]{3,2,1,0:T(8,128)(2,1)S(1)}, u32[]{:S(2)}, u32[]{:S(2)}) %all-to-all-start.1) | async-done | bytes 524320 | tf_op jit(solution)/shard_map/all_to_all | solution.py:430
  37.9 0.0 copy-done
  37.9 0.0 copy-done.1
  37.9 0.0 copy-done.2
  37.9 0.0 copy-done.3
  37.9 3.5 %shard_map.86 = (bf16[8,16,512]{2,1,0:T(8,128)(2,1)S(1)}, bf16[8,96,512]{2,1,0:T(8,128)(2,1)S(1)}, bf16[8,32,512]{2,1,0:T(8,128)(2,1)S(1)}) custom-call(s32[1]{0:T(128)} %bitcast.me_ref, s32[2,26]{1,0:T(2,128)S(1)} %copy-done.3, bf16[2,8,8,512]{3,2,1,0:T(8,128)(2,1)S(1)} %copy-done, bf16[8,16,512]{2,1,0:T(8,128)(2,1)S(1)} %copy-done.1, ...), custom_call_target="tpu_custom_call" | custom-call | tf_op jit(solution)/shard_map/pallas_call | solution.py:405
  41.4 14.0 %all_to_all.36.parts_ref.even_in = bf16[8,96,512]{2,1,0:T(8,128)(2,1)S(1)} all-to-all(bf16[8,96,512]{2,1,0:T(8,128)(2,1)S(1)} %get-tuple-element.16), channel_id=1, replica_groups={{0,1,2,3,4,5,6,7},{8,9,10,11,12,13,14,15},{16,17,18,19,20,21,22,23},{24..., dimensions={0} | all-to-all | bytes 1572864 | tf_op jit(solution)/shard_map/all_to_all | solution.py:430
  55.4 0.1 shard_map.87
  55.4 9.9 %all_to_all.37.parts_ref = bf16[8,16,256]{2,1,0:T(8,128)(2,1)S(1)} all-to-all(bf16[8,16,256]{2,1,0:T(8,128)(2,1)S(1)} %shard_map.87), channel_id=1, replica_groups=mesh['grp'=8,'dev'=32] {'grp'}, dimensions={0} | all-to-all | bytes 131072 | tf_op jit(solution)/shard_map/all_to_all | solution.py:475
  65.4 11.1 %all_to_all.38.parts_ref = bf16[4,16,256]{2,1,0:T(8,128)(2,1)S(1)} all-to-all(bf16[4,16,256]{2,1,0:T(8,128)(2,1)S(1)} %shard_map.88), channel_id=1, replica_groups={{0,8,16,24},{1,9,17,25},{2,10,18,26},{3,11,19,27},{4,12,20,28},{5,13,21..., dimensions={0} | all-to-all | bytes 65536 | tf_op jit(solution)/shard_map/all_to_all | solution.py:430
  76.4 9.4 %all_to_all.39.pieces_ref = bf16[8,16,256]{2,1,0:T(8,128)(2,1)S(1)} all-to-all(bf16[8,16,256]{2,1,0:T(8,128)(2,1)S(1)} %shard_map.89), channel_id=1, replica_groups=mesh['grp'=8,'dev'=32] {'grp'}, dimensions={0} | all-to-all | bytes 131072 | tf_op jit(solution)/shard_map/all_to_all | solution.py:483
  85.9 0.1 shard_map.90
  85.9 16.8 %all_to_all.40.odd_in = bf16[8,96,512]{2,1,0:T(8,128)(2,1)S(1)} all-to-all(bf16[8,96,512]{2,1,0:T(8,128)(2,1)S(1)} %shard_map.90), channel_id=1, replica_groups={{4,5,6,7,8,9,10,11},{12,13,14,15,16,17,18,19},{20,21,22,23,24,25,26,27}..., dimensions={0} | all-to-all | bytes 1572864 | tf_op jit(solution)/shard_map/all_to_all | solution.py:430
  102.7 2.6 %shard_map.91 = (bf16[2,8,8,512]{3,2,1,0:T(8,128)(2,1)}, f32[64,1728]{1,0:T(8,128)}, f32[64,1728]{1,0:T(8,128)}) custom-call(s32[1]{0:T(128)} %bitcast.me_ref, s32[2,26]{1,0:T(2,128)S(1)} %copy-done.3, bf16[8,16,512]{2,1,0:T(8,128)(2,1)S(1)} %get-tuple-element.15.grads_ref, s32[2,8,64]{2,1,0:T(8,128)S(1)} %copy-done.2, ...), custom_call_target="tpu_custom_call" | custom-call | tf_op jit(solution)/shard_map/pallas_call | solution.py:405
  (2 shorter events, 0.0 us)
Async XLA Ops:
  18.7 10.1 %copy-start.4 = (bf16[1728,64]{0,1:T(8,128)(2,1)S(1)}, bf16[1728,64]{0,1:T(8,128)(2,1)}, u32[]{:S(2)}) copy-start(bf16[1728,64]{0,1:T(8,128)(2,1)} %param.9) | copy-start | bytes 663556
  18.7 19.2 %all-to-all-start.1 = ((bf16[8,4,16,512]{3,2,1,0:T(8,128)(2,1)}), bf16[8,4,16,512]{3,2,1,0:T(8,128)(2,1)S(1)}, u32[]{:S(2)}, u32[]{:S(2)}) async-start(bf16[8,4,16,512]{3,2,1,0:T(8,128)(2,1)} %get-tuple-element.14), calls=%async_computation.1 | async-start | bytes 1048576 | tf_op jit(solution)/shard_map/all_to_all | solution.py:430
  28.8 0.9 copy-start.5
  29.7 8.2 %copy-start = (bf16[2,8,8,512]{3,2,1,0:T(8,128)(2,1)S(1)}, bf16[2,8,8,512]{3,2,1,0:T(8,128)(2,1)}, u32[]{:S(2)}) copy-start(bf16[2,8,8,512]{3,2,1,0:T(8,128)(2,1)} %x_ref.1) | copy-start | bytes 393220
  29.7 8.2 %copy-start.1 = (bf16[8,16,512]{2,1,0:T(8,128)(2,1)S(1)}, bf16[8,16,512]{2,1,0:T(8,128)(2,1)}, u32[]{:S(2)}) copy-start(bf16[8,16,512]{2,1,0:T(8,128)(2,1)} %get-tuple-element.12.masked_ref) | copy-start | bytes 393220
  29.7 8.2 %copy-start.2 = (s32[2,8,64]{2,1,0:T(8,128)S(1)}, s32[2,8,64]{2,1,0:T(8,128)}, u32[]{:S(2)}) copy-start(s32[2,8,64]{2,1,0:T(8,128)} %occ_ref.3) | copy-start | bytes 12292
  30.0 7.9 %copy-start.3 = (s32[2,26]{1,0:T(2,128)S(1)}, s32[2,26]{1,0:T(2,128)}, u32[]{:S(2)}) copy-start(s32[2,26]{1,0:T(2,128)} %nb_ref.5) | copy-start | bytes 628

commit v3 on v2

--- a/solution.py
+++ b/solution.py
@@ -9,7 +9,6 @@
 from jax.sharding import PartitionSpec as P
 
 AXES = ("grp", "dev")
-GROUP = 8
 EDGE = 8
 WIDE = 512
 PADDED = 640
@@ -37,15 +36,20 @@
     other = nb_ref[brick, number]
     present = other >= 0
     owner = jnp.maximum(other, 0) >> 1
-    same = (owner >> 3) == (me >> 3)
-    box = jnp.where(same, owner & 7, 8 + ((owner + 4) & 7))
-    return present, box, other & 1
+    return present, owner & 3, (owner >> 2) - (me >> 2), owner == me, other & 1
 
 
 def send_place(nb_ref, me, brick, number):
-    present, box, slot = locate(nb_ref, me, brick, number)
-    unused = (8 + ((me + 4) & 7)) * 4
-    return jnp.where(present, box * 4 + brick * 2 + slot, unused)
+    present, member, up, own, slot = locate(nb_ref, me, brick, number)
+    relayed = (up > 0) | ((up < 0) & (member != (me & 3)))
+    place = jnp.where(own, 32, member * 8 + jnp.where(relayed, 4, 0))
+    return jnp.where(present, place + brick * 2 + slot, 32)
+
+
+def take_place(nb_ref, me, brick, number):
+    present, member, up, own, slot = locate(nb_ref, me, brick, number)
+    place = member * 4 + jnp.where(up == 0, 0, jnp.where(up < 0, 16, 32))
+    return present, jnp.where(own, 48, place) + slot * 2 + brick
 
 
 def face_kind(offset):
@@ -92,8 +96,8 @@
     x_hbm,
     g_hbm,
     occ_hbm,
-    even_ref,
-    odd_ref,
+    near_ref,
+    kept_ref,
     masked_ref,
     x_ref,
     g_ref,
@@ -132,8 +136,16 @@
             packets[key] = jnp.concatenate([first[key], second[key]], axis=0).astype(BF16)
         for number, offset in enumerate(DIRECTIONS):
             boxes[send_place(nb_ref, me, brick, number)] = packets[face_kind(offset)]
-    even_ref[...] = boxes[0:32].reshape(8, 4, 16, WIDE)
-    odd_ref[...] = boxes[32:64].reshape(8, 4, 16, WIDE)
+    near_ref[...] = boxes[0:32].reshape(4, 128, WIDE)
+    kept_ref[...] = boxes[32:36]
+
+
+def route_kernel(me_ref, near_ref, above_ref, below_ref):
+    size = above_ref.shape[1]
+    own = me_ref[0] & 3
+    above_ref[...] = near_ref[:, size : 2 * size, :]
+    below_ref[...] = near_ref[:, size : 2 * size, :]
+    below_ref[own] = near_ref[own, 0:size, :]
 
 
 def beside(low, middle, high):
@@ -234,13 +246,16 @@
     x_ref,
     masked_ref,
     occ_ref,
-    even_in,
-    odd_in,
+    near_ref,
+    below_ref,
+    above_ref,
+    kept_in,
     first_ref,
     second_ref,
     grads_ref,
-    even_ref,
-    odd_ref,
+    out_ref,
+    kept_ref,
+    taken,
     padded,
     shifted,
     windows,
@@ -251,14 +266,17 @@
     boxes,
 ):
     me = me_ref[0]
+    for member in range(4):
+        at = 4 * member
+        taken[at : at + 4] = near_ref[member, 0:64, :].reshape(4, 16, WIDE)
+        taken[at + 16 : at + 20] = below_ref[member].reshape(4, 16, WIDE)
+        taken[at + 32 : at + 36] = above_ref[member].reshape(4, 16, WIDE)
+    taken[48:52] = kept_in[...]
     for brick in range(2):
         values = {}
         for number, offset in enumerate(DIRECTIONS):
-            present, box, slot = locate(nb_ref, me, brick, number)
-            place = slot * 2 + brick
-            low = even_in[box & 7, place].astype(F32)
-            high = odd_in[box & 7, place].astype(F32)
-            values[offset] = jnp.where(present, jnp.where(box < 8, low, high), 0.0)
+            present, place = take_place(nb_ref, me, brick, number)
+            values[offset] = jnp.where(present, taken[place].astype(F32), 0.0)
 
         def own_first(x):
             return x_ref[brick, x].astype(F32)
@@ -290,32 +308,33 @@
         faces = face_values(wide, brick)
         for number, offset in enumerate(DIRECTIONS):
             boxes[send_place(nb_ref, me, brick, number)] = faces[face_kind(offset)]
-    for box in range(8):
-        even_ref[box, 0:32, :] = boxes[4 * box : 4 * box + 4].reshape(32, WIDE).astype(BF16)
-        odd_ref[box] = boxes[32 + 4 * box : 36 + 4 * box].reshape(32, WIDE).astype(BF16)
+    for member in range(4):
+        out_ref[member, 0:64, :] = (
+            boxes[8 * member : 8 * member + 8].reshape(64, WIDE).astype(BF16)
+        )
+    kept_ref[...] = boxes[32:36]
 
     for half, own, field in ((0, hidden, 1), (1, pre_grads, 0)):
         turned = own.astype(F32).T.astype(BF16)
         product[...] = jnp.dot(turned, windows[field], preferred_element_type=F32)
         packed = gather_blocks(product).astype(BF16)
-        for chunk in range(4):
+        for chunk in range(2):
             for part in range(4):
-                at = 32 + 16 * part
-                even_ref[4 * half + chunk, at : at + 16, :] = packed[
-                    16 * chunk : 16 * chunk + 16, part * WIDE : (part + 1) * WIDE
+                at = 64 + 32 * part
+                out_ref[2 * half + chunk, at : at + 32, :] = packed[
+                    32 * chunk : 32 * chunk + 32, part * WIDE : (part + 1) * WIDE
                 ]
 
 
 def first_sum_kernel(parts_ref, pieces_ref):
-    total = parts_ref[0, 32:96, :].astype(F32)
-    for member in range(1, GROUP):
-        total = total + parts_ref[member, 32:96, :].astype(F32)
-    for member in range(GROUP):
-        rows = total[EDGE * member : EDGE * member + EDGE]
-        pieces_ref[member] = jnp.concatenate([rows[:, :256], rows[:, 256:]], axis=0).astype(BF16)
-
-
-def next_sum_kernel(scaling, parts_ref, copies_ref):
+    total = parts_ref[0, 64:192, :].astype(F32)
+    for member in range(1, 4):
+        total = total + parts_ref[member, 64:192, :].astype(F32)
+    pieces_ref[...] = total.astype(BF16).reshape(pieces_ref.shape)
+
+
+def next_sum_kernel(scaling, arrived_ref, parts_ref, copies_ref):
+    del arrived_ref
     total = parts_ref[0].astype(F32)
     for member in range(1, parts_ref.shape[0]):
         total = total + parts_ref[member].astype(F32)
@@ -324,47 +343,41 @@
         copies_ref[member] = total.astype(copies_ref.dtype)
 
 
-def share_kernel(pieces_ref, odd_ref, out_ref):
-    rows = []
-    for member in range(GROUP):
-        piece = pieces_ref[member].astype(F32)
-        rows.append(jnp.concatenate([piece[:EDGE], piece[EDGE:]], axis=1))
-    chunk = jnp.concatenate(rows, axis=0).astype(BF16)
-    for member in range(GROUP):
-        out_ref[member, 0:32, :] = odd_ref[member]
-        out_ref[member, 32:96, :] = chunk
-
-
-def last_kernel(
+def share_kernel(pieces_ref, copies_ref):
+    chunk = pieces_ref[...].reshape(128, WIDE)
+    for member in range(4):
+        copies_ref[member] = chunk
+
+
+def input_grads_kernel(
     me_ref,
     nb_ref,
     grads_ref,
     occ_ref,
-    even_in,
-    odd_in,
+    near_ref,
+    below_ref,
+    above_ref,
+    kept_ref,
     first_ref,
     out_ref,
-    first_out,
-    second_out,
+    taken,
     padded,
     shifted,
     windows,
     flipped,
-    boxes,
 ):
     me = me_ref[0]
-    for box in range(8):
-        boxes[4 * box : 4 * box + 4] = (
-            even_in[box, 0:32, :].astype(F32).reshape(4, EDGE, WIDE)
-        )
-        boxes[32 + 4 * box : 36 + 4 * box] = (
-            odd_in[box, 0:32, :].astype(F32).reshape(4, EDGE, WIDE)
-        )
+    for member in range(4):
+        at = 4 * member
+        taken[at : at + 4] = near_ref[member, 0:32, :].astype(F32).reshape(4, EDGE, WIDE)
+        taken[at + 16 : at + 20] = below_ref[member].astype(F32).reshape(4, EDGE, WIDE)
+        taken[at + 32 : at + 36] = above_ref[member].astype(F32).reshape(4, EDGE, WIDE)
+    taken[48:52] = kept_ref[...]
     for brick in range(2):
         values = {}
         for number, offset in enumerate(DIRECTIONS):
-            present, box, slot = locate(nb_ref, me, brick, number)
-            values[offset] = jnp.where(present, boxes[4 * box + slot * 2 + brick], 0.0)
+            present, place = take_place(nb_ref, me, brick, number)
+            values[offset] = jnp.where(present, taken[place], 0.0)
 
         def own(x):
             return grads_ref[x].astype(F32)[brick * EDGE : (brick + 1) * EDGE]
@@ -378,14 +391,15 @@
             at = 16 * x + EDGE * brick
             out_ref[brick, x] = result[at : at + EDGE].astype(BF16)
 
+
+def unpack_kernel(parts_ref, first_out, second_out):
     halves = []
     for half in range(2):
         rows = []
-        for chunk in range(4 * half, 4 * half + 4):
-            slot = (chunk + 4) & 7
+        for chunk in (2 * half, 2 * half + 1):
             rows.append(
                 jnp.concatenate(
-                    [odd_in[slot, 32 + 16 * part : 48 + 16 * part, :] for part in range(4)],
+                    [parts_ref[chunk, 32 * part : 32 * part + 32, :] for part in range(4)],
                     axis=1,
                 )
             )
@@ -398,7 +412,7 @@
     second_out[...] = jnp.concatenate(blocks[26::-1], axis=1)
 
 
-def call(kernel, shapes, scratch, arguments, scalars=0, outside=0, megabytes=40):
+def call(kernel, shapes, scratch, arguments, scalars=0, outside=0, megabytes=40, flops=0):
     specs = [pl.BlockSpec(memory_space=pltpu.SMEM)] * scalars
     specs += [pl.BlockSpec(memory_space=pl.ANY)] * outside
     specs += [pl.BlockSpec(memory_space=pltpu.VMEM)] * (len(arguments) - len(specs))
@@ -408,38 +422,44 @@
         in_specs=specs,
         out_specs=[pl.BlockSpec(memory_space=pltpu.VMEM)] * len(shapes),
         scratch_shapes=scratch,
+        cost_estimate=pl.CostEstimate(flops=flops, bytes_accessed=2**19, transcendentals=0),
         compiler_params=pltpu.CompilerParams(vmem_limit_bytes=megabytes * 2**20),
     )(*arguments)
 
 
 def per_device(inputs, occupancy, neighbours, first_kernel, second_kernel, out_grads):
-    devices = lax.axis_size("grp") * lax.axis_size("dev")
-    members = devices // GROUP
+    along_grp, along_dev = lax.axis_size("grp"), lax.axis_size("dev")
+    devices = along_grp * along_dev
     scaling = 1.0 / math.sqrt(inputs.shape[0] * devices * EDGE**3)
-    even = [[GROUP * k + j for j in range(GROUP)] for k in range(members)]
-    odd = [[(GROUP * k + 4 + j) % devices for j in range(GROUP)] for k in range(members)]
-    quarters = lax.axis_size("dev") // GROUP
-    strided = [
-        [lax.axis_size("dev") * grp + GROUP * quarter + member for quarter in range(quarters)]
-        for grp in range(lax.axis_size("grp"))
-        for member in range(GROUP)
+    fours = [[4 * row + member for member in range(4)] for row in range(devices // 4)]
+    rows = along_dev // 4
+    stacks = [
+        [along_dev * grp + 4 * row + member for row in range(rows)]
+        for grp in range(along_grp)
+        for member in range(4)
     ]
-    me = (lax.axis_index("grp") * lax.axis_size("dev") + lax.axis_index("dev")).reshape(1)
-
-    def swap(value, groups):
-        return lax.all_to_all(value, AXES, 0, 0, axis_index_groups=groups, tiled=True)
-
+    me = (lax.axis_index("grp") * along_dev + lax.axis_index("dev")).reshape(1)
     vmem = pltpu.VMEM
-    halo = ((GROUP, 4, 16, WIDE), BF16)
-    even_out, odd_out, masked = call(
+
+    def swap(value, members):
+        return lax.all_to_all(value, AXES, 0, 0, axis_index_groups=members, tiled=True)
+
+    def send_on(near, size):
+        packets = ((4, size, WIDE), BF16)
+        above, below = call(route_kernel, [packets, packets], [], [me, near], scalars=1)
+        from_below = lax.ppermute(above, AXES, [(i, i + 4) for i in range(devices - 4)])
+        from_above = lax.ppermute(below, AXES, [(i + 4, i) for i in range(devices - 4)])
+        return from_below, from_above
+
+    near, kept, masked = call(
         pack_kernel,
-        [halo, halo, ((EDGE, 16, WIDE), BF16)],
+        [((4, 128, WIDE), BF16), ((4, 16, WIDE), BF16), ((EDGE, 16, WIDE), BF16)],
         [
             vmem((2, EDGE, EDGE, WIDE), BF16),
             vmem((2, EDGE, EDGE, WIDE), BF16),
             vmem((2, EDGE, 64), jnp.int32),
             vmem((4, 64, WIDE), F32),
-            vmem((64, 16, WIDE), BF16),
+            vmem((36, 16, WIDE), BF16),
             pltpu.SemaphoreType.DMA((3,)),
         ],
         [me, neighbours, inputs, out_grads, occupancy],
@@ -447,16 +467,13 @@
         outside=3,
         megabytes=60,
     )
-    even_in = swap(even_out, even)
-    odd_in = swap(odd_out, odd)
-    pre_grads, even_out, odd_out = call(
+    near = swap(near, fours)
+    below, above = send_on(near, 64)
+    pre_grads, near, kept = call(
         main_kernel,
+        [((EDGE, 16, WIDE), BF16), ((4, 192, WIDE), BF16), ((4, EDGE, WIDE), F32)],
         [
-            ((EDGE, 16, WIDE), BF16),
-            ((GROUP, 96, WIDE), BF16),
-            ((GROUP, 32, WIDE), BF16),
-        ],
-        [
+            vmem((52, 16, WIDE), BF16),
             vmem((2, 2, 10 * ROWS, PADDED), F32),
             vmem((2, 3, 10, 16, PADDED), BF16),
             vmem((2, 512, 2304), BF16),
@@ -464,41 +481,63 @@
             vmem((128, 2304), BF16),
             vmem((128, 2304), F32),
             vmem((2, 64, WIDE), F32),
-            vmem((64, EDGE, WIDE), F32),
-        ],
-        [me, neighbours, inputs, masked, occupancy, even_in, odd_in, first_kernel, second_kernel],
-        scalars=2,
-    )
-    even_in = swap(even_out, even)
-    piece = (16, 256)
-    (pieces,) = call(first_sum_kernel, [((GROUP,) + piece, BF16)], [], [even_in])
-    pieces = lax.all_to_all(pieces, "grp", 0, 0, tiled=True)
-    (pieces,) = call(
-        functools.partial(next_sum_kernel, 1.0), [((quarters,) + piece, BF16)], [], [pieces]
-    )
-    pieces = swap(pieces, strided)
-    (pieces,) = call(
-        functools.partial(next_sum_kernel, scaling), [((GROUP,) + piece, BF16)], [], [pieces]
-    )
-    pieces = lax.all_to_all(pieces, "grp", 0, 0, tiled=True)
-    (odd_out,) = call(share_kernel, [((GROUP, 96, WIDE), BF16)], [], [pieces, odd_out])
-    odd_in = swap(odd_out, odd)
-    input_grads, first_grads, second_grads = call(
-        last_kernel,
-        [
-            ((2, EDGE, EDGE, WIDE), BF16),
-            ((64, 27 * 64), F32),
-            ((64, 27 * 64), F32),
+            vmem((36, EDGE, WIDE), F32),
         ],
         [
+            me,
+            neighbours,
+            inputs,
+            masked,
+            occupancy,
+            near,
+            below,
+            above,
+            kept,
+            first_kernel,
+            second_kernel,
+        ],
+        scalars=2,
+        flops=2**30,
+    )
+    near = swap(near, fours)
+    below, above = send_on(near, 32)
+    piece = (128 // along_grp, WIDE)
+    (sums,) = call(first_sum_kernel, [((along_grp,) + piece, BF16)], [], [near])
+    sums = lax.all_to_all(sums, "grp", 0, 0, tiled=True)
+    (sums,) = call(
+        functools.partial(next_sum_kernel, 1.0),
+        [((rows,) + piece, BF16)],
+        [],
+        [below, sums],
+        outside=1,
+    )
+    sums = swap(sums, stacks)
+    (sums,) = call(
+        functools.partial(next_sum_kernel, scaling),
+        [((along_grp,) + piece, BF16)],
+        [],
+        [above, sums],
+        outside=1,
+    )
+    sums = lax.all_to_all(sums, "grp", 0, 0, tiled=True)
+    (sums,) = call(share_kernel, [((4, 128, WIDE), BF16)], [], [sums])
+    sums = swap(sums, fours)
+    (input_grads,) = call(
+        input_grads_kernel,
+        [((2, EDGE, EDGE, WIDE), BF16)],
+        [
+            vmem((52, EDGE, WIDE), F32),
             vmem((2, 10 * ROWS, PADDED), F32),
             vmem((3, 10, 16, PADDED), BF16),
             vmem((512, 2304), BF16),
             vmem((128, 2304), BF16),
-            vmem((64, EDGE, WIDE), F32),
         ],
-        [me, neighbours, pre_grads, occupancy, even_in, odd_in, first_kernel],
+        [me, neighbours, pre_grads, occupancy, near, below, above, kept, first_kernel],
         scalars=2,
+        flops=2**28,
+    )
+    first_grads, second_grads = call(
+        unpack_kernel, [((64, 27 * 64), F32), ((64, 27 * 64), F32)], [], [sums]
     )
     return input_grads, first_grads.T, second_grads.T
 

time: 106 us -> 104 us (0.981)
  blocking collectives: 76.2 us -> 49.6 us
  starting transfers between devices: 10.1 us -> 28.6 us
  waiting for transfers between devices: 7.87 us -> 11.6 us
  Pallas kernels: 9.26 us -> 11.6 us
    all_to_all x6 -> x4, blocking collectives: 76.2 us -> 49.6 us  [the longest x2 27.9 us: swap(): lax.all_to_all(value, AXES, 0, 0, axis_index_groups=members, tiled=True)]
    ppermute x0 -> x4, starting transfers between devices: none -> 19.9 us  [the longest x2 13.6 us: send_on(): lax.ppermute(below, AXES, [(i + 4, i) for i in range(devices - 4)])]
    ppermute x0 -> x4, waiting for transfers between devices: none -> 5.26 us  [the longest x2 3.13 us: send_on(): lax.ppermute(below, AXES, [(i + 4, i) for i in range(devices - 4)])]
    pallas_call x7 -> x10, Pallas kernels: 9.26 us -> 11.6 us  [call(): pl.pallas_call(kernel, out_shape=[jax.ShapeDtypeStruct(shape, kind) for s...]
    all_to_all x1 -> x2, waiting for transfers between devices: 7.87 us -> 6.3 us  [swap(): lax.all_to_all(value, AXES, 0, 0, axis_index_groups=members, tiled=True)]
    all_to_all x1 -> x2, starting transfers between devices: 10.1 us -> 8.69 us  [swap(): lax.all_to_all(value, AXES, 0, 0, axis_index_groups=members, tiled=True)]
  transfers between devices with their start and end apart: 1 -> 6, of which waited for: 1 -> 4; matrix products, arithmetic and copies ran while one was open for 1% -> 1% of each run, Pallas kernels for 0% -> 2%
where the time goes in v3:
time: 104 us; the launch traced here: 103 us
  blocking collectives  49.6 us (48%)
  starting transfers between devices  28.6 us (28%)
  Pallas kernels  11.6 us (11%)
  waiting for transfers between devices  11.6 us (11%)
  local copies, waits for them, and re-layouts  1.23 us (1%)
    all_to_all x2, blocking collectives, swap(): lax.all_to_all(value, AXES, 0, 0, axis_index_groups=members, tiled=True)  27.9 us
    all_to_all x2, blocking collectives, per_device(): sums = lax.all_to_all(sums, 'grp', 0, 0, tiled=True)  21.7 us
    ppermute x2, starting transfers between devices, send_on(): lax.ppermute(below, AXES, [(i + 4, i) for i in range(devices - 4)])  13.6 us
    pallas_call x10, Pallas kernels, call(): pl.pallas_call(kernel, out_shape=[jax.ShapeDtypeStruct(shape, kind) for s...  11.6 us
    all_to_all x2, starting transfers between devices, swap(): lax.all_to_all(value, AXES, 0, 0, axis_index_groups=members, tiled=True)  8.69 us
    ppermute x2, starting transfers between devices, send_on(): lax.ppermute(above, AXES, [(i, i + 4) for i in range(devices - 4)])  6.32 us
    all_to_all x2, waiting for transfers between devices, swap(): lax.all_to_all(value, AXES, 0, 0, axis_index_groups=members, tiled=True)  6.3 us
    ppermute x2, waiting for transfers between devices, send_on(): lax.ppermute(below, AXES, [(i + 4, i) for i in range(devices - 4)])  3.13 us
  transfers between devices with their start and end apart: 6, of which 4 were waited for; matrix products, arithmetic and copies ran while one was open for 1% of the time, Pallas kernels for 2%

profile of v3, /device:TPU:1, one launch (start us, length us, event | category | flops | bytes accessed | tf_op | source)
XLA Modules:
  0.0 103.4 jit_solution(1174361196869946570)
XLA Ops:
  0.6 3.0 %shard_map.85 = (bf16[4,128,512]{2,1,0:T(8,128)(2,1)}, bf16[4,16,512]{2,1,0:T(8,128)(2,1)}, bf16[8,16,512]{2,1,0:T(8,128)(2,1)}) custom-call(s32[1]{0:T(128)} %bitcast.me_ref, s32[2,26]{1,0:T(2,128)} %nb_ref.5, bf16[2,8,8,512]{3,2,1,0:T(8,128)(2,1)} %x_ref.1, bf16[2,8,8,512]{3,2,1,0:T(8,128)(2,1)} %g_hbm.1, s32[2,8,64]{2,1,0:T(8,128)} %occ_ref.3), custom_call_target="tpu_custom_call" | custom-call | bytes 524288 | tf_op jit(solution)/shard_map/pallas_call | solution.py:419
  3.6 12.9 %all_to_all.30.near_ref = bf16[4,128,512]{2,1,0:T(8,128)(2,1)S(1)} all-to-all(bf16[4,128,512]{2,1,0:T(8,128)(2,1)} %get-tuple-element.16), channel_id=1, replica_groups={{0,1,2,3},{4,5,6,7},{8,9,10,11},{12,13,14,15},{16,17,18,19},{20,21,22,2..., dimensions={0} | all-to-all | bytes 1048576 | tf_op jit(solution)/shard_map/all_to_all | solution.py:445
  16.5 4.4 %collective-permute-start = (bf16[4,64,512]{2,1,0:T(8,128)(2,1)S(1)}, bf16[4,64,512]{2,1,0:T(8,128)(2,1)S(1)}, u32[]{:S(2)}, u32[]{:S(2)}) collective-permute-start(bf16[4,64,512]{2,1,0:T(8,128)(2,1)S(1)} %get-tuple-element.17), channel_id=1, source_target_pairs={{0,4},{1,5},{2,6},{3,7},{4,8},{5,9},{6,10},{7,11},{8,12},{9,13},{1... | collective-permute-start | bytes 786440 | tf_op jit(solution)/shard_map/ppermute | solution.py:450
  20.9 0.0 copy-start.6
  20.9 7.7 %collective-permute-start.1 = (bf16[4,64,512]{2,1,0:T(8,128)(2,1)S(1)}, bf16[4,64,512]{2,1,0:T(8,128)(2,1)S(1)}, u32[]{:S(2)}, u32[]{:S(2)}) collective-permute-start(bf16[4,64,512]{2,1,0:T(8,128)(2,1)S(1)} %get-tuple-element.18), channel_id=1, source_target_pairs={{4,0},{5,1},{6,2},{7,3},{8,4},{9,5},{10,6},{11,7},{12,8},{13,9},{1... | collective-permute-start | bytes 786440 | tf_op jit(solution)/shard_map/ppermute | solution.py:451
  28.7 0.0 copy-done.5
  28.7 0.3 copy.9.first_ref
  29.0 0.0 copy-start
  29.0 0.0 copy-start.1
  29.0 0.0 copy-start.3
  29.0 0.0 copy-start.4
  29.0 0.3 copy.10.second_ref
  29.3 2.1 %collective-permute-done.below_ref = bf16[4,64,512]{2,1,0:T(8,128)(2,1)S(1)} collective-permute-done((bf16[4,64,512]{2,1,0:T(8,128)(2,1)S(1)}, bf16[4,64,512]{2,1,0:T(8,128)(2,1)S(1)}, u32[]{:S(2)}, u32[]{:S(2)}) %collective-permute-start) | collective-permute-done | bytes 262176 | tf_op jit(solution)/shard_map/ppermute | solution.py:450
  31.4 0.6 collective-permute-done.1.above_ref
  32.0 0.7 copy-done.2
  32.7 3.5 %shard_map.87 = (bf16[8,16,512]{2,1,0:T(8,128)(2,1)S(1)}, bf16[4,192,512]{2,1,0:T(8,128)(2,1)S(1)}, f32[4,8,512]{2,1,0:T(8,128)S(1)}) custom-call(s32[1]{0:T(128)} %bitcast.me_ref, s32[2,26]{1,0:T(2,128)S(1)} %copy-done.2, bf16[2,8,8,512]{3,2,1,0:T(8,128)(2,1)S(1)} %copy-done, bf16[8,16,512]{2,1,0:T(8,128)(2,1)S(1)} %copy-done.3, s32[2,8,64]{2,1,0:T(8,128)S(1)} %copy-done.1, ...), custom_call_target="tpu_custom_call" | custom-call | flops 1073741824 | bytes 524288 | tf_op jit(solution)/shard_map/pallas_call | solution.py:419
  36.1 15.0 %all_to_all.31.near_ref.parts_ref = bf16[4,192,512]{2,1,0:T(8,128)(2,1)S(1)} all-to-all(bf16[4,192,512]{2,1,0:T(8,128)(2,1)S(1)} %get-tuple-element.21), channel_id=1, replica_groups={{0,1,2,3},{4,5,6,7},{8,9,10,11},{12,13,14,15},{16,17,18,19},{20,21,22,2..., dimensions={0} | all-to-all | bytes 1572864 | tf_op jit(solution)/shard_map/all_to_all | solution.py:445
  51.1 1.9 %collective-permute-start.2 = (bf16[4,32,512]{2,1,0:T(8,128)(2,1)S(1)}, bf16[4,32,512]{2,1,0:T(8,128)(2,1)S(1)}, u32[]{:S(2)}, u32[]{:S(2)}) collective-permute-start(bf16[4,32,512]{2,1,0:T(8,128)(2,1)S(1)} %get-tuple-element.22), channel_id=1, source_target_pairs={{0,4},{1,5},{2,6},{3,7},{4,8},{5,9},{6,10},{7,11},{8,12},{9,13},{1... | collective-permute-start | bytes 393224 | tf_op jit(solution)/shard_map/ppermute | solution.py:450
  53.1 0.1 shard_map.90
  53.2 12.3 %all_to_all.32.parts_ref = bf16[8,16,512]{2,1,0:T(8,128)(2,1)S(1)} all-to-all(bf16[8,16,512]{2,1,0:T(8,128)(2,1)S(1)} %shard_map.90), channel_id=1, replica_groups=mesh['grp'=8,'dev'=32] {'grp'}, dimensions={0} | all-to-all | bytes 262144 | tf_op jit(solution)/shard_map/all_to_all | solution.py:506
  65.4 0.0 collective-permute-done.2.below_ref.arrived_ref
  65.4 0.7 shard_map.91
  66.1 5.2 %all-to-all-start.3 = ((bf16[8,16,512]{2,1,0:T(8,128)(2,1)}), bf16[8,16,512]{2,1,0:T(8,128)(2,1)S(1)}, u32[]{:S(2)}, u32[]{:S(2)}) async-start(bf16[8,16,512]{2,1,0:T(8,128)(2,1)} %shard_map.91), calls=%async_computation.3 | async-start | bytes 262144 | tf_op jit(solution)/shard_map/all_to_all | solution.py:445
  71.3 5.9 %collective-permute-start.3 = (bf16[4,32,512]{2,1,0:T(8,128)(2,1)S(1)}, bf16[4,32,512]{2,1,0:T(8,128)(2,1)S(1)}, u32[]{:S(2)}, u32[]{:S(2)}) collective-permute-start(bf16[4,32,512]{2,1,0:T(8,128)(2,1)S(1)} %get-tuple-element.23), channel_id=1, source_target_pairs={{4,0},{5,1},{6,2},{7,3},{8,4},{9,5},{10,6},{11,7},{12,8},{13,9},{1... | collective-permute-start | bytes 393224 | tf_op jit(solution)/shard_map/ppermute | solution.py:451
  77.2 2.6 %collective-permute-done.3.above_ref.arrived_ref = bf16[4,32,512]{2,1,0:T(8,128)(2,1)S(1)} collective-permute-done((bf16[4,32,512]{2,1,0:T(8,128)(2,1)S(1)}, bf16[4,32,512]{2,1,0:T(8,128)(2,1)S(1)}, u32[]{:S(2)}, u32[]{:S(2)}) %collective-permute-start.3) | collective-permute-done | bytes 131104 | tf_op jit(solution)/shard_map/ppermute | solution.py:451
  79.8 0.0 all-to-all-done.3.parts_ref
  79.8 9.4 %all_to_all.33.pieces_ref = bf16[8,16,512]{2,1,0:T(8,128)(2,1)S(1)} all-to-all(bf16[8,16,512]{2,1,0:T(8,128)(2,1)S(1)} %shard_map.92), channel_id=1, replica_groups=mesh['grp'=8,'dev'=32] {'grp'}, dimensions={0} | all-to-all | bytes 262144 | tf_op jit(solution)/shard_map/all_to_all | solution.py:522
  89.2 0.8 shard_map.93
  90.1 3.5 %all-to-all-start.5 = ((bf16[4,128,512]{2,1,0:T(8,128)(2,1)}), bf16[4,128,512]{2,1,0:T(8,128)(2,1)S(1)}, u32[]{:S(2)}, u32[]{:S(2)}) async-start(bf16[4,128,512]{2,1,0:T(8,128)(2,1)} %shard_map.93), calls=%async_computation.5 | async-start | bytes 1048576 | tf_op jit(solution)/shard_map/all_to_all | solution.py:445
  93.6 2.3 %shard_map.89 = bf16[2,8,8,512]{3,2,1,0:T(8,128)(2,1)} custom-call(s32[1]{0:T(128)} %bitcast.me_ref, s32[2,26]{1,0:T(2,128)S(1)} %copy-done.2, bf16[8,16,512]{2,1,0:T(8,128)(2,1)S(1)} %get-tuple-element.20.grads_ref, s32[2,8,64]{2,1,0:T(8,128)S(1)} %copy-done.1, bf16[4,192,512]{2,1,0:T(8,128)(2,1)S(1)} %all_to_all.31.near_ref.parts_ref, ...), custom_call_target="tpu_custom_call" | custom-call | flops 268435456 | bytes 524288 | tf_op jit(solution)/shard_map/pallas_call | solution.py:419
  95.9 6.3 %all-to-all-done.5.parts_ref = bf16[4,128,512]{2,1,0:T(8,128)(2,1)S(1)} async-done(((bf16[4,128,512]{2,1,0:T(8,128)(2,1)}), bf16[4,128,512]{2,1,0:T(8,128)(2,1)S(1)}, u32[]{:S(2)}, u32[]{:S(2)}) %all-to-all-start.5) | async-done | bytes 524320 | tf_op jit(solution)/shard_map/all_to_all | solution.py:445
  102.2 1.2 %shard_map.94 = (f32[64,1728]{1,0:T(8,128)}, f32[64,1728]{1,0:T(8,128)}) custom-call(bf16[4,128,512]{2,1,0:T(8,128)(2,1)S(1)} %all-to-all-done.5.parts_ref), custom_call_target="tpu_custom_call" | custom-call | bytes 524288 | tf_op jit(solution)/shard_map/pallas_call | solution.py:419
  (10 shorter events, 0.1 us)
Async XLA Ops:
  16.5 12.2 %copy-start.5 = (bf16[1728,64]{0,1:T(8,128)(2,1)S(1)}, bf16[1728,64]{0,1:T(8,128)(2,1)}, u32[]{:S(2)}) copy-start(bf16[1728,64]{0,1:T(8,128)(2,1)} %param.9) | copy-start | bytes 663556
  16.5 14.9 %collective-permute-start = (bf16[4,64,512]{2,1,0:T(8,128)(2,1)S(1)}, bf16[4,64,512]{2,1,0:T(8,128)(2,1)S(1)}, u32[]{:S(2)}, u32[]{:S(2)}) collective-permute-start(bf16[4,64,512]{2,1,0:T(8,128)(2,1)S(1)} %get-tuple-element.17), channel_id=1, source_target_pairs={{0,4},{1,5},{2,6},{3,7},{4,8},{5,9},{6,10},{7,11},{8,12},{9,13},{1... | collective-permute-start | bytes 786440 | tf_op jit(solution)/shard_map/ppermute | solution.py:450
  20.9 8.0 %copy-start.6 = (bf16[1728,64]{0,1:T(8,128)(2,1)S(1)}, bf16[1728,64]{0,1:T(8,128)(2,1)}, u32[]{:S(2)}) copy-start(bf16[1728,64]{0,1:T(8,128)(2,1)} %param.10) | copy-start | bytes 663556
  20.9 11.0 %collective-permute-start.1 = (bf16[4,64,512]{2,1,0:T(8,128)(2,1)S(1)}, bf16[4,64,512]{2,1,0:T(8,128)(2,1)S(1)}, u32[]{:S(2)}, u32[]{:S(2)}) collective-permute-start(bf16[4,64,512]{2,1,0:T(8,128)(2,1)S(1)} %get-tuple-element.18), channel_id=1, source_target_pairs={{4,0},{5,1},{6,2},{7,3},{8,4},{9,5},{10,6},{11,7},{12,8},{13,9},{1... | collective-permute-start | bytes 786440 | tf_op jit(solution)/shard_map/ppermute | solution.py:451
  29.0 3.0 %copy-start = (bf16[2,8,8,512]{3,2,1,0:T(8,128)(2,1)S(1)}, bf16[2,8,8,512]{3,2,1,0:T(8,128)(2,1)}, u32[]{:S(2)}) copy-start(bf16[2,8,8,512]{3,2,1,0:T(8,128)(2,1)} %x_ref.1) | copy-start | bytes 393220
  29.0 3.0 %copy-start.1 = (s32[2,8,64]{2,1,0:T(8,128)S(1)}, s32[2,8,64]{2,1,0:T(8,128)}, u32[]{:S(2)}) copy-start(s32[2,8,64]{2,1,0:T(8,128)} %occ_ref.3) | copy-start | bytes 12292
  29.0 3.0 %copy-start.3 = (bf16[8,16,512]{2,1,0:T(8,128)(2,1)S(1)}, bf16[8,16,512]{2,1,0:T(8,128)(2,1)}, u32[]{:S(2)}) copy-start(bf16[8,16,512]{2,1,0:T(8,128)(2,1)} %get-tuple-element.15.masked_ref) | copy-start | bytes 393220
  29.0 3.0 %copy-start.4 = (bf16[4,16,512]{2,1,0:T(8,128)(2,1)S(1)}, bf16[4,16,512]{2,1,0:T(8,128)(2,1)}, u32[]{:S(2)}) copy-start(bf16[4,16,512]{2,1,0:T(8,128)(2,1)} %get-tuple-element.19.kept_in) | copy-start | bytes 196612
  32.0 0.7 copy-start.2
  51.1 14.3 %collective-permute-start.2 = (bf16[4,32,512]{2,1,0:T(8,128)(2,1)S(1)}, bf16[4,32,512]{2,1,0:T(8,128)(2,1)S(1)}, u32[]{:S(2)}, u32[]{:S(2)}) collective-permute-start(bf16[4,32,512]{2,1,0:T(8,128)(2,1)S(1)} %get-tuple-element.22), channel_id=1, source_target_pairs={{0,4},{1,5},{2,6},{3,7},{4,8},{5,9},{6,10},{7,11},{8,12},{9,13},{1... | collective-permute-start | bytes 393224 | tf_op jit(solution)/shard_map/ppermute | solution.py:450
  66.1 13.7 %all-to-all-start.3 = ((bf16[8,16,512]{2,1,0:T(8,128)(2,1)}), bf16[8,16,512]{2,1,0:T(8,128)(2,1)S(1)}, u32[]{:S(2)}, u32[]{:S(2)}) async-start(bf16[8,16,512]{2,1,0:T(8,128)(2,1)} %shard_map.91), calls=%async_computation.3 | async-start | bytes 262144 | tf_op jit(solution)/shard_map/all_to_all | solution.py:445
  71.3 8.5 %collective-permute-start.3 = (bf16[4,32,512]{2,1,0:T(8,128)(2,1)S(1)}, bf16[4,32,512]{2,1,0:T(8,128)(2,1)S(1)}, u32[]{:S(2)}, u32[]{:S(2)}) collective-permute-start(bf16[4,32,512]{2,1,0:T(8,128)(2,1)S(1)} %get-tuple-element.23), channel_id=1, source_target_pairs={{4,0},{5,1},{6,2},{7,3},{8,4},{9,5},{10,6},{11,7},{12,8},{13,9},{1... | collective-permute-start | bytes 393224 | tf_op jit(solution)/shard_map/ppermute | solution.py:451
  90.1 12.1 %all-to-all-start.5 = ((bf16[4,128,512]{2,1,0:T(8,128)(2,1)}), bf16[4,128,512]{2,1,0:T(8,128)(2,1)S(1)}, u32[]{:S(2)}, u32[]{:S(2)}) async-start(bf16[4,128,512]{2,1,0:T(8,128)(2,1)} %shard_map.93), calls=%async_computation.5 | async-start | bytes 1048576 | tf_op jit(solution)/shard_map/all_to_all | solution.py:445

commit v4 on v3

--- a/solution.py
+++ b/solution.py
@@ -333,20 +333,13 @@
     pieces_ref[...] = total.astype(BF16).reshape(pieces_ref.shape)
 
 
-def next_sum_kernel(scaling, arrived_ref, parts_ref, copies_ref):
-    del arrived_ref
+def next_sum_kernel(scaling, parts_ref, copies_ref):
     total = parts_ref[0].astype(F32)
     for member in range(1, parts_ref.shape[0]):
         total = total + parts_ref[member].astype(F32)
     total = total * scaling
     for member in range(copies_ref.shape[0]):
         copies_ref[member] = total.astype(copies_ref.dtype)
-
-
-def share_kernel(pieces_ref, copies_ref):
-    chunk = pieces_ref[...].reshape(128, WIDE)
-    for member in range(4):
-        copies_ref[member] = chunk
 
 
 def input_grads_kernel(
@@ -399,7 +392,13 @@
         for chunk in (2 * half, 2 * half + 1):
             rows.append(
                 jnp.concatenate(
-                    [parts_ref[chunk, 32 * part : 32 * part + 32, :] for part in range(4)],
+                    [
+                        jnp.concatenate(
+                            [parts_ref[4 * piece + chunk] for piece in (2 * part, 2 * part + 1)],
+                            axis=0,
+                        )
+                        for part in range(4)
+                    ],
                     axis=1,
                 )
             )
@@ -437,6 +436,10 @@
         [along_dev * grp + 4 * row + member for row in range(rows)]
         for grp in range(along_grp)
         for member in range(4)
+    ]
+    planes = [
+        [along_dev * grp + 4 * row + member for grp in range(along_grp) for member in range(4)]
+        for row in range(rows)
     ]
     me = (lax.axis_index("grp") * along_dev + lax.axis_index("dev")).reshape(1)
     vmem = pltpu.VMEM
@@ -504,24 +507,12 @@
     piece = (128 // along_grp, WIDE)
     (sums,) = call(first_sum_kernel, [((along_grp,) + piece, BF16)], [], [near])
     sums = lax.all_to_all(sums, "grp", 0, 0, tiled=True)
-    (sums,) = call(
-        functools.partial(next_sum_kernel, 1.0),
-        [((rows,) + piece, BF16)],
-        [],
-        [below, sums],
-        outside=1,
-    )
+    (sums,) = call(functools.partial(next_sum_kernel, 1.0), [((rows,) + piece, BF16)], [], [sums])
     sums = swap(sums, stacks)
     (sums,) = call(
-        functools.partial(next_sum_kernel, scaling),
-        [((along_grp,) + piece, BF16)],
-        [],
-        [above, sums],
-        outside=1,
-    )
-    sums = lax.all_to_all(sums, "grp", 0, 0, tiled=True)
-    (sums,) = call(share_kernel, [((4, 128, WIDE), BF16)], [], [sums])
-    sums = swap(sums, fours)
+        functools.partial(next_sum_kernel, scaling), [((4 * along_grp,) + piece, BF16)], [], [sums]
+    )
+    sums = swap(sums, planes)
     (input_grads,) = call(
         input_grads_kernel,
         [((2, EDGE, EDGE, WIDE), BF16)],

time: 104 us -> 95.1 us (0.914)
  waiting for transfers between devices: 11.6 us -> 4.67 us
  starting transfers between devices: 28.6 us -> 24.8 us
  blocking collectives: 49.6 us -> 51.6 us
    all_to_all x2 -> x3, blocking collectives: 27.9 us -> 39.9 us  [swap(): lax.all_to_all(value, AXES, 0, 0, axis_index_groups=members, tiled=True)]
    all_to_all x2 -> x1, blocking collectives: 21.7 us -> 11.7 us  [per_device(): sums = lax.all_to_all(sums, 'grp', 0, 0, tiled=True)]
    all_to_all x2 -> x1, waiting for transfers between devices: 6.3 us -> 0.05 us  [swap(): lax.all_to_all(value, AXES, 0, 0, axis_index_groups=members, tiled=True)]
    all_to_all x2 -> x1, starting transfers between devices: 8.69 us -> 5.93 us  [swap(): lax.all_to_all(value, AXES, 0, 0, axis_index_groups=members, tiled=True)]
    ppermute x2, waiting for transfers between devices: 3.13 us -> 0.85 us  [send_on(): lax.ppermute(below, AXES, [(i + 4, i) for i in range(devices - 4)])]
    ppermute x2, waiting for transfers between devices: 2.13 us -> 3.77 us  [send_on(): lax.ppermute(above, AXES, [(i, i + 4) for i in range(devices - 4)])]
    ppermute x2, starting transfers between devices: 13.6 us -> 12.3 us  [send_on(): lax.ppermute(below, AXES, [(i + 4, i) for i in range(devices - 4)])]
    pallas_call x10 -> x9, Pallas kernels: 11.6 us -> 11 us  [call(): pl.pallas_call(kernel, out_shape=[jax.ShapeDtypeStruct(shape, kind) for s...]
  transfers between devices with their start and end apart: 6 -> 5, of which waited for: 4 -> 5; matrix products, arithmetic and copies ran while one was open for 1% -> 1% of each run, Pallas kernels for 2% -> 2%
where the time goes in v4:
time: 95.1 us; the launch traced here: 94.1 us
  blocking collectives  51.6 us (54%)
  starting transfers between devices  24.8 us (26%)
  Pallas kernels  11 us (12%)
  waiting for transfers between devices  4.67 us (5%)
  local copies, waits for them, and re-layouts  1.23 us (1%)
    all_to_all x3, blocking collectives, swap(): lax.all_to_all(value, AXES, 0, 0, axis_index_groups=members, tiled=True)  39.9 us
    ppermute x2, starting transfers between devices, send_on(): lax.ppermute(below, AXES, [(i + 4, i) for i in range(devices - 4)])  12.3 us
    all_to_all x1, blocking collectives, per_device(): sums = lax.all_to_all(sums, 'grp', 0, 0, tiled=True)  11.7 us
    pallas_call x9, Pallas kernels, call(): pl.pallas_call(kernel, out_shape=[jax.ShapeDtypeStruct(shape, kind) for s...  11 us
    ppermute x2, starting transfers between devices, send_on(): lax.ppermute(above, AXES, [(i, i + 4) for i in range(devices - 4)])  6.59 us
    all_to_all x1, starting transfers between devices, swap(): lax.all_to_all(value, AXES, 0, 0, axis_index_groups=members, tiled=True)  5.93 us
    ppermute x2, waiting for transfers between devices, send_on(): lax.ppermute(above, AXES, [(i, i + 4) for i in range(devices - 4)])  3.77 us
  transfers between devices with their start and end apart: 5, of which 5 were waited for; matrix products, arithmetic and copies ran while one was open for 1% of the time, Pallas kernels for 2%

profile of v4, /device:TPU:1, one launch (start us, length us, event | category | flops | bytes accessed | tf_op | source)
XLA Modules:
  0.0 94.1 jit_solution(15372028060171407089)
XLA Ops:
  0.6 3.0 %shard_map.85 = (bf16[4,128,512]{2,1,0:T(8,128)(2,1)}, bf16[4,16,512]{2,1,0:T(8,128)(2,1)}, bf16[8,16,512]{2,1,0:T(8,128)(2,1)}) custom-call(s32[1]{0:T(128)} %bitcast.me_ref, s32[2,26]{1,0:T(2,128)} %nb_ref.5, bf16[2,8,8,512]{3,2,1,0:T(8,128)(2,1)} %x_ref.1, bf16[2,8,8,512]{3,2,1,0:T(8,128)(2,1)} %g_hbm.1, s32[2,8,64]{2,1,0:T(8,128)} %occ_ref.3), custom_call_target="tpu_custom_call" | custom-call | bytes 524288 | tf_op jit(solution)/shard_map/pallas_call | solution.py:418
  3.6 12.9 %all_to_all.25.near_ref = bf16[4,128,512]{2,1,0:T(8,128)(2,1)S(1)} all-to-all(bf16[4,128,512]{2,1,0:T(8,128)(2,1)} %get-tuple-element.16), channel_id=1, replica_groups={{0,1,2,3},{4,5,6,7},{8,9,10,11},{12,13,14,15},{16,17,18,19},{20,21,22,2..., dimensions={0} | all-to-all | bytes 1048576 | tf_op jit(solution)/shard_map/all_to_all | solution.py:448
  16.5 4.4 %collective-permute-start = (bf16[4,64,512]{2,1,0:T(8,128)(2,1)S(1)}, bf16[4,64,512]{2,1,0:T(8,128)(2,1)S(1)}, u32[]{:S(2)}, u32[]{:S(2)}) collective-permute-start(bf16[4,64,512]{2,1,0:T(8,128)(2,1)S(1)} %get-tuple-element.17), channel_id=1, source_target_pairs={{0,4},{1,5},{2,6},{3,7},{4,8},{5,9},{6,10},{7,11},{8,12},{9,13},{1... | collective-permute-start | bytes 786440 | tf_op jit(solution)/shard_map/ppermute | solution.py:453
  20.9 0.0 copy-start.6
  20.9 7.7 %collective-permute-start.1 = (bf16[4,64,512]{2,1,0:T(8,128)(2,1)S(1)}, bf16[4,64,512]{2,1,0:T(8,128)(2,1)S(1)}, u32[]{:S(2)}, u32[]{:S(2)}) collective-permute-start(bf16[4,64,512]{2,1,0:T(8,128)(2,1)S(1)} %get-tuple-element.18), channel_id=1, source_target_pairs={{4,0},{5,1},{6,2},{7,3},{8,4},{9,5},{10,6},{11,7},{12,8},{13,9},{1... | collective-permute-start | bytes 786440 | tf_op jit(solution)/shard_map/ppermute | solution.py:454
  28.7 0.0 copy-done.5
  28.7 0.3 copy.9.first_ref
  29.0 0.0 copy-done.6
  29.0 0.0 copy-start
  29.0 0.0 copy-start.1
  29.0 0.0 copy-start.3
  29.0 0.0 copy-start.4
  29.0 0.3 copy.10.second_ref
  29.3 2.1 %collective-permute-done.below_ref = bf16[4,64,512]{2,1,0:T(8,128)(2,1)S(1)} collective-permute-done((bf16[4,64,512]{2,1,0:T(8,128)(2,1)S(1)}, bf16[4,64,512]{2,1,0:T(8,128)(2,1)S(1)}, u32[]{:S(2)}, u32[]{:S(2)}) %collective-permute-start) | collective-permute-done | bytes 262176 | tf_op jit(solution)/shard_map/ppermute | solution.py:453
  31.4 0.6 collective-permute-done.1.above_ref
  32.0 0.0 copy-done
  32.0 0.0 copy-done.1
  32.0 0.7 copy-done.2
  32.7 3.5 %shard_map.87 = (bf16[8,16,512]{2,1,0:T(8,128)(2,1)S(1)}, bf16[4,192,512]{2,1,0:T(8,128)(2,1)S(1)}, f32[4,8,512]{2,1,0:T(8,128)S(1)}) custom-call(s32[1]{0:T(128)} %bitcast.me_ref, s32[2,26]{1,0:T(2,128)S(1)} %copy-done.2, bf16[2,8,8,512]{3,2,1,0:T(8,128)(2,1)S(1)} %copy-done, bf16[8,16,512]{2,1,0:T(8,128)(2,1)S(1)} %copy-done.3, s32[2,8,64]{2,1,0:T(8,128)S(1)} %copy-done.1, ...), custom_call_target="tpu_custom_call" | custom-call | flops 1073741824 | bytes 524288 | tf_op jit(solution)/shard_map/pallas_call | solution.py:418
  36.1 14.9 %all_to_all.26.near_ref.parts_ref = bf16[4,192,512]{2,1,0:T(8,128)(2,1)S(1)} all-to-all(bf16[4,192,512]{2,1,0:T(8,128)(2,1)S(1)} %get-tuple-element.21), channel_id=1, replica_groups={{0,1,2,3},{4,5,6,7},{8,9,10,11},{12,13,14,15},{16,17,18,19},{20,21,22,2..., dimensions={0} | all-to-all | bytes 1572864 | tf_op jit(solution)/shard_map/all_to_all | solution.py:448
  51.0 0.1 shard_map.90
  51.1 11.7 %all_to_all.27.parts_ref = bf16[8,16,512]{2,1,0:T(8,128)(2,1)S(1)} all-to-all(bf16[8,16,512]{2,1,0:T(8,128)(2,1)S(1)} %shard_map.90), channel_id=1, replica_groups=mesh['grp'=8,'dev'=32] {'grp'}, dimensions={0} | all-to-all | bytes 262144 | tf_op jit(solution)/shard_map/all_to_all | solution.py:509
  62.8 12.1 %all_to_all.28.parts_ref = bf16[8,16,512]{2,1,0:T(8,128)(2,1)S(1)} all-to-all(bf16[8,16,512]{2,1,0:T(8,128)(2,1)S(1)} %shard_map.91), channel_id=1, replica_groups={{0,4,8,12,16,20,24,28},{1,5,9,13,17,21,25,29},{2,6,10,14,18,22,26,30},{..., dimensions={0} | all-to-all | bytes 262144 | tf_op jit(solution)/shard_map/all_to_all | solution.py:448
  74.9 0.9 shard_map.92
  75.8 5.9 %all-to-all-start.4 = ((bf16[32,16,512]{2,1,0:T(8,128)(2,1)}), bf16[32,16,512]{2,1,0:T(8,128)(2,1)S(1)}, u32[]{:S(2)}, u32[]{:S(2)}) async-start(bf16[32,16,512]{2,1,0:T(8,128)(2,1)} %shard_map.92), calls=%async_computation.4 | async-start | bytes 1048576 | tf_op jit(solution)/shard_map/all_to_all | solution.py:448
  81.7 2.2 %collective-permute-start.2 = (bf16[4,32,512]{2,1,0:T(8,128)(2,1)S(1)}, bf16[4,32,512]{2,1,0:T(8,128)(2,1)S(1)}, u32[]{:S(2)}, u32[]{:S(2)}) collective-permute-start(bf16[4,32,512]{2,1,0:T(8,128)(2,1)S(1)} %get-tuple-element.22), channel_id=1, source_target_pairs={{0,4},{1,5},{2,6},{3,7},{4,8},{5,9},{6,10},{7,11},{8,12},{9,13},{1... | collective-permute-start | bytes 393224 | tf_op jit(solution)/shard_map/ppermute | solution.py:453
  83.9 4.6 %collective-permute-start.3 = (bf16[4,32,512]{2,1,0:T(8,128)(2,1)S(1)}, bf16[4,32,512]{2,1,0:T(8,128)(2,1)S(1)}, u32[]{:S(2)}, u32[]{:S(2)}) collective-permute-start(bf16[4,32,512]{2,1,0:T(8,128)(2,1)S(1)} %get-tuple-element.23), channel_id=1, source_target_pairs={{4,0},{5,1},{6,2},{7,3},{8,4},{9,5},{10,6},{11,7},{12,8},{13,9},{1... | collective-permute-start | bytes 393224 | tf_op jit(solution)/shard_map/ppermute | solution.py:454
  88.5 1.6 %collective-permute-done.2.below_ref = bf16[4,32,512]{2,1,0:T(8,128)(2,1)S(1)} collective-permute-done((bf16[4,32,512]{2,1,0:T(8,128)(2,1)S(1)}, bf16[4,32,512]{2,1,0:T(8,128)(2,1)S(1)}, u32[]{:S(2)}, u32[]{:S(2)}) %collective-permute-start.2) | collective-permute-done | bytes 131104 | tf_op jit(solution)/shard_map/ppermute | solution.py:453
  90.2 0.3 collective-permute-done.3.above_ref
  90.5 2.3 %shard_map.89 = bf16[2,8,8,512]{3,2,1,0:T(8,128)(2,1)} custom-call(s32[1]{0:T(128)} %bitcast.me_ref, s32[2,26]{1,0:T(2,128)S(1)} %copy-done.2, bf16[8,16,512]{2,1,0:T(8,128)(2,1)S(1)} %get-tuple-element.20.grads_ref, s32[2,8,64]{2,1,0:T(8,128)S(1)} %copy-done.1, bf16[4,192,512]{2,1,0:T(8,128)(2,1)S(1)} %all_to_all.26.near_ref.parts_ref, ...), custom_call_target="tpu_custom_call" | custom-call | flops 268435456 | bytes 524288 | tf_op jit(solution)/shard_map/pallas_call | solution.py:418
  92.8 0.1 all-to-all-done.4.parts_ref
  92.8 1.2 %shard_map.93 = (f32[64,1728]{1,0:T(8,128)}, f32[64,1728]{1,0:T(8,128)}) custom-call(bf16[32,16,512]{2,1,0:T(8,128)(2,1)S(1)} %all-to-all-done.4.parts_ref), custom_call_target="tpu_custom_call" | custom-call | bytes 524288 | tf_op jit(solution)/shard_map/pallas_call | solution.py:418
  (7 shorter events, 0.1 us)
Async XLA Ops:
  16.5 12.2 %copy-start.5 = (bf16[1728,64]{0,1:T(8,128)(2,1)S(1)}, bf16[1728,64]{0,1:T(8,128)(2,1)}, u32[]{:S(2)}) copy-start(bf16[1728,64]{0,1:T(8,128)(2,1)} %param.9) | copy-start | bytes 663556
  16.5 14.9 %collective-permute-start = (bf16[4,64,512]{2,1,0:T(8,128)(2,1)S(1)}, bf16[4,64,512]{2,1,0:T(8,128)(2,1)S(1)}, u32[]{:S(2)}, u32[]{:S(2)}) collective-permute-start(bf16[4,64,512]{2,1,0:T(8,128)(2,1)S(1)} %get-tuple-element.17), channel_id=1, source_target_pairs={{0,4},{1,5},{2,6},{3,7},{4,8},{5,9},{6,10},{7,11},{8,12},{9,13},{1... | collective-permute-start | bytes 786440 | tf_op jit(solution)/shard_map/ppermute | solution.py:453
  20.9 8.0 %copy-start.6 = (bf16[1728,64]{0,1:T(8,128)(2,1)S(1)}, bf16[1728,64]{0,1:T(8,128)(2,1)}, u32[]{:S(2)}) copy-start(bf16[1728,64]{0,1:T(8,128)(2,1)} %param.10) | copy-start | bytes 663556
  20.9 11.0 %collective-permute-start.1 = (bf16[4,64,512]{2,1,0:T(8,128)(2,1)S(1)}, bf16[4,64,512]{2,1,0:T(8,128)(2,1)S(1)}, u32[]{:S(2)}, u32[]{:S(2)}) collective-permute-start(bf16[4,64,512]{2,1,0:T(8,128)(2,1)S(1)} %get-tuple-element.18), channel_id=1, source_target_pairs={{4,0},{5,1},{6,2},{7,3},{8,4},{9,5},{10,6},{11,7},{12,8},{13,9},{1... | collective-permute-start | bytes 786440 | tf_op jit(solution)/shard_map/ppermute | solution.py:454
  29.0 3.0 %copy-start = (bf16[2,8,8,512]{3,2,1,0:T(8,128)(2,1)S(1)}, bf16[2,8,8,512]{3,2,1,0:T(8,128)(2,1)}, u32[]{:S(2)}) copy-start(bf16[2,8,8,512]{3,2,1,0:T(8,128)(2,1)} %x_ref.1) | copy-start | bytes 393220
  29.0 3.0 %copy-start.1 = (s32[2,8,64]{2,1,0:T(8,128)S(1)}, s32[2,8,64]{2,1,0:T(8,128)}, u32[]{:S(2)}) copy-start(s32[2,8,64]{2,1,0:T(8,128)} %occ_ref.3) | copy-start | bytes 12292
  29.0 3.0 %copy-start.3 = (bf16[8,16,512]{2,1,0:T(8,128)(2,1)S(1)}, bf16[8,16,512]{2,1,0:T(8,128)(2,1)}, u32[]{:S(2)}) copy-start(bf16[8,16,512]{2,1,0:T(8,128)(2,1)} %get-tuple-element.15.masked_ref) | copy-start | bytes 393220
  29.0 3.0 %copy-start.4 = (bf16[4,16,512]{2,1,0:T(8,128)(2,1)S(1)}, bf16[4,16,512]{2,1,0:T(8,128)(2,1)}, u32[]{:S(2)}) copy-start(bf16[4,16,512]{2,1,0:T(8,128)(2,1)} %get-tuple-element.19.kept_in) | copy-start | bytes 196612
  32.0 0.7 copy-start.2
  75.8 17.1 %all-to-all-start.4 = ((bf16[32,16,512]{2,1,0:T(8,128)(2,1)}), bf16[32,16,512]{2,1,0:T(8,128)(2,1)S(1)}, u32[]{:S(2)}, u32[]{:S(2)}) async-start(bf16[32,16,512]{2,1,0:T(8,128)(2,1)} %shard_map.92), calls=%async_computation.4 | async-start | bytes 1048576 | tf_op jit(solution)/shard_map/all_to_all | solution.py:448
  81.7 8.4 %collective-permute-start.2 = (bf16[4,32,512]{2,1,0:T(8,128)(2,1)S(1)}, bf16[4,32,512]{2,1,0:T(8,128)(2,1)S(1)}, u32[]{:S(2)}, u32[]{:S(2)}) collective-permute-start(bf16[4,32,512]{2,1,0:T(8,128)(2,1)S(1)} %get-tuple-element.22), channel_id=1, source_target_pairs={{0,4},{1,5},{2,6},{3,7},{4,8},{5,9},{6,10},{7,11},{8,12},{9,13},{1... | collective-permute-start | bytes 393224 | tf_op jit(solution)/shard_map/ppermute | solution.py:453
  83.9 6.5 %collective-permute-start.3 = (bf16[4,32,512]{2,1,0:T(8,128)(2,1)S(1)}, bf16[4,32,512]{2,1,0:T(8,128)(2,1)S(1)}, u32[]{:S(2)}, u32[]{:S(2)}) collective-permute-start(bf16[4,32,512]{2,1,0:T(8,128)(2,1)S(1)} %get-tuple-element.23), channel_id=1, source_target_pairs={{4,0},{5,1},{6,2},{7,3},{8,4},{9,5},{10,6},{11,7},{12,8},{13,9},{1... | collective-permute-start | bytes 393224 | tf_op jit(solution)/shard_map/ppermute | solution.py:454

commit v5 on v4

--- a/solution.py
+++ b/solution.py
@@ -13,7 +13,7 @@
 WIDE = 512
 PADDED = 640
 ROWS = 24
-PACKED = 2048
+PACKED = 1792
 BF16 = jnp.bfloat16
 F32 = jnp.float32
 
@@ -217,6 +217,24 @@
         flipped[64:128, lanes] = jnp.concatenate([none] + blocks, axis=1)
 
 
+def spread_kernel(
+    first_ref,
+    second_ref,
+    occ_ref,
+    nb_ref,
+    direct_ref,
+    flipped_ref,
+    first_flipped_ref,
+    occupied_ref,
+    near_nb_ref,
+):
+    near_nb_ref[...] = nb_ref[...]
+    occupied_ref[...] = spread(occ_ref)
+    fill_direct(first_ref, direct_ref)
+    fill_flipped(second_ref, flipped_ref)
+    fill_flipped(first_ref, first_flipped_ref)
+
+
 def times_flipped(windows, flipped):
     return lax.dot_general(
         windows, flipped, (((1,), (1,)), ((), ())), preferred_element_type=F32
@@ -240,18 +258,25 @@
     return jnp.concatenate(pieces, axis=1)
 
 
+def tile_place(chunk, tile):
+    row, lane = EDGE * (tile // 4), 128 * (tile % 4)
+    if row < 96:
+        return 32 * chunk + row % 32, WIDE * (row // 32) + lane
+    return 32 * chunk + row - 96 + 16 * (lane // 256), 3 * WIDE + lane % 256
+
+
 def main_kernel(
     me_ref,
     nb_ref,
     x_ref,
     masked_ref,
-    occ_ref,
+    occupied_ref,
     near_ref,
     below_ref,
     above_ref,
     kept_in,
-    first_ref,
-    second_ref,
+    direct,
+    flipped,
     grads_ref,
     out_ref,
     kept_ref,
@@ -259,8 +284,6 @@
     padded,
     shifted,
     windows,
-    direct,
-    flipped,
     product,
     wide,
     boxes,
@@ -288,9 +311,7 @@
         fill_padded(padded.at[1, brick], own_second, lambda offset: values[offset][8:16])
     for field in range(2):
         fill_windows(padded.at[field, 0], padded.at[field, 1], shifted.at[field], windows.at[field])
-    fill_direct(first_ref, direct)
-    fill_flipped(second_ref, flipped)
-    occupied = paired(spread(occ_ref))
+    occupied = paired(occupied_ref[...])
     pre_act = jnp.dot(windows[0], direct[...], preferred_element_type=F32)
     logistic = 1.0 / (1.0 + jnp.exp(-pre_act))
     hidden = (pre_act * logistic * occupied).astype(BF16)
@@ -319,18 +340,28 @@
         product[...] = jnp.dot(turned, windows[field], preferred_element_type=F32)
         packed = gather_blocks(product).astype(BF16)
         for chunk in range(2):
-            for part in range(4):
+            start = 32 * chunk
+            for part in range(3):
                 at = 64 + 32 * part
                 out_ref[2 * half + chunk, at : at + 32, :] = packed[
-                    32 * chunk : 32 * chunk + 32, part * WIDE : (part + 1) * WIDE
+                    start : start + 32, part * WIDE : (part + 1) * WIDE
                 ]
+            rest = packed[start : start + 32, 3 * WIDE :]
+            out_ref[2 * half + chunk, 160:176, :] = jnp.concatenate(
+                [rest[0:16], rest[16:32]], axis=1
+            )
 
 
 def first_sum_kernel(parts_ref, pieces_ref):
-    total = parts_ref[0, 64:192, :].astype(F32)
+    total = parts_ref[0, 64:176, :].astype(F32)
     for member in range(1, 4):
-        total = total + parts_ref[member, 64:192, :].astype(F32)
-    pieces_ref[...] = total.astype(BF16).reshape(pieces_ref.shape)
+        total = total + parts_ref[member, 64:176, :].astype(F32)
+    count = pieces_ref.shape[1]
+    for tile in range(56):
+        row, lane = EDGE * (tile // 4), 128 * (tile % 4)
+        pieces_ref[tile // count, tile % count] = total[
+            row : row + EDGE, lane : lane + 128
+        ].astype(BF16)
 
 
 def next_sum_kernel(scaling, parts_ref, copies_ref):
@@ -346,18 +377,17 @@
     me_ref,
     nb_ref,
     grads_ref,
-    occ_ref,
+    occupied_ref,
     near_ref,
     below_ref,
     above_ref,
     kept_ref,
-    first_ref,
+    flipped,
     out_ref,
     taken,
     padded,
     shifted,
     windows,
-    flipped,
 ):
     me = me_ref[0]
     for member in range(4):
@@ -377,49 +407,44 @@
 
         fill_padded(padded.at[brick], own, lambda offset: values[offset])
     fill_windows(padded.at[0], padded.at[1], shifted, windows)
-    fill_flipped(first_ref, flipped)
-    result = unpaired(times_flipped(windows[...], flipped[...])) * spread(occ_ref)
+    result = unpaired(times_flipped(windows[...], flipped[...])) * occupied_ref[...]
     for x in range(EDGE):
         for brick in range(2):
             at = 16 * x + EDGE * brick
             out_ref[brick, x] = result[at : at + EDGE].astype(BF16)
 
 
-def unpack_kernel(parts_ref, first_out, second_out):
-    halves = []
-    for half in range(2):
-        rows = []
-        for chunk in (2 * half, 2 * half + 1):
-            rows.append(
-                jnp.concatenate(
-                    [
-                        jnp.concatenate(
-                            [parts_ref[4 * piece + chunk] for piece in (2 * part, 2 * part + 1)],
-                            axis=0,
-                        )
-                        for part in range(4)
-                    ],
-                    axis=1,
-                )
-            )
-        halves.append(jnp.concatenate(rows, axis=0).astype(F32))
-    first_out[...] = halves[1][:, : 27 * 64]
+def unpack_kernel(parts_ref, first_hbm, second_hbm, first_out, second_out, halves, sems):
+    count = parts_ref.shape[1]
+    for chunk in (2, 3, 0, 1):
+        for tile in range(56):
+            row, lane = tile_place(chunk, tile)
+            halves[row : row + EDGE, lane : lane + 128] = parts_ref[
+                4 * (tile // count) + chunk, tile % count
+            ].astype(F32)
+    first_out[...] = halves[64:128, : 27 * 64]
+    first_copy = pltpu.make_async_copy(first_out, first_hbm, sems.at[0])
+    first_copy.start()
     blocks = []
     for pair in range(14):
-        turned = halves[0][:, pair * 128 : pair * 128 + 128].T
+        turned = halves[0:64, pair * 128 : pair * 128 + 128].T
         blocks += [turned[0:64], turned[64:128]]
     second_out[...] = jnp.concatenate(blocks[26::-1], axis=1)
-
-
-def call(kernel, shapes, scratch, arguments, scalars=0, outside=0, megabytes=40, flops=0):
+    second_copy = pltpu.make_async_copy(second_out, second_hbm, sems.at[1])
+    second_copy.start()
+    first_copy.wait()
+    second_copy.wait()
+
+
+def call(kernel, shapes, scratch, arguments, scalars=0, outside=0, leaving=False, megabytes=40, flops=0):
     specs = [pl.BlockSpec(memory_space=pltpu.SMEM)] * scalars
-    specs += [pl.BlockSpec(memory_space=pl.ANY)] * outside
+    specs += [pl.BlockSpec(memory_space=pltpu.HBM)] * outside
     specs += [pl.BlockSpec(memory_space=pltpu.VMEM)] * (len(arguments) - len(specs))
     return pl.pallas_call(
         kernel,
         out_shape=[jax.ShapeDtypeStruct(shape, kind) for shape, kind in shapes],
         in_specs=specs,
-        out_specs=[pl.BlockSpec(memory_space=pltpu.VMEM)] * len(shapes),
+        out_specs=[pl.BlockSpec(memory_space=pltpu.HBM if leaving else pltpu.VMEM)] * len(shapes),
         scratch_shapes=scratch,
         cost_estimate=pl.CostEstimate(flops=flops, bytes_accessed=2**19, transcendentals=0),
         compiler_params=pltpu.CompilerParams(vmem_limit_bytes=megabytes * 2**20),
@@ -456,7 +481,11 @@
 
     near, kept, masked = call(
         pack_kernel,
-        [((4, 128, WIDE), BF16), ((4, 16, WIDE), BF16), ((EDGE, 16, WIDE), BF16)],
+        [
+            ((4, 128, WIDE), BF16),
+            ((4, 16, WIDE), BF16),
+            ((EDGE, 16, WIDE), BF16),
+        ],
         [
             vmem((2, EDGE, EDGE, WIDE), BF16),
             vmem((2, EDGE, EDGE, WIDE), BF16),
@@ -472,39 +501,37 @@
     )
     near = swap(near, fours)
     below, above = send_on(near, 64)
+    direct, flipped, first_flipped, occupied, near_nb = call(
+        spread_kernel,
+        [
+            ((2304, 128), BF16),
+            ((128, 2304), BF16),
+            ((128, 2304), BF16),
+            ((128, WIDE), F32),
+            ((2, 26), jnp.int32),
+        ],
+        [],
+        [first_kernel, second_kernel, occupancy, neighbours],
+    )
     pre_grads, near, kept = call(
         main_kernel,
-        [((EDGE, 16, WIDE), BF16), ((4, 192, WIDE), BF16), ((4, EDGE, WIDE), F32)],
+        [((EDGE, 16, WIDE), BF16), ((4, 176, WIDE), BF16), ((4, EDGE, WIDE), F32)],
         [
             vmem((52, 16, WIDE), BF16),
             vmem((2, 2, 10 * ROWS, PADDED), F32),
             vmem((2, 3, 10, 16, PADDED), BF16),
             vmem((2, 512, 2304), BF16),
-            vmem((2304, 128), BF16),
-            vmem((128, 2304), BF16),
             vmem((128, 2304), F32),
             vmem((2, 64, WIDE), F32),
             vmem((36, EDGE, WIDE), F32),
         ],
-        [
-            me,
-            neighbours,
-            inputs,
-            masked,
-            occupancy,
-            near,
-            below,
-            above,
-            kept,
-            first_kernel,
-            second_kernel,
-        ],
+        [me, near_nb, inputs, masked, occupied, near, below, above, kept, direct, flipped],
         scalars=2,
         flops=2**30,
     )
     near = swap(near, fours)
     below, above = send_on(near, 32)
-    piece = (128 // along_grp, WIDE)
+    piece = (56 // along_grp, EDGE, 128)
     (sums,) = call(first_sum_kernel, [((along_grp,) + piece, BF16)], [], [near])
     sums = lax.all_to_all(sums, "grp", 0, 0, tiled=True)
     (sums,) = call(functools.partial(next_sum_kernel, 1.0), [((rows,) + piece, BF16)], [], [sums])
@@ -521,14 +548,22 @@
             vmem((2, 10 * ROWS, PADDED), F32),
             vmem((3, 10, 16, PADDED), BF16),
             vmem((512, 2304), BF16),
-            vmem((128, 2304), BF16),
         ],
-        [me, neighbours, pre_grads, occupancy, near, below, above, kept, first_kernel],
+        [me, near_nb, pre_grads, occupied, near, below, above, kept, first_flipped],
         scalars=2,
         flops=2**28,
     )
     first_grads, second_grads = call(
-        unpack_kernel, [((64, 27 * 64), F32), ((64, 27 * 64), F32)], [], [sums]
+        unpack_kernel,
+        [((64, 27 * 64), F32), ((64, 27 * 64), F32)],
+        [
+            vmem((64, 27 * 64), F32),
+            vmem((64, 27 * 64), F32),
+            vmem((128, PACKED), F32),
+            pltpu.SemaphoreType.DMA((2,)),
+        ],
+        [sums],
+        leaving=True,
     )
     return input_grads, first_grads.T, second_grads.T
 

time: 95.1 us -> 93.3 us (0.981)
    pallas_call x9 -> x10, Pallas kernels: 11 us -> 11.3 us  [call(): pl.pallas_call(kernel, out_shape=[jax.ShapeDtypeStruct(shape, kind) for s...]
  transfers between devices with their start and end apart: 5 -> 5, of which waited for: 5 -> 4; matrix products, arithmetic and copies ran while one was open for 1% -> 1% of each run, Pallas kernels for 2% -> 3%
where the time goes in v5:
time: 93.3 us; the launch traced here: 92.2 us
  blocking collectives  50.7 us (54%)
  starting transfers between devices  24.7 us (26%)
  Pallas kernels  11.3 us (12%)
  waiting for transfers between devices  3.79 us (4%)
  local copies, waits for them, and re-layouts  0.98 us (1%)
    all_to_all x3, blocking collectives, swap(): lax.all_to_all(value, AXES, 0, 0, axis_index_groups=members, tiled=True)  39.1 us
    ppermute x2, starting transfers between devices, send_on(): lax.ppermute(below, AXES, [(i + 4, i) for i in range(devices - 4)])  12.3 us
    all_to_all x1, blocking collectives, per_device(): sums = lax.all_to_all(sums, 'grp', 0, 0, tiled=True)  11.6 us
    pallas_call x10, Pallas kernels, call(): pl.pallas_call(kernel, out_shape=[jax.ShapeDtypeStruct(shape, kind) for s...  11.3 us
    ppermute x2, starting transfers between devices, send_on(): lax.ppermute(above, AXES, [(i, i + 4) for i in range(devices - 4)])  6.58 us
    all_to_all x1, starting transfers between devices, swap(): lax.all_to_all(value, AXES, 0, 0, axis_index_groups=members, tiled=True)  5.78 us
    ppermute x2, waiting for transfers between devices, send_on(): lax.ppermute(above, AXES, [(i, i + 4) for i in range(devices - 4)])  2.94 us
  transfers between devices with their start and end apart: 5, of which 4 were waited for; matrix products, arithmetic and copies ran while one was open for 1% of the time, Pallas kernels for 3%

profile of v5, /device:TPU:1, one launch (start us, length us, event | category | flops | bytes accessed | tf_op | source)
XLA Modules:
  0.0 92.2 jit_solution(10381932795355485041)
XLA Ops:
  0.6 3.0 %shard_map.86 = (bf16[4,128,512]{2,1,0:T(8,128)(2,1)}, bf16[4,16,512]{2,1,0:T(8,128)(2,1)}, bf16[8,16,512]{2,1,0:T(8,128)(2,1)}) custom-call(s32[1]{0:T(128)} %bitcast.me_ref, s32[2,26]{1,0:T(2,128)} %nb_ref.3, bf16[2,8,8,512]{3,2,1,0:T(8,128)(2,1)} %x_ref.1, bf16[2,8,8,512]{3,2,1,0:T(8,128)(2,1)} %g_hbm.1, s32[2,8,64]{2,1,0:T(8,128)} %occ_hbm.1), custom_call_target="tpu_custom_call" | custom-call | bytes 524288 | tf_op jit(solution)/shard_map/pallas_call | solution.py:443
  3.6 12.9 %all_to_all.25.near_ref = bf16[4,128,512]{2,1,0:T(8,128)(2,1)S(1)} all-to-all(bf16[4,128,512]{2,1,0:T(8,128)(2,1)} %get-tuple-element.23), channel_id=1, replica_groups={{0,1,2,3},{4,5,6,7},{8,9,10,11},{12,13,14,15},{16,17,18,19},{20,21,22,2..., dimensions={0} | all-to-all | bytes 1048576 | tf_op jit(solution)/shard_map/all_to_all | solution.py:473
  16.5 4.4 %collective-permute-start = (bf16[4,64,512]{2,1,0:T(8,128)(2,1)S(1)}, bf16[4,64,512]{2,1,0:T(8,128)(2,1)S(1)}, u32[]{:S(2)}, u32[]{:S(2)}) collective-permute-start(bf16[4,64,512]{2,1,0:T(8,128)(2,1)S(1)} %get-tuple-element.24), channel_id=1, source_target_pairs={{0,4},{1,5},{2,6},{3,7},{4,8},{5,9},{6,10},{7,11},{8,12},{9,13},{1... | collective-permute-start | bytes 786440 | tf_op jit(solution)/shard_map/ppermute | solution.py:478
  20.9 0.0 copy-start.6
  20.9 7.8 %collective-permute-start.1 = (bf16[4,64,512]{2,1,0:T(8,128)(2,1)S(1)}, bf16[4,64,512]{2,1,0:T(8,128)(2,1)S(1)}, u32[]{:S(2)}, u32[]{:S(2)}) collective-permute-start(bf16[4,64,512]{2,1,0:T(8,128)(2,1)S(1)} %get-tuple-element.25), channel_id=1, source_target_pairs={{4,0},{5,1},{6,2},{7,3},{8,4},{9,5},{10,6},{11,7},{12,8},{13,9},{1... | collective-permute-start | bytes 786440 | tf_op jit(solution)/shard_map/ppermute | solution.py:479
  28.7 0.0 copy-done.5
  28.7 0.3 copy.9.first_ref
  29.0 0.0 copy-done.6
  29.0 0.0 copy-start.1
  29.0 0.0 copy-start.2
  29.0 0.3 copy.10.second_ref
  29.3 0.4 copy-done.1
  29.7 0.0 copy-done.2
  29.7 0.4 shard_map.85
  30.1 1.3 %collective-permute-done.below_ref = bf16[4,64,512]{2,1,0:T(8,128)(2,1)S(1)} collective-permute-done((bf16[4,64,512]{2,1,0:T(8,128)(2,1)S(1)}, bf16[4,64,512]{2,1,0:T(8,128)(2,1)S(1)}, u32[]{:S(2)}, u32[]{:S(2)}) %collective-permute-start) | collective-permute-done | bytes 262176 | tf_op jit(solution)/shard_map/ppermute | solution.py:478
  31.4 0.6 collective-permute-done.1.above_ref
  32.0 0.0 copy-done
  32.0 0.0 copy-done.3
  32.0 3.4 %shard_map.88 = (bf16[8,16,512]{2,1,0:T(8,128)(2,1)S(1)}, bf16[4,176,512]{2,1,0:T(8,128)(2,1)S(1)}, f32[4,8,512]{2,1,0:T(8,128)S(1)}) custom-call(s32[1]{0:T(128)} %bitcast.me_ref, s32[2,26]{1,0:T(2,128)S(1)} %get-tuple-element.20.nb_ref, bf16[2,8,8,512]{3,2,1,0:T(8,128)(2,1)S(1)} %copy-done, bf16[8,16,512]{2,1,0:T(8,128)(2,1)S(1)} %copy-done.3, ...), custom_call_target="tpu_custom_call" | custom-call | flops 1073741824 | bytes 524288 | tf_op jit(solution)/shard_map/pallas_call | solution.py:443
  35.4 14.1 %all_to_all.26.near_ref.parts_ref = bf16[4,176,512]{2,1,0:T(8,128)(2,1)S(1)} all-to-all(bf16[4,176,512]{2,1,0:T(8,128)(2,1)S(1)} %get-tuple-element.30), channel_id=1, replica_groups={{0,1,2,3},{4,5,6,7},{8,9,10,11},{12,13,14,15},{16,17,18,19},{20,21,22,2..., dimensions={0} | all-to-all | bytes 1441792 | tf_op jit(solution)/shard_map/all_to_all | solution.py:473
  49.5 0.1 shard_map.91
  49.6 11.6 %all_to_all.27.parts_ref = bf16[8,7,8,128]{3,2,1,0:T(8,128)(2,1)S(1)} all-to-all(bf16[8,7,8,128]{3,2,1,0:T(8,128)(2,1)S(1)} %shard_map.91), channel_id=1, replica_groups=mesh['grp'=8,'dev'=32] {'grp'}, dimensions={0} | all-to-all | bytes 229376 | tf_op jit(solution)/shard_map/all_to_all | solution.py:536
  61.2 12.1 %all_to_all.28.parts_ref = bf16[8,7,8,128]{3,2,1,0:T(8,128)(2,1)S(1)} all-to-all(bf16[8,7,8,128]{3,2,1,0:T(8,128)(2,1)S(1)} %shard_map.92), channel_id=1, replica_groups={{0,4,8,12,16,20,24,28},{1,5,9,13,17,21,25,29},{2,6,10,14,18,22,26,30},{..., dimensions={0} | all-to-all | bytes 229376 | tf_op jit(solution)/shard_map/all_to_all | solution.py:473
  73.3 0.8 shard_map.93
  74.1 5.8 %all-to-all-start.4 = ((bf16[32,7,8,128]{3,2,1,0:T(8,128)(2,1)}), bf16[32,7,8,128]{3,2,1,0:T(8,128)(2,1)S(1)}, u32[]{:S(2)}, u32[]{:S(2)}) async-start(bf16[32,7,8,128]{3,2,1,0:T(8,128)(2,1)} %shard_map.93), calls=%async_computation.4 | async-start | bytes 917504 | tf_op jit(solution)/shard_map/all_to_all | solution.py:473
  79.9 2.2 %collective-permute-start.2 = (bf16[4,32,512]{2,1,0:T(8,128)(2,1)S(1)}, bf16[4,32,512]{2,1,0:T(8,128)(2,1)S(1)}, u32[]{:S(2)}, u32[]{:S(2)}) collective-permute-start(bf16[4,32,512]{2,1,0:T(8,128)(2,1)S(1)} %get-tuple-element.31), channel_id=1, source_target_pairs={{0,4},{1,5},{2,6},{3,7},{4,8},{5,9},{6,10},{7,11},{8,12},{9,13},{1... | collective-permute-start | bytes 393224 | tf_op jit(solution)/shard_map/ppermute | solution.py:478
  82.1 4.6 %collective-permute-start.3 = (bf16[4,32,512]{2,1,0:T(8,128)(2,1)S(1)}, bf16[4,32,512]{2,1,0:T(8,128)(2,1)S(1)}, u32[]{:S(2)}, u32[]{:S(2)}) collective-permute-start(bf16[4,32,512]{2,1,0:T(8,128)(2,1)S(1)} %get-tuple-element.32), channel_id=1, source_target_pairs={{4,0},{5,1},{6,2},{7,3},{8,4},{9,5},{10,6},{11,7},{12,8},{13,9},{1... | collective-permute-start | bytes 393224 | tf_op jit(solution)/shard_map/ppermute | solution.py:479
  86.7 1.6 %collective-permute-done.2.below_ref = bf16[4,32,512]{2,1,0:T(8,128)(2,1)S(1)} collective-permute-done((bf16[4,32,512]{2,1,0:T(8,128)(2,1)S(1)}, bf16[4,32,512]{2,1,0:T(8,128)(2,1)S(1)}, u32[]{:S(2)}, u32[]{:S(2)}) %collective-permute-start.2) | collective-permute-done | bytes 131104 | tf_op jit(solution)/shard_map/ppermute | solution.py:478
  88.3 0.3 collective-permute-done.3.above_ref
  88.6 2.3 %shard_map.90 = bf16[2,8,8,512]{3,2,1,0:T(8,128)(2,1)} custom-call(s32[1]{0:T(128)} %bitcast.me_ref, s32[2,26]{1,0:T(2,128)S(1)} %get-tuple-element.20.nb_ref, bf16[8,16,512]{2,1,0:T(8,128)(2,1)S(1)} %get-tuple-element.29.grads_ref, f32[128,512]{1,0:T(8,128)S(1)} %get-tuple-element.22.occupied_ref, bf16[4,176,512]{2,1,0:T(8,128)(2,1)S(1)} %all_to_all.26.near_ref.parts_ref, ...), custom_call_target="tpu_custom_call" | custom-call | flops 268435456 | bytes 524288 | tf_op jit(solution)/shard_map/pallas_call | solution.py:443
  90.9 0.0 all-to-all-done.4.parts_ref
  90.9 1.2 %shard_map.94 = (f32[64,1728]{1,0:T(8,128)}, f32[64,1728]{1,0:T(8,128)}) custom-call(bf16[32,7,8,128]{3,2,1,0:T(8,128)(2,1)S(1)} %all-to-all-done.4.parts_ref), custom_call_target="tpu_custom_call" | custom-call | bytes 524288 | tf_op jit(solution)/shard_map/pallas_call | solution.py:443
  (8 shorter events, 0.1 us)
Async XLA Ops:
  16.5 12.2 %copy-start.5 = (bf16[1728,64]{0,1:T(8,128)(2,1)S(1)}, bf16[1728,64]{0,1:T(8,128)(2,1)}, u32[]{:S(2)}) copy-start(bf16[1728,64]{0,1:T(8,128)(2,1)} %param.9) | copy-start | bytes 663556
  16.5 14.9 %collective-permute-start = (bf16[4,64,512]{2,1,0:T(8,128)(2,1)S(1)}, bf16[4,64,512]{2,1,0:T(8,128)(2,1)S(1)}, u32[]{:S(2)}, u32[]{:S(2)}) collective-permute-start(bf16[4,64,512]{2,1,0:T(8,128)(2,1)S(1)} %get-tuple-element.24), channel_id=1, source_target_pairs={{0,4},{1,5},{2,6},{3,7},{4,8},{5,9},{6,10},{7,11},{8,12},{9,13},{1... | collective-permute-start | bytes 786440 | tf_op jit(solution)/shard_map/ppermute | solution.py:478
  20.9 8.1 %copy-start.6 = (bf16[1728,64]{0,1:T(8,128)(2,1)S(1)}, bf16[1728,64]{0,1:T(8,128)(2,1)}, u32[]{:S(2)}) copy-start(bf16[1728,64]{0,1:T(8,128)(2,1)} %param.10) | copy-start | bytes 663556
  20.9 11.1 %collective-permute-start.1 = (bf16[4,64,512]{2,1,0:T(8,128)(2,1)S(1)}, bf16[4,64,512]{2,1,0:T(8,128)(2,1)S(1)}, u32[]{:S(2)}, u32[]{:S(2)}) collective-permute-start(bf16[4,64,512]{2,1,0:T(8,128)(2,1)S(1)} %get-tuple-element.25), channel_id=1, source_target_pairs={{4,0},{5,1},{6,2},{7,3},{8,4},{9,5},{10,6},{11,7},{12,8},{13,9},{1... | collective-permute-start | bytes 786440 | tf_op jit(solution)/shard_map/ppermute | solution.py:479
  29.0 0.7 copy-start.1
  29.0 0.7 copy-start.2
  29.7 2.3 %copy-start = (bf16[2,8,8,512]{3,2,1,0:T(8,128)(2,1)S(1)}, bf16[2,8,8,512]{3,2,1,0:T(8,128)(2,1)}, u32[]{:S(2)}) copy-start(bf16[2,8,8,512]{3,2,1,0:T(8,128)(2,1)} %x_ref.1) | copy-start | bytes 393220
  29.7 2.3 %copy-start.3 = (bf16[8,16,512]{2,1,0:T(8,128)(2,1)S(1)}, bf16[8,16,512]{2,1,0:T(8,128)(2,1)}, u32[]{:S(2)}) copy-start(bf16[8,16,512]{2,1,0:T(8,128)(2,1)} %get-tuple-element.21.masked_ref) | copy-start | bytes 393220
  29.7 2.3 %copy-start.4 = (bf16[4,16,512]{2,1,0:T(8,128)(2,1)S(1)}, bf16[4,16,512]{2,1,0:T(8,128)(2,1)}, u32[]{:S(2)}) copy-start(bf16[4,16,512]{2,1,0:T(8,128)(2,1)} %get-tuple-element.26.kept_in) | copy-start | bytes 196612
  74.1 16.9 %all-to-all-start.4 = ((bf16[32,7,8,128]{3,2,1,0:T(8,128)(2,1)}), bf16[32,7,8,128]{3,2,1,0:T(8,128)(2,1)S(1)}, u32[]{:S(2)}, u32[]{:S(2)}) async-start(bf16[32,7,8,128]{3,2,1,0:T(8,128)(2,1)} %shard_map.93), calls=%async_computation.4 | async-start | bytes 917504 | tf_op jit(solution)/shard_map/all_to_all | solution.py:473
  79.9 8.4 %collective-permute-start.2 = (bf16[4,32,512]{2,1,0:T(8,128)(2,1)S(1)}, bf16[4,32,512]{2,1,0:T(8,128)(2,1)S(1)}, u32[]{:S(2)}, u32[]{:S(2)}) collective-permute-start(bf16[4,32,512]{2,1,0:T(8,128)(2,1)S(1)} %get-tuple-element.31), channel_id=1, source_target_pairs={{0,4},{1,5},{2,6},{3,7},{4,8},{5,9},{6,10},{7,11},{8,12},{9,13},{1... | collective-permute-start | bytes 393224 | tf_op jit(solution)/shard_map/ppermute | solution.py:478
  82.1 6.5 %collective-permute-start.3 = (bf16[4,32,512]{2,1,0:T(8,128)(2,1)S(1)}, bf16[4,32,512]{2,1,0:T(8,128)(2,1)S(1)}, u32[]{:S(2)}, u32[]{:S(2)}) collective-permute-start(bf16[4,32,512]{2,1,0:T(8,128)(2,1)S(1)} %get-tuple-element.32), channel_id=1, source_target_pairs={{4,0},{5,1},{6,2},{7,3},{8,4},{9,5},{10,6},{11,7},{12,8},{13,9},{1... | collective-permute-start | bytes 393224 | tf_op jit(solution)/shard_map/ppermute | solution.py:479

commit v6 on v5

--- a/solution.py
+++ b/solution.py
@@ -48,8 +48,10 @@
 
 def take_place(nb_ref, me, brick, number):
     present, member, up, own, slot = locate(nb_ref, me, brick, number)
-    place = member * 4 + jnp.where(up == 0, 0, jnp.where(up < 0, 16, 32))
-    return present, jnp.where(own, 48, place) + slot * 2 + brick
+    longer = (up < 0) == ((me & 3) < 2)
+    relayed = jnp.where(longer, 16 + 4 * member, 32 + 4 * (member & 1))
+    place = jnp.where(up == 0, 4 * member, relayed)
+    return present, jnp.where(own, 40, place) + slot * 2 + brick
 
 
 def face_kind(offset):
@@ -92,7 +94,7 @@
 
 def pack_kernel(
     me_ref,
-    nb_ref,
+    nb_hbm,
     x_hbm,
     g_hbm,
     occ_hbm,
@@ -104,12 +106,13 @@
     occ_ref,
     wide,
     boxes,
+    nb_ref,
     sems,
 ):
     copies = [
         pltpu.make_async_copy(source, target, sems.at[number])
         for number, (source, target) in enumerate(
-            ((occ_hbm, occ_ref), (g_hbm, g_ref), (x_hbm, x_ref))
+            ((occ_hbm, occ_ref), (g_hbm, g_ref), (x_hbm, x_ref), (nb_hbm, nb_ref))
         )
     ]
     for copy in copies:
@@ -128,6 +131,7 @@
             wide[2 + brick, x * EDGE : (x + 1) * EDGE, :] = piece
             both.append(piece)
         masked_ref[x] = jnp.concatenate(both, axis=0).astype(BF16)
+    copies[3].wait()
     for brick in range(2):
         first = face_values(wide, brick)
         second = face_values(wide, 2 + brick)
@@ -140,12 +144,20 @@
     kept_ref[...] = boxes[32:36]
 
 
-def route_kernel(me_ref, near_ref, above_ref, below_ref):
-    size = above_ref.shape[1]
+def route_kernel(me_ref, near_ref, longer_ref, shorter_ref):
+    size = longer_ref.shape[1]
     own = me_ref[0] & 3
-    above_ref[...] = near_ref[:, size : 2 * size, :]
-    below_ref[...] = near_ref[:, size : 2 * size, :]
-    below_ref[own] = near_ref[own, 0:size, :]
+    longer_ref[...] = near_ref[:, size : 2 * size, :]
+    for number in range(2):
+        shorter_ref[number] = near_ref[(own & 2) + number, size : 2 * size, :]
+
+    @pl.when(own >= 2)
+    def _():
+        longer_ref[own] = near_ref[own, 0:size, :]
+
+    @pl.when(own < 2)
+    def _():
+        shorter_ref[own & 1] = near_ref[own, 0:size, :]
 
 
 def beside(low, middle, high):
@@ -272,8 +284,8 @@
     masked_ref,
     occupied_ref,
     near_ref,
-    below_ref,
-    above_ref,
+    longer_ref,
+    shorter_ref,
     kept_in,
     direct,
     flipped,
@@ -292,9 +304,10 @@
     for member in range(4):
         at = 4 * member
         taken[at : at + 4] = near_ref[member, 0:64, :].reshape(4, 16, WIDE)
-        taken[at + 16 : at + 20] = below_ref[member].reshape(4, 16, WIDE)
-        taken[at + 32 : at + 36] = above_ref[member].reshape(4, 16, WIDE)
-    taken[48:52] = kept_in[...]
+        taken[at + 16 : at + 20] = longer_ref[member].reshape(4, 16, WIDE)
+    for number in range(2):
+        taken[32 + 4 * number : 36 + 4 * number] = shorter_ref[number].reshape(4, 16, WIDE)
+    taken[40:44] = kept_in[...]
     for brick in range(2):
         values = {}
         for number, offset in enumerate(DIRECTIONS):
@@ -379,8 +392,8 @@
     grads_ref,
     occupied_ref,
     near_ref,
-    below_ref,
-    above_ref,
+    longer_ref,
+    shorter_ref,
     kept_ref,
     flipped,
     out_ref,
@@ -393,9 +406,12 @@
     for member in range(4):
         at = 4 * member
         taken[at : at + 4] = near_ref[member, 0:32, :].astype(F32).reshape(4, EDGE, WIDE)
-        taken[at + 16 : at + 20] = below_ref[member].astype(F32).reshape(4, EDGE, WIDE)
-        taken[at + 32 : at + 36] = above_ref[member].astype(F32).reshape(4, EDGE, WIDE)
-    taken[48:52] = kept_ref[...]
+        taken[at + 16 : at + 20] = longer_ref[member].astype(F32).reshape(4, EDGE, WIDE)
+    for number in range(2):
+        taken[32 + 4 * number : 36 + 4 * number] = (
+            shorter_ref[number].astype(F32).reshape(4, EDGE, WIDE)
+        )
+    taken[40:44] = kept_ref[...]
     for brick in range(2):
         values = {}
         for number, offset in enumerate(DIRECTIONS):
@@ -472,12 +488,21 @@
     def swap(value, members):
         return lax.all_to_all(value, AXES, 0, 0, axis_index_groups=members, tiled=True)
 
+    longer_way = [(i, i + 4 if i & 2 == 0 else i - 4) for i in range(devices)]
+    shorter_way = [(i, i - 4 if i & 2 == 0 else i + 4) for i in range(devices)]
+
     def send_on(near, size):
-        packets = ((4, size, WIDE), BF16)
-        above, below = call(route_kernel, [packets, packets], [], [me, near], scalars=1)
-        from_below = lax.ppermute(above, AXES, [(i, i + 4) for i in range(devices - 4)])
-        from_above = lax.ppermute(below, AXES, [(i + 4, i) for i in range(devices - 4)])
-        return from_below, from_above
+        longer, shorter = call(
+            route_kernel,
+            [((4, size, WIDE), BF16), ((2, size, WIDE), BF16)],
+            [],
+            [me, near],
+            scalars=1,
+        )
+        return [
+            lax.ppermute(value, AXES, [(i, j) for i, j in way if 0 <= j < devices])
+            for value, way in ((longer, longer_way), (shorter, shorter_way))
+        ]
 
     near, kept, masked = call(
         pack_kernel,
@@ -492,15 +517,16 @@
             vmem((2, EDGE, 64), jnp.int32),
             vmem((4, 64, WIDE), F32),
             vmem((36, 16, WIDE), BF16),
-            pltpu.SemaphoreType.DMA((3,)),
+            pltpu.SMEM((2, 26), jnp.int32),
+            pltpu.SemaphoreType.DMA((4,)),
         ],
         [me, neighbours, inputs, out_grads, occupancy],
-        scalars=2,
-        outside=3,
+        scalars=1,
+        outside=4,
         megabytes=60,
     )
     near = swap(near, fours)
-    below, above = send_on(near, 64)
+    longer, shorter = send_on(near, 64)
     direct, flipped, first_flipped, occupied, near_nb = call(
         spread_kernel,
         [
@@ -517,7 +543,7 @@
         main_kernel,
         [((EDGE, 16, WIDE), BF16), ((4, 176, WIDE), BF16), ((4, EDGE, WIDE), F32)],
         [
-            vmem((52, 16, WIDE), BF16),
+            vmem((44, 16, WIDE), BF16),
             vmem((2, 2, 10 * ROWS, PADDED), F32),
             vmem((2, 3, 10, 16, PADDED), BF16),
             vmem((2, 512, 2304), BF16),
@@ -525,12 +551,12 @@
             vmem((2, 64, WIDE), F32),
             vmem((36, EDGE, WIDE), F32),
         ],
-        [me, near_nb, inputs, masked, occupied, near, below, above, kept, direct, flipped],
+        [me, near_nb, inputs, masked, occupied, near, longer, shorter, kept, direct, flipped],
         scalars=2,
         flops=2**30,
     )
     near = swap(near, fours)
-    below, above = send_on(near, 32)
+    longer, shorter = send_on(near, 32)
     piece = (56 // along_grp, EDGE, 128)
     (sums,) = call(first_sum_kernel, [((along_grp,) + piece, BF16)], [], [near])
     sums = lax.all_to_all(sums, "grp", 0, 0, tiled=True)
@@ -544,12 +570,12 @@
         input_grads_kernel,
         [((2, EDGE, EDGE, WIDE), BF16)],
         [
-            vmem((52, EDGE, WIDE), F32),
+            vmem((44, EDGE, WIDE), F32),
             vmem((2, 10 * ROWS, PADDED), F32),
             vmem((3, 10, 16, PADDED), BF16),
             vmem((512, 2304), BF16),
         ],
-        [me, near_nb, pre_grads, occupied, near, below, above, kept, first_flipped],
+        [me, near_nb, pre_grads, occupied, near, longer, shorter, kept, first_flipped],
         scalars=2,
         flops=2**28,
     )

time: 93.3 us -> 90.7 us (0.972)
  blocking collectives: 50.7 us -> 49.7 us
    all_to_all x3, blocking collectives: 39.1 us -> 36.2 us  [swap(): lax.all_to_all(value, AXES, 0, 0, axis_index_groups=members, tiled=True)]
    all_to_all x1, blocking collectives: 11.6 us -> 13.4 us  [per_device(): sums = lax.all_to_all(sums, 'grp', 0, 0, tiled=True)]
where the time goes in v6:
time: 90.7 us; the launch traced here: 89.7 us
  blocking collectives  49.7 us (55%)
  starting transfers between devices  24.6 us (27%)
  Pallas kernels  10.7 us (12%)
  waiting for transfers between devices  2.94 us (3%)
  local copies, waits for them, and re-layouts  0.98 us (1%)
    all_to_all x3, blocking collectives, swap(): lax.all_to_all(value, AXES, 0, 0, axis_index_groups=members, tiled=True)  36.2 us
    ppermute x4, starting transfers between devices, send_on(): lax.ppermute(value, AXES, [(i, j) for i, j in way if 0 <= j < devices])  18.9 us
    all_to_all x1, blocking collectives, per_device(): sums = lax.all_to_all(sums, 'grp', 0, 0, tiled=True)  13.4 us
    pallas_call x10, Pallas kernels, call(): pl.pallas_call(kernel, out_shape=[jax.ShapeDtypeStruct(shape, kind) for s...  10.7 us
    all_to_all x1, starting transfers between devices, swap(): lax.all_to_all(value, AXES, 0, 0, axis_index_groups=members, tiled=True)  5.7 us
    ppermute x4, waiting for transfers between devices, send_on(): lax.ppermute(value, AXES, [(i, j) for i, j in way if 0 <= j < devices])  2.94 us
  transfers between devices with their start and end apart: 5, of which 4 were waited for; matrix products, arithmetic and copies ran while one was open for 1% of the time, Pallas kernels for 3%

profile of v6, /device:TPU:1, one launch (start us, length us, event | category | flops | bytes accessed | tf_op | source)
XLA Modules:
  0.0 89.7 jit_solution(11391788540949267377)
XLA Ops:
  0.6 2.4 %shard_map.86 = (bf16[4,128,512]{2,1,0:T(8,128)(2,1)}, bf16[4,16,512]{2,1,0:T(8,128)(2,1)}, bf16[8,16,512]{2,1,0:T(8,128)(2,1)}) custom-call(s32[1]{0:T(128)} %bitcast.me_ref, s32[2,26]{1,0:T(2,128)} %nb_hbm.1, bf16[2,8,8,512]{3,2,1,0:T(8,128)(2,1)} %x_ref.1, bf16[2,8,8,512]{3,2,1,0:T(8,128)(2,1)} %g_hbm.1, s32[2,8,64]{2,1,0:T(8,128)} %occ_hbm.1), custom_call_target="tpu_custom_call" | custom-call | bytes 524288 | tf_op jit(solution)/shard_map/pallas_call | solution.py:459
  3.0 12.9 %all_to_all.25.near_ref = bf16[4,128,512]{2,1,0:T(8,128)(2,1)S(1)} all-to-all(bf16[4,128,512]{2,1,0:T(8,128)(2,1)} %get-tuple-element.23), channel_id=1, replica_groups={{0,1,2,3},{4,5,6,7},{8,9,10,11},{12,13,14,15},{16,17,18,19},{20,21,22,2..., dimensions={0} | all-to-all | bytes 1048576 | tf_op jit(solution)/shard_map/all_to_all | solution.py:489
  15.9 4.4 %collective-permute-start = (bf16[4,64,512]{2,1,0:T(8,128)(2,1)S(1)}, bf16[4,64,512]{2,1,0:T(8,128)(2,1)S(1)}, u32[]{:S(2)}, u32[]{:S(2)}) collective-permute-start(bf16[4,64,512]{2,1,0:T(8,128)(2,1)S(1)} %get-tuple-element.24), channel_id=1, source_target_pairs={{0,4},{1,5},{4,8},{5,9},{6,2},{7,3},{8,12},{9,13},{10,6},{11,7},{1... | collective-permute-start | bytes 786440 | tf_op jit(solution)/shard_map/ppermute | solution.py:503
  20.3 0.0 copy-start.6
  20.3 7.7 %collective-permute-start.1 = (bf16[2,64,512]{2,1,0:T(8,128)(2,1)S(1)}, bf16[2,64,512]{2,1,0:T(8,128)(2,1)S(1)}, u32[]{:S(2)}, u32[]{:S(2)}) collective-permute-start(bf16[2,64,512]{2,1,0:T(8,128)(2,1)S(1)} %get-tuple-element.25), channel_id=1, source_target_pairs={{2,6},{3,7},{4,0},{5,1},{6,10},{7,11},{8,4},{9,5},{10,14},{11,15},... | collective-permute-start | bytes 393224 | tf_op jit(solution)/shard_map/ppermute | solution.py:503
  28.1 0.0 copy-done.5
  28.1 0.3 copy.9.first_ref
  28.4 0.0 copy-done.6
  28.4 0.0 copy-start.1
  28.4 0.0 copy-start.2
  28.4 0.3 copy.10.second_ref
  28.6 0.4 copy-done.1
  29.1 0.0 copy-done.2
  29.1 0.4 shard_map.85
  29.5 0.5 collective-permute-done.1.shorter_ref
  30.0 0.8 collective-permute-done.longer_ref
  30.8 0.0 copy-done
  30.8 0.0 copy-done.3
  30.8 3.4 %shard_map.88 = (bf16[8,16,512]{2,1,0:T(8,128)(2,1)S(1)}, bf16[4,176,512]{2,1,0:T(8,128)(2,1)S(1)}, f32[4,8,512]{2,1,0:T(8,128)S(1)}) custom-call(s32[1]{0:T(128)} %bitcast.me_ref, s32[2,26]{1,0:T(2,128)S(1)} %get-tuple-element.20.nb_ref, bf16[2,8,8,512]{3,2,1,0:T(8,128)(2,1)S(1)} %copy-done, bf16[8,16,512]{2,1,0:T(8,128)(2,1)S(1)} %copy-done.3, ...), custom_call_target="tpu_custom_call" | custom-call | flops 1073741824 | bytes 524288 | tf_op jit(solution)/shard_map/pallas_call | solution.py:459
  34.2 13.4 %all_to_all.26.near_ref.parts_ref = bf16[4,176,512]{2,1,0:T(8,128)(2,1)S(1)} all-to-all(bf16[4,176,512]{2,1,0:T(8,128)(2,1)S(1)} %get-tuple-element.30), channel_id=1, replica_groups={{0,1,2,3},{4,5,6,7},{8,9,10,11},{12,13,14,15},{16,17,18,19},{20,21,22,2..., dimensions={0} | all-to-all | bytes 1441792 | tf_op jit(solution)/shard_map/all_to_all | solution.py:489
  47.6 0.1 shard_map.91
  47.6 13.4 %all_to_all.27.parts_ref = bf16[8,7,8,128]{3,2,1,0:T(8,128)(2,1)S(1)} all-to-all(bf16[8,7,8,128]{3,2,1,0:T(8,128)(2,1)S(1)} %shard_map.91), channel_id=1, replica_groups=mesh['grp'=8,'dev'=32] {'grp'}, dimensions={0} | all-to-all | bytes 229376 | tf_op jit(solution)/shard_map/all_to_all | solution.py:562
  61.1 10.0 %all_to_all.28.parts_ref = bf16[8,7,8,128]{3,2,1,0:T(8,128)(2,1)S(1)} all-to-all(bf16[8,7,8,128]{3,2,1,0:T(8,128)(2,1)S(1)} %shard_map.92), channel_id=1, replica_groups={{0,4,8,12,16,20,24,28},{1,5,9,13,17,21,25,29},{2,6,10,14,18,22,26,30},{..., dimensions={0} | all-to-all | bytes 229376 | tf_op jit(solution)/shard_map/all_to_all | solution.py:489
  71.1 0.8 shard_map.93
  71.9 5.7 %all-to-all-start.4 = ((bf16[32,7,8,128]{3,2,1,0:T(8,128)(2,1)}), bf16[32,7,8,128]{3,2,1,0:T(8,128)(2,1)S(1)}, u32[]{:S(2)}, u32[]{:S(2)}) async-start(bf16[32,7,8,128]{3,2,1,0:T(8,128)(2,1)} %shard_map.93), calls=%async_computation.4 | async-start | bytes 917504 | tf_op jit(solution)/shard_map/all_to_all | solution.py:489
  77.7 2.2 %collective-permute-start.2 = (bf16[4,32,512]{2,1,0:T(8,128)(2,1)S(1)}, bf16[4,32,512]{2,1,0:T(8,128)(2,1)S(1)}, u32[]{:S(2)}, u32[]{:S(2)}) collective-permute-start(bf16[4,32,512]{2,1,0:T(8,128)(2,1)S(1)} %get-tuple-element.31), channel_id=1, source_target_pairs={{0,4},{1,5},{4,8},{5,9},{6,2},{7,3},{8,12},{9,13},{10,6},{11,7},{1... | collective-permute-start | bytes 393224 | tf_op jit(solution)/shard_map/ppermute | solution.py:503
  79.9 4.6 %collective-permute-start.3 = (bf16[2,32,512]{2,1,0:T(8,128)(2,1)S(1)}, bf16[2,32,512]{2,1,0:T(8,128)(2,1)S(1)}, u32[]{:S(2)}, u32[]{:S(2)}) collective-permute-start(bf16[2,32,512]{2,1,0:T(8,128)(2,1)S(1)} %get-tuple-element.32), channel_id=1, source_target_pairs={{2,6},{3,7},{4,0},{5,1},{6,10},{7,11},{8,4},{9,5},{10,14},{11,15},... | collective-permute-start | bytes 196616 | tf_op jit(solution)/shard_map/ppermute | solution.py:503
  84.4 1.3 %collective-permute-done.3.shorter_ref = bf16[2,32,512]{2,1,0:T(8,128)(2,1)S(1)} collective-permute-done((bf16[2,32,512]{2,1,0:T(8,128)(2,1)S(1)}, bf16[2,32,512]{2,1,0:T(8,128)(2,1)S(1)}, u32[]{:S(2)}, u32[]{:S(2)}) %collective-permute-start.3) | collective-permute-done | bytes 65568 | tf_op jit(solution)/shard_map/ppermute | solution.py:503
  85.8 0.3 collective-permute-done.2.longer_ref
  86.1 2.4 %shard_map.90 = bf16[2,8,8,512]{3,2,1,0:T(8,128)(2,1)} custom-call(s32[1]{0:T(128)} %bitcast.me_ref, s32[2,26]{1,0:T(2,128)S(1)} %get-tuple-element.20.nb_ref, bf16[8,16,512]{2,1,0:T(8,128)(2,1)S(1)} %get-tuple-element.29.grads_ref, f32[128,512]{1,0:T(8,128)S(1)} %get-tuple-element.22.occupied_ref, bf16[4,176,512]{2,1,0:T(8,128)(2,1)S(1)} %all_to_all.26.near_ref.parts_ref, ...), custom_call_target="tpu_custom_call" | custom-call | flops 268435456 | bytes 524288 | tf_op jit(solution)/shard_map/pallas_call | solution.py:459
  88.4 0.0 all-to-all-done.4.parts_ref
  88.5 1.2 %shard_map.94 = (f32[64,1728]{1,0:T(8,128)}, f32[64,1728]{1,0:T(8,128)}) custom-call(bf16[32,7,8,128]{3,2,1,0:T(8,128)(2,1)S(1)} %all-to-all-done.4.parts_ref), custom_call_target="tpu_custom_call" | custom-call | bytes 524288 | tf_op jit(solution)/shard_map/pallas_call | solution.py:459
  (8 shorter events, 0.1 us)
Async XLA Ops:
  15.9 12.2 %copy-start.5 = (bf16[1728,64]{0,1:T(8,128)(2,1)S(1)}, bf16[1728,64]{0,1:T(8,128)(2,1)}, u32[]{:S(2)}) copy-start(bf16[1728,64]{0,1:T(8,128)(2,1)} %param.9) | copy-start | bytes 663556
  15.9 14.9 %collective-permute-start = (bf16[4,64,512]{2,1,0:T(8,128)(2,1)S(1)}, bf16[4,64,512]{2,1,0:T(8,128)(2,1)S(1)}, u32[]{:S(2)}, u32[]{:S(2)}) collective-permute-start(bf16[4,64,512]{2,1,0:T(8,128)(2,1)S(1)} %get-tuple-element.24), channel_id=1, source_target_pairs={{0,4},{1,5},{4,8},{5,9},{6,2},{7,3},{8,12},{9,13},{10,6},{11,7},{1... | collective-permute-start | bytes 786440 | tf_op jit(solution)/shard_map/ppermute | solution.py:503
  20.3 8.0 %copy-start.6 = (bf16[1728,64]{0,1:T(8,128)(2,1)S(1)}, bf16[1728,64]{0,1:T(8,128)(2,1)}, u32[]{:S(2)}) copy-start(bf16[1728,64]{0,1:T(8,128)(2,1)} %param.10) | copy-start | bytes 663556
  20.3 9.7 %collective-permute-start.1 = (bf16[2,64,512]{2,1,0:T(8,128)(2,1)S(1)}, bf16[2,64,512]{2,1,0:T(8,128)(2,1)S(1)}, u32[]{:S(2)}, u32[]{:S(2)}) collective-permute-start(bf16[2,64,512]{2,1,0:T(8,128)(2,1)S(1)} %get-tuple-element.25), channel_id=1, source_target_pairs={{2,6},{3,7},{4,0},{5,1},{6,10},{7,11},{8,4},{9,5},{10,14},{11,15},... | collective-permute-start | bytes 393224 | tf_op jit(solution)/shard_map/ppermute | solution.py:503
  28.4 0.7 copy-start.1
  28.4 0.7 copy-start.2
  29.1 1.7 %copy-start = (bf16[2,8,8,512]{3,2,1,0:T(8,128)(2,1)S(1)}, bf16[2,8,8,512]{3,2,1,0:T(8,128)(2,1)}, u32[]{:S(2)}) copy-start(bf16[2,8,8,512]{3,2,1,0:T(8,128)(2,1)} %x_ref.1) | copy-start | bytes 393220
  29.1 1.7 %copy-start.3 = (bf16[8,16,512]{2,1,0:T(8,128)(2,1)S(1)}, bf16[8,16,512]{2,1,0:T(8,128)(2,1)}, u32[]{:S(2)}) copy-start(bf16[8,16,512]{2,1,0:T(8,128)(2,1)} %get-tuple-element.21.masked_ref) | copy-start | bytes 393220
  29.1 1.7 %copy-start.4 = (bf16[4,16,512]{2,1,0:T(8,128)(2,1)S(1)}, bf16[4,16,512]{2,1,0:T(8,128)(2,1)}, u32[]{:S(2)}) copy-start(bf16[4,16,512]{2,1,0:T(8,128)(2,1)} %get-tuple-element.26.kept_in) | copy-start | bytes 196612
  71.9 16.5 %all-to-all-start.4 = ((bf16[32,7,8,128]{3,2,1,0:T(8,128)(2,1)}), bf16[32,7,8,128]{3,2,1,0:T(8,128)(2,1)S(1)}, u32[]{:S(2)}, u32[]{:S(2)}) async-start(bf16[32,7,8,128]{3,2,1,0:T(8,128)(2,1)} %shard_map.93), calls=%async_computation.4 | async-start | bytes 917504 | tf_op jit(solution)/shard_map/all_to_all | solution.py:489
  77.7 8.4 %collective-permute-start.2 = (bf16[4,32,512]{2,1,0:T(8,128)(2,1)S(1)}, bf16[4,32,512]{2,1,0:T(8,128)(2,1)S(1)}, u32[]{:S(2)}, u32[]{:S(2)}) collective-permute-start(bf16[4,32,512]{2,1,0:T(8,128)(2,1)S(1)} %get-tuple-element.31), channel_id=1, source_target_pairs={{0,4},{1,5},{4,8},{5,9},{6,2},{7,3},{8,12},{9,13},{10,6},{11,7},{1... | collective-permute-start | bytes 393224 | tf_op jit(solution)/shard_map/ppermute | solution.py:503
  79.9 5.9 %collective-permute-start.3 = (bf16[2,32,512]{2,1,0:T(8,128)(2,1)S(1)}, bf16[2,32,512]{2,1,0:T(8,128)(2,1)S(1)}, u32[]{:S(2)}, u32[]{:S(2)}) collective-permute-start(bf16[2,32,512]{2,1,0:T(8,128)(2,1)S(1)} %get-tuple-element.32), channel_id=1, source_target_pairs={{2,6},{3,7},{4,0},{5,1},{6,10},{7,11},{8,4},{9,5},{10,14},{11,15},... | collective-permute-start | bytes 196616 | tf_op jit(solution)/shard_map/ppermute | solution.py:503

commit v7 on v6

--- a/solution.py
+++ b/solution.py
@@ -198,19 +198,32 @@
                 [first[start : start + EDGE, :], second[start : start + EDGE, :]], axis=0
             ).astype(BF16)
     for pair in range(4):
+        for along_y in range(3):
+            windows[pair * 160 : (pair + 1) * 160, along_y * 256 : along_y * 256 + 256] = shifted[
+                along_y, :, :, pair * 128 : pair * 128 + 256
+            ].reshape(160, 256)
+
+
+def add_shifted(product):
+    pairs = []
+    for pair in range(4):
+        total = None
         for along_x in range(3):
-            for along_y in range(3):
-                place = (3 * along_x + along_y) * 256
-                windows[pair * 128 : (pair + 1) * 128, place : place + 256] = shifted[
-                    along_y, along_x : along_x + EDGE, :, pair * 128 : pair * 128 + 256
-                ].reshape(128, 256)
+            at = pair * 160 + along_x * 16
+            part = product[at : at + 128, along_x * 128 : along_x * 128 + 128]
+            total = part if total is None else total + part
+        pairs.append(total)
+    return jnp.concatenate(pairs, axis=0)
 
 
 def fill_direct(kernel_ref, direct):
     for group in range(9):
         block = kernel_ref[group * 192 : (group + 1) * 192, :]
         none = jnp.zeros((64, 64), BF16)
-        direct[group * 256 : (group + 1) * 256, :] = jnp.concatenate(
+        along_x, along_y = group // 3, group % 3
+        direct[
+            along_y * 256 : along_y * 256 + 256, along_x * 128 : along_x * 128 + 128
+        ] = jnp.concatenate(
             [
                 jnp.concatenate([block, none], axis=0),
                 jnp.concatenate([none, block], axis=0),
@@ -224,9 +237,10 @@
     for group in range(9):
         base = 3 * (8 - group)
         blocks = [kernel_ref[(base + z) * 64 : (base + z + 1) * 64, :] for z in (2, 1, 0)]
-        lanes = slice(group * 256, (group + 1) * 256)
-        flipped[0:64, lanes] = jnp.concatenate(blocks + [none], axis=1)
-        flipped[64:128, lanes] = jnp.concatenate([none] + blocks, axis=1)
+        row = group // 3 * 128
+        lanes = slice(group % 3 * 256, group % 3 * 256 + 256)
+        flipped[row : row + 64, lanes] = jnp.concatenate(blocks + [none], axis=1)
+        flipped[row + 64 : row + 128, lanes] = jnp.concatenate([none] + blocks, axis=1)
 
 
 def spread_kernel(
@@ -325,11 +339,11 @@
     for field in range(2):
         fill_windows(padded.at[field, 0], padded.at[field, 1], shifted.at[field], windows.at[field])
     occupied = paired(occupied_ref[...])
-    pre_act = jnp.dot(windows[0], direct[...], preferred_element_type=F32)
+    pre_act = add_shifted(jnp.dot(windows[0], direct[...], preferred_element_type=F32))
     logistic = 1.0 / (1.0 + jnp.exp(-pre_act))
     hidden = (pre_act * logistic * occupied).astype(BF16)
     slope = logistic * (1.0 + pre_act * (1.0 - logistic))
-    hidden_grad = times_flipped(windows[1], flipped[...])
+    hidden_grad = add_shifted(times_flipped(windows[1], flipped[...]))
     pre_grads = (hidden_grad * slope * occupied).astype(BF16)
 
     natural = unpaired(pre_grads.astype(F32))
@@ -350,7 +364,12 @@
 
     for half, own, field in ((0, hidden, 1), (1, pre_grads, 0)):
         turned = own.astype(F32).T.astype(BF16)
-        product[...] = jnp.dot(turned, windows[field], preferred_element_type=F32)
+        for along_x in range(3):
+            rows = [160 * pair + 16 * along_x for pair in range(4)]
+            moved = jnp.concatenate([windows[field, at : at + 128, :] for at in rows], axis=0)
+            product[:, along_x * 768 : along_x * 768 + 768] = jnp.dot(
+                turned, moved, preferred_element_type=F32
+            )
         packed = gather_blocks(product).astype(BF16)
         for chunk in range(2):
             start = 32 * chunk
@@ -386,7 +405,7 @@
         copies_ref[member] = total.astype(copies_ref.dtype)
 
 
-def input_grads_kernel(
+def last_kernel(
     me_ref,
     nb_ref,
     grads_ref,
@@ -396,41 +415,20 @@
     shorter_ref,
     kept_ref,
     flipped,
+    parts_ref,
+    out_hbm,
+    first_hbm,
+    second_hbm,
     out_ref,
+    first_out,
+    second_out,
+    halves,
     taken,
     padded,
     shifted,
     windows,
+    sems,
 ):
-    me = me_ref[0]
-    for member in range(4):
-        at = 4 * member
-        taken[at : at + 4] = near_ref[member, 0:32, :].astype(F32).reshape(4, EDGE, WIDE)
-        taken[at + 16 : at + 20] = longer_ref[member].astype(F32).reshape(4, EDGE, WIDE)
-    for number in range(2):
-        taken[32 + 4 * number : 36 + 4 * number] = (
-            shorter_ref[number].astype(F32).reshape(4, EDGE, WIDE)
-        )
-    taken[40:44] = kept_ref[...]
-    for brick in range(2):
-        values = {}
-        for number, offset in enumerate(DIRECTIONS):
-            present, place = take_place(nb_ref, me, brick, number)
-            values[offset] = jnp.where(present, taken[place], 0.0)
-
-        def own(x):
-            return grads_ref[x].astype(F32)[brick * EDGE : (brick + 1) * EDGE]
-
-        fill_padded(padded.at[brick], own, lambda offset: values[offset])
-    fill_windows(padded.at[0], padded.at[1], shifted, windows)
-    result = unpaired(times_flipped(windows[...], flipped[...])) * occupied_ref[...]
-    for x in range(EDGE):
-        for brick in range(2):
-            at = 16 * x + EDGE * brick
-            out_ref[brick, x] = result[at : at + EDGE].astype(BF16)
-
-
-def unpack_kernel(parts_ref, first_hbm, second_hbm, first_out, second_out, halves, sems):
     count = parts_ref.shape[1]
     for chunk in (2, 3, 0, 1):
         for tile in range(56):
@@ -448,8 +446,38 @@
     second_out[...] = jnp.concatenate(blocks[26::-1], axis=1)
     second_copy = pltpu.make_async_copy(second_out, second_hbm, sems.at[1])
     second_copy.start()
+
+    me = me_ref[0]
+    for member in range(4):
+        at = 4 * member
+        taken[at : at + 4] = near_ref[member, 0:32, :].astype(F32).reshape(4, EDGE, WIDE)
+        taken[at + 16 : at + 20] = longer_ref[member].astype(F32).reshape(4, EDGE, WIDE)
+    for number in range(2):
+        taken[32 + 4 * number : 36 + 4 * number] = (
+            shorter_ref[number].astype(F32).reshape(4, EDGE, WIDE)
+        )
+    taken[40:44] = kept_ref[...]
+    for brick in range(2):
+        values = {}
+        for number, offset in enumerate(DIRECTIONS):
+            present, place = take_place(nb_ref, me, brick, number)
+            values[offset] = jnp.where(present, taken[place], 0.0)
+
+        def own(x):
+            return grads_ref[x].astype(F32)[brick * EDGE : (brick + 1) * EDGE]
+
+        fill_padded(padded.at[brick], own, lambda offset: values[offset])
+    fill_windows(padded.at[0], padded.at[1], shifted, windows)
+    result = unpaired(add_shifted(times_flipped(windows[...], flipped[...]))) * occupied_ref[...]
+    for x in range(EDGE):
+        for brick in range(2):
+            at = 16 * x + EDGE * brick
+            out_ref[brick, x] = result[at : at + EDGE].astype(BF16)
+    out_copy = pltpu.make_async_copy(out_ref, out_hbm, sems.at[2])
+    out_copy.start()
     first_copy.wait()
     second_copy.wait()
+    out_copy.wait()
 
 
 def call(kernel, shapes, scratch, arguments, scalars=0, outside=0, leaving=False, megabytes=40, flops=0):
@@ -530,9 +558,9 @@
     direct, flipped, first_flipped, occupied, near_nb = call(
         spread_kernel,
         [
-            ((2304, 128), BF16),
-            ((128, 2304), BF16),
-            ((128, 2304), BF16),
+            ((768, 384), BF16),
+            ((384, 768), BF16),
+            ((384, 768), BF16),
             ((128, WIDE), F32),
             ((2, 26), jnp.int32),
         ],
@@ -546,7 +574,7 @@
             vmem((44, 16, WIDE), BF16),
             vmem((2, 2, 10 * ROWS, PADDED), F32),
             vmem((2, 3, 10, 16, PADDED), BF16),
-            vmem((2, 512, 2304), BF16),
+            vmem((2, 640, 768), BF16),
             vmem((128, 2304), F32),
             vmem((2, 64, WIDE), F32),
             vmem((36, EDGE, WIDE), F32),
@@ -566,30 +594,35 @@
         functools.partial(next_sum_kernel, scaling), [((4 * along_grp,) + piece, BF16)], [], [sums]
     )
     sums = swap(sums, planes)
-    (input_grads,) = call(
-        input_grads_kernel,
-        [((2, EDGE, EDGE, WIDE), BF16)],
+    input_grads, first_grads, second_grads = call(
+        last_kernel,
+        [((2, EDGE, EDGE, WIDE), BF16), ((64, 27 * 64), F32), ((64, 27 * 64), F32)],
         [
+            vmem((2, EDGE, EDGE, WIDE), BF16),
+            vmem((64, 27 * 64), F32),
+            vmem((64, 27 * 64), F32),
+            vmem((128, PACKED), F32),
             vmem((44, EDGE, WIDE), F32),
             vmem((2, 10 * ROWS, PADDED), F32),
             vmem((3, 10, 16, PADDED), BF16),
-            vmem((512, 2304), BF16),
+            vmem((640, 768), BF16),
+            pltpu.SemaphoreType.DMA((3,)),
         ],
-        [me, near_nb, pre_grads, occupied, near, longer, shorter, kept, first_flipped],
+        [
+            me,
+            near_nb,
+            pre_grads,
+            occupied,
+            near,
+            longer,
+            shorter,
+            kept,
+            first_flipped,
+            sums,
+        ],
         scalars=2,
+        leaving=True,
         flops=2**28,
-    )
-    first_grads, second_grads = call(
-        unpack_kernel,
-        [((64, 27 * 64), F32), ((64, 27 * 64), F32)],
-        [
-            vmem((64, 27 * 64), F32),
-            vmem((64, 27 * 64), F32),
-            vmem((128, PACKED), F32),
-            pltpu.SemaphoreType.DMA((2,)),
-        ],
-        [sums],
-        leaving=True,
     )
     return input_grads, first_grads.T, second_grads.T
 

time: 90.7 us -> 91.3 us (level)
  waiting for transfers between devices: 2.94 us -> 5.07 us
  Pallas kernels: 10.7 us -> 9.62 us
    all_to_all x1, waiting for transfers between devices: 0.01 us -> 2.14 us  [swap(): lax.all_to_all(value, AXES, 0, 0, axis_index_groups=members, tiled=True)]
    pallas_call x10 -> x9, Pallas kernels: 10.7 us -> 9.62 us  [call(): pl.pallas_call(kernel, out_shape=[jax.ShapeDtypeStruct(shape, kind) for s...]
  transfers between devices with their start and end apart: 5 -> 5, of which waited for: 4 -> 5; matrix products, arithmetic and copies ran while one was open for 1% -> 1% of each run, Pallas kernels for 3% -> 1%
where the time goes in v7:
time: 91.3 us; the launch traced here: 90.7 us
  blocking collectives  49.7 us (54%)
  starting transfers between devices  24.6 us (27%)
  Pallas kernels  9.62 us (11%)
  waiting for transfers between devices  5.07 us (6%)
  local copies, waits for them, and re-layouts  0.98 us (1%)
    all_to_all x3, blocking collectives, swap(): lax.all_to_all(value, AXES, 0, 0, axis_index_groups=members, tiled=True)  36.2 us
    ppermute x4, starting transfers between devices, send_on(): lax.ppermute(value, AXES, [(i, j) for i, j in way if 0 <= j < devices])  18.9 us
    all_to_all x1, blocking collectives, per_device(): sums = lax.all_to_all(sums, 'grp', 0, 0, tiled=True)  13.4 us
    pallas_call x9, Pallas kernels, call(): pl.pallas_call(kernel, out_shape=[jax.ShapeDtypeStruct(shape, kind) for s...  9.62 us
    all_to_all x1, starting transfers between devices, swap(): lax.all_to_all(value, AXES, 0, 0, axis_index_groups=members, tiled=True)  5.7 us
    ppermute x4, waiting for transfers between devices, send_on(): lax.ppermute(value, AXES, [(i, j) for i, j in way if 0 <= j < devices])  2.94 us
    all_to_all x1, waiting for transfers between devices, swap(): lax.all_to_all(value, AXES, 0, 0, axis_index_groups=members, tiled=True)  2.14 us
  transfers between devices with their start and end apart: 5, of which 5 were waited for; matrix products, arithmetic and copies ran while one was open for 1% of the time, Pallas kernels for 1%

profile of v7, /device:TPU:1, one launch (start us, length us, event | category | flops | bytes accessed | tf_op | source)
XLA Modules:
  0.0 90.7 jit_solution(5673155096031879809)
XLA Ops:
  0.6 2.4 %shard_map.86 = (bf16[4,128,512]{2,1,0:T(8,128)(2,1)}, bf16[4,16,512]{2,1,0:T(8,128)(2,1)}, bf16[8,16,512]{2,1,0:T(8,128)(2,1)}) custom-call(s32[1]{0:T(128)} %bitcast.me_ref, s32[2,26]{1,0:T(2,128)} %nb_hbm.1, bf16[2,8,8,512]{3,2,1,0:T(8,128)(2,1)} %x_ref.1, bf16[2,8,8,512]{3,2,1,0:T(8,128)(2,1)} %g_hbm.1, s32[2,8,64]{2,1,0:T(8,128)} %occ_hbm.1), custom_call_target="tpu_custom_call" | custom-call | bytes 524288 | tf_op jit(solution)/shard_map/pallas_call | solution.py:487
  3.0 12.9 %all_to_all.25.near_ref = bf16[4,128,512]{2,1,0:T(8,128)(2,1)S(1)} all-to-all(bf16[4,128,512]{2,1,0:T(8,128)(2,1)} %get-tuple-element.24), channel_id=1, replica_groups={{0,1,2,3},{4,5,6,7},{8,9,10,11},{12,13,14,15},{16,17,18,19},{20,21,22,2..., dimensions={0} | all-to-all | bytes 1048576 | tf_op jit(solution)/shard_map/all_to_all | solution.py:517
  15.9 4.4 %collective-permute-start = (bf16[4,64,512]{2,1,0:T(8,128)(2,1)S(1)}, bf16[4,64,512]{2,1,0:T(8,128)(2,1)S(1)}, u32[]{:S(2)}, u32[]{:S(2)}) collective-permute-start(bf16[4,64,512]{2,1,0:T(8,128)(2,1)S(1)} %get-tuple-element.25), channel_id=1, source_target_pairs={{0,4},{1,5},{4,8},{5,9},{6,2},{7,3},{8,12},{9,13},{10,6},{11,7},{1... | collective-permute-start | bytes 786440 | tf_op jit(solution)/shard_map/ppermute | solution.py:531
  20.3 0.0 copy-start.6
  20.3 7.7 %collective-permute-start.1 = (bf16[2,64,512]{2,1,0:T(8,128)(2,1)S(1)}, bf16[2,64,512]{2,1,0:T(8,128)(2,1)S(1)}, u32[]{:S(2)}, u32[]{:S(2)}) collective-permute-start(bf16[2,64,512]{2,1,0:T(8,128)(2,1)S(1)} %get-tuple-element.26), channel_id=1, source_target_pairs={{2,6},{3,7},{4,0},{5,1},{6,10},{7,11},{8,4},{9,5},{10,14},{11,15},... | collective-permute-start | bytes 393224 | tf_op jit(solution)/shard_map/ppermute | solution.py:531
  28.1 0.0 copy-done.5
  28.1 0.3 copy.9.first_ref
  28.4 0.0 copy-done.6
  28.4 0.0 copy-start.1
  28.4 0.0 copy-start.2
  28.4 0.3 copy.10.second_ref
  28.6 0.4 copy-done.1
  29.1 0.0 copy-done.2
  29.1 0.4 shard_map.85
  29.5 0.5 collective-permute-done.1.shorter_ref
  30.0 0.8 collective-permute-done.longer_ref
  30.8 0.0 copy-done
  30.8 0.0 copy-done.3
  30.8 0.0 copy-done.4
  30.8 3.3 %shard_map.88 = (bf16[8,16,512]{2,1,0:T(8,128)(2,1)S(1)}, bf16[4,176,512]{2,1,0:T(8,128)(2,1)S(1)}, f32[4,8,512]{2,1,0:T(8,128)S(1)}) custom-call(s32[1]{0:T(128)} %bitcast.me_ref, s32[2,26]{1,0:T(2,128)S(1)} %get-tuple-element.21.nb_ref, bf16[2,8,8,512]{3,2,1,0:T(8,128)(2,1)S(1)} %copy-done, bf16[8,16,512]{2,1,0:T(8,128)(2,1)S(1)} %copy-done.3, ...), custom_call_target="tpu_custom_call" | custom-call | flops 1073741824 | bytes 524288 | tf_op jit(solution)/shard_map/pallas_call | solution.py:487
  34.1 13.4 %all_to_all.26.near_ref.parts_ref = bf16[4,176,512]{2,1,0:T(8,128)(2,1)S(1)} all-to-all(bf16[4,176,512]{2,1,0:T(8,128)(2,1)S(1)} %get-tuple-element.31), channel_id=1, replica_groups={{0,1,2,3},{4,5,6,7},{8,9,10,11},{12,13,14,15},{16,17,18,19},{20,21,22,2..., dimensions={0} | all-to-all | bytes 1441792 | tf_op jit(solution)/shard_map/all_to_all | solution.py:517
  47.5 0.1 shard_map.90
  47.5 13.4 %all_to_all.27.parts_ref = bf16[8,7,8,128]{3,2,1,0:T(8,128)(2,1)S(1)} all-to-all(bf16[8,7,8,128]{3,2,1,0:T(8,128)(2,1)S(1)} %shard_map.90), channel_id=1, replica_groups=mesh['grp'=8,'dev'=32] {'grp'}, dimensions={0} | all-to-all | bytes 229376 | tf_op jit(solution)/shard_map/all_to_all | solution.py:590
  61.0 10.0 %all_to_all.28.parts_ref = bf16[8,7,8,128]{3,2,1,0:T(8,128)(2,1)S(1)} all-to-all(bf16[8,7,8,128]{3,2,1,0:T(8,128)(2,1)S(1)} %shard_map.91), channel_id=1, replica_groups={{0,4,8,12,16,20,24,28},{1,5,9,13,17,21,25,29},{2,6,10,14,18,22,26,30},{..., dimensions={0} | all-to-all | bytes 229376 | tf_op jit(solution)/shard_map/all_to_all | solution.py:517
  71.0 0.8 shard_map.92
  71.8 5.7 %all-to-all-start.4 = ((bf16[32,7,8,128]{3,2,1,0:T(8,128)(2,1)}), bf16[32,7,8,128]{3,2,1,0:T(8,128)(2,1)S(1)}, u32[]{:S(2)}, u32[]{:S(2)}) async-start(bf16[32,7,8,128]{3,2,1,0:T(8,128)(2,1)} %shard_map.92), calls=%async_computation.4 | async-start | bytes 917504 | tf_op jit(solution)/shard_map/all_to_all | solution.py:517
  77.5 2.2 %collective-permute-start.2 = (bf16[4,32,512]{2,1,0:T(8,128)(2,1)S(1)}, bf16[4,32,512]{2,1,0:T(8,128)(2,1)S(1)}, u32[]{:S(2)}, u32[]{:S(2)}) collective-permute-start(bf16[4,32,512]{2,1,0:T(8,128)(2,1)S(1)} %get-tuple-element.32), channel_id=1, source_target_pairs={{0,4},{1,5},{4,8},{5,9},{6,2},{7,3},{8,12},{9,13},{10,6},{11,7},{1... | collective-permute-start | bytes 393224 | tf_op jit(solution)/shard_map/ppermute | solution.py:531
  79.7 4.6 %collective-permute-start.3 = (bf16[2,32,512]{2,1,0:T(8,128)(2,1)S(1)}, bf16[2,32,512]{2,1,0:T(8,128)(2,1)S(1)}, u32[]{:S(2)}, u32[]{:S(2)}) collective-permute-start(bf16[2,32,512]{2,1,0:T(8,128)(2,1)S(1)} %get-tuple-element.33), channel_id=1, source_target_pairs={{2,6},{3,7},{4,0},{5,1},{6,10},{7,11},{8,4},{9,5},{10,14},{11,15},... | collective-permute-start | bytes 196616 | tf_op jit(solution)/shard_map/ppermute | solution.py:531
  84.3 1.3 %collective-permute-done.3.shorter_ref = bf16[2,32,512]{2,1,0:T(8,128)(2,1)S(1)} collective-permute-done((bf16[2,32,512]{2,1,0:T(8,128)(2,1)S(1)}, bf16[2,32,512]{2,1,0:T(8,128)(2,1)S(1)}, u32[]{:S(2)}, u32[]{:S(2)}) %collective-permute-start.3) | collective-permute-done | bytes 65568 | tf_op jit(solution)/shard_map/ppermute | solution.py:531
  85.6 0.3 collective-permute-done.2.longer_ref
  86.0 2.1 %all-to-all-done.4.parts_ref = bf16[32,7,8,128]{3,2,1,0:T(8,128)(2,1)S(1)} async-done(((bf16[32,7,8,128]{3,2,1,0:T(8,128)(2,1)}), bf16[32,7,8,128]{3,2,1,0:T(8,128)(2,1)S(1)}, u32[]{:S(2)}, u32[]{:S(2)}) %all-to-all-start.4) | async-done | bytes 458784 | tf_op jit(solution)/shard_map/all_to_all | solution.py:517
  88.1 2.6 %shard_map.93 = (bf16[2,8,8,512]{3,2,1,0:T(8,128)(2,1)}, f32[64,1728]{1,0:T(8,128)}, f32[64,1728]{1,0:T(8,128)}) custom-call(s32[1]{0:T(128)} %bitcast.me_ref, s32[2,26]{1,0:T(2,128)S(1)} %get-tuple-element.21.nb_ref, bf16[8,16,512]{2,1,0:T(8,128)(2,1)S(1)} %get-tuple-element.30.grads_ref, f32[128,512]{1,0:T(8,128)S(1)} %get-tuple-element.23.occupied_ref, ...), custom_call_target="tpu_custom_call" | custom-call | flops 268435456 | bytes 524288 | tf_op jit(solution)/shard_map/pallas_call | solution.py:487
  (7 shorter events, 0.1 us)
Async XLA Ops:
  15.9 12.2 %copy-start.5 = (bf16[1728,64]{0,1:T(8,128)(2,1)S(1)}, bf16[1728,64]{0,1:T(8,128)(2,1)}, u32[]{:S(2)}) copy-start(bf16[1728,64]{0,1:T(8,128)(2,1)} %param.9) | copy-start | bytes 663556
  15.9 14.9 %collective-permute-start = (bf16[4,64,512]{2,1,0:T(8,128)(2,1)S(1)}, bf16[4,64,512]{2,1,0:T(8,128)(2,1)S(1)}, u32[]{:S(2)}, u32[]{:S(2)}) collective-permute-start(bf16[4,64,512]{2,1,0:T(8,128)(2,1)S(1)} %get-tuple-element.25), channel_id=1, source_target_pairs={{0,4},{1,5},{4,8},{5,9},{6,2},{7,3},{8,12},{9,13},{10,6},{11,7},{1... | collective-permute-start | bytes 786440 | tf_op jit(solution)/shard_map/ppermute | solution.py:531
  20.3 8.0 %copy-start.6 = (bf16[1728,64]{0,1:T(8,128)(2,1)S(1)}, bf16[1728,64]{0,1:T(8,128)(2,1)}, u32[]{:S(2)}) copy-start(bf16[1728,64]{0,1:T(8,128)(2,1)} %param.10) | copy-start | bytes 663556
  20.3 9.7 %collective-permute-start.1 = (bf16[2,64,512]{2,1,0:T(8,128)(2,1)S(1)}, bf16[2,64,512]{2,1,0:T(8,128)(2,1)S(1)}, u32[]{:S(2)}, u32[]{:S(2)}) collective-permute-start(bf16[2,64,512]{2,1,0:T(8,128)(2,1)S(1)} %get-tuple-element.26), channel_id=1, source_target_pairs={{2,6},{3,7},{4,0},{5,1},{6,10},{7,11},{8,4},{9,5},{10,14},{11,15},... | collective-permute-start | bytes 393224 | tf_op jit(solution)/shard_map/ppermute | solution.py:531
  28.4 0.7 copy-start.1
  28.4 0.7 copy-start.2
  29.1 1.7 %copy-start = (bf16[2,8,8,512]{3,2,1,0:T(8,128)(2,1)S(1)}, bf16[2,8,8,512]{3,2,1,0:T(8,128)(2,1)}, u32[]{:S(2)}) copy-start(bf16[2,8,8,512]{3,2,1,0:T(8,128)(2,1)} %x_ref.1) | copy-start | bytes 393220
  29.1 1.7 %copy-start.3 = (bf16[8,16,512]{2,1,0:T(8,128)(2,1)S(1)}, bf16[8,16,512]{2,1,0:T(8,128)(2,1)}, u32[]{:S(2)}) copy-start(bf16[8,16,512]{2,1,0:T(8,128)(2,1)} %get-tuple-element.22.masked_ref) | copy-start | bytes 393220
  29.1 1.7 %copy-start.4 = (bf16[4,16,512]{2,1,0:T(8,128)(2,1)S(1)}, bf16[4,16,512]{2,1,0:T(8,128)(2,1)}, u32[]{:S(2)}) copy-start(bf16[4,16,512]{2,1,0:T(8,128)(2,1)} %get-tuple-element.27.kept_in) | copy-start | bytes 196612
  71.8 16.3 %all-to-all-start.4 = ((bf16[32,7,8,128]{3,2,1,0:T(8,128)(2,1)}), bf16[32,7,8,128]{3,2,1,0:T(8,128)(2,1)S(1)}, u32[]{:S(2)}, u32[]{:S(2)}) async-start(bf16[32,7,8,128]{3,2,1,0:T(8,128)(2,1)} %shard_map.92), calls=%async_computation.4 | async-start | bytes 917504 | tf_op jit(solution)/shard_map/all_to_all | solution.py:517
  77.5 8.4 %collective-permute-start.2 = (bf16[4,32,512]{2,1,0:T(8,128)(2,1)S(1)}, bf16[4,32,512]{2,1,0:T(8,128)(2,1)S(1)}, u32[]{:S(2)}, u32[]{:S(2)}) collective-permute-start(bf16[4,32,512]{2,1,0:T(8,128)(2,1)S(1)} %get-tuple-element.32), channel_id=1, source_target_pairs={{0,4},{1,5},{4,8},{5,9},{6,2},{7,3},{8,12},{9,13},{10,6},{11,7},{1... | collective-permute-start | bytes 393224 | tf_op jit(solution)/shard_map/ppermute | solution.py:531
  79.7 5.9 %collective-permute-start.3 = (bf16[2,32,512]{2,1,0:T(8,128)(2,1)S(1)}, bf16[2,32,512]{2,1,0:T(8,128)(2,1)S(1)}, u32[]{:S(2)}, u32[]{:S(2)}) collective-permute-start(bf16[2,32,512]{2,1,0:T(8,128)(2,1)S(1)} %get-tuple-element.33), channel_id=1, source_target_pairs={{2,6},{3,7},{4,0},{5,1},{6,10},{7,11},{8,4},{9,5},{10,14},{11,15},... | collective-permute-start | bytes 196616 | tf_op jit(solution)/shard_map/ppermute | solution.py:531

commit v8 on v6

--- a/solution.py
+++ b/solution.py
@@ -198,19 +198,32 @@
                 [first[start : start + EDGE, :], second[start : start + EDGE, :]], axis=0
             ).astype(BF16)
     for pair in range(4):
+        for along_y in range(3):
+            windows[pair * 160 : (pair + 1) * 160, along_y * 256 : along_y * 256 + 256] = shifted[
+                along_y, :, :, pair * 128 : pair * 128 + 256
+            ].reshape(160, 256)
+
+
+def add_shifted(product):
+    pairs = []
+    for pair in range(4):
+        total = None
         for along_x in range(3):
-            for along_y in range(3):
-                place = (3 * along_x + along_y) * 256
-                windows[pair * 128 : (pair + 1) * 128, place : place + 256] = shifted[
-                    along_y, along_x : along_x + EDGE, :, pair * 128 : pair * 128 + 256
-                ].reshape(128, 256)
+            at = pair * 160 + along_x * 16
+            part = product[at : at + 128, along_x * 128 : along_x * 128 + 128]
+            total = part if total is None else total + part
+        pairs.append(total)
+    return jnp.concatenate(pairs, axis=0)
 
 
 def fill_direct(kernel_ref, direct):
     for group in range(9):
         block = kernel_ref[group * 192 : (group + 1) * 192, :]
         none = jnp.zeros((64, 64), BF16)
-        direct[group * 256 : (group + 1) * 256, :] = jnp.concatenate(
+        along_x, along_y = group // 3, group % 3
+        direct[
+            along_y * 256 : along_y * 256 + 256, along_x * 128 : along_x * 128 + 128
+        ] = jnp.concatenate(
             [
                 jnp.concatenate([block, none], axis=0),
                 jnp.concatenate([none, block], axis=0),
@@ -224,9 +237,10 @@
     for group in range(9):
         base = 3 * (8 - group)
         blocks = [kernel_ref[(base + z) * 64 : (base + z + 1) * 64, :] for z in (2, 1, 0)]
-        lanes = slice(group * 256, (group + 1) * 256)
-        flipped[0:64, lanes] = jnp.concatenate(blocks + [none], axis=1)
-        flipped[64:128, lanes] = jnp.concatenate([none] + blocks, axis=1)
+        row = group // 3 * 128
+        lanes = slice(group % 3 * 256, group % 3 * 256 + 256)
+        flipped[row : row + 64, lanes] = jnp.concatenate(blocks + [none], axis=1)
+        flipped[row + 64 : row + 128, lanes] = jnp.concatenate([none] + blocks, axis=1)
 
 
 def spread_kernel(
@@ -325,11 +339,11 @@
     for field in range(2):
         fill_windows(padded.at[field, 0], padded.at[field, 1], shifted.at[field], windows.at[field])
     occupied = paired(occupied_ref[...])
-    pre_act = jnp.dot(windows[0], direct[...], preferred_element_type=F32)
+    pre_act = add_shifted(jnp.dot(windows[0], direct[...], preferred_element_type=F32))
     logistic = 1.0 / (1.0 + jnp.exp(-pre_act))
     hidden = (pre_act * logistic * occupied).astype(BF16)
     slope = logistic * (1.0 + pre_act * (1.0 - logistic))
-    hidden_grad = times_flipped(windows[1], flipped[...])
+    hidden_grad = add_shifted(times_flipped(windows[1], flipped[...]))
     pre_grads = (hidden_grad * slope * occupied).astype(BF16)
 
     natural = unpaired(pre_grads.astype(F32))
@@ -350,7 +364,12 @@
 
     for half, own, field in ((0, hidden, 1), (1, pre_grads, 0)):
         turned = own.astype(F32).T.astype(BF16)
-        product[...] = jnp.dot(turned, windows[field], preferred_element_type=F32)
+        for along_x in range(3):
+            rows = [160 * pair + 16 * along_x for pair in range(4)]
+            moved = jnp.concatenate([windows[field, at : at + 128, :] for at in rows], axis=0)
+            product[:, along_x * 768 : along_x * 768 + 768] = jnp.dot(
+                turned, moved, preferred_element_type=F32
+            )
         packed = gather_blocks(product).astype(BF16)
         for chunk in range(2):
             start = 32 * chunk
@@ -423,7 +442,7 @@
 
         fill_padded(padded.at[brick], own, lambda offset: values[offset])
     fill_windows(padded.at[0], padded.at[1], shifted, windows)
-    result = unpaired(times_flipped(windows[...], flipped[...])) * occupied_ref[...]
+    result = unpaired(add_shifted(times_flipped(windows[...], flipped[...]))) * occupied_ref[...]
     for x in range(EDGE):
         for brick in range(2):
             at = 16 * x + EDGE * brick
@@ -530,9 +549,9 @@
     direct, flipped, first_flipped, occupied, near_nb = call(
         spread_kernel,
         [
-            ((2304, 128), BF16),
-            ((128, 2304), BF16),
-            ((128, 2304), BF16),
+            ((768, 384), BF16),
+            ((384, 768), BF16),
+            ((384, 768), BF16),
             ((128, WIDE), F32),
             ((2, 26), jnp.int32),
         ],
@@ -546,7 +565,7 @@
             vmem((44, 16, WIDE), BF16),
             vmem((2, 2, 10 * ROWS, PADDED), F32),
             vmem((2, 3, 10, 16, PADDED), BF16),
-            vmem((2, 512, 2304), BF16),
+            vmem((2, 640, 768), BF16),
             vmem((128, 2304), F32),
             vmem((2, 64, WIDE), F32),
             vmem((36, EDGE, WIDE), F32),
@@ -573,7 +592,7 @@
             vmem((44, EDGE, WIDE), F32),
             vmem((2, 10 * ROWS, PADDED), F32),
             vmem((3, 10, 16, PADDED), BF16),
-            vmem((512, 2304), BF16),
+            vmem((640, 768), BF16),
         ],
         [me, near_nb, pre_grads, occupied, near, longer, shorter, kept, first_flipped],
         scalars=2,

time: 90.7 us -> 90.6 us (level)
  no operation moved by 1% of the time
where the time goes in v8:
time: 90.6 us; the launch traced here: 89.5 us
  blocking collectives  49.7 us (55%)
  starting transfers between devices  24.6 us (27%)
  Pallas kernels  10.6 us (12%)
  waiting for transfers between devices  2.94 us (3%)
  local copies, waits for them, and re-layouts  0.98 us (1%)
    all_to_all x3, blocking collectives, swap(): lax.all_to_all(value, AXES, 0, 0, axis_index_groups=members, tiled=True)  36.2 us
    ppermute x4, starting transfers between devices, send_on(): lax.ppermute(value, AXES, [(i, j) for i, j in way if 0 <= j < devices])  18.9 us
    all_to_all x1, blocking collectives, per_device(): sums = lax.all_to_all(sums, 'grp', 0, 0, tiled=True)  13.4 us
    pallas_call x10, Pallas kernels, call(): pl.pallas_call(kernel, out_shape=[jax.ShapeDtypeStruct(shape, kind) for s...  10.6 us
    all_to_all x1, starting transfers between devices, swap(): lax.all_to_all(value, AXES, 0, 0, axis_index_groups=members, tiled=True)  5.7 us
    ppermute x4, waiting for transfers between devices, send_on(): lax.ppermute(value, AXES, [(i, j) for i, j in way if 0 <= j < devices])  2.94 us
  transfers between devices with their start and end apart: 5, of which 4 were waited for; matrix products, arithmetic and copies ran while one was open for 1% of the time, Pallas kernels for 3%

profile of v8, /device:TPU:1, one launch (start us, length us, event | category | flops | bytes accessed | tf_op | source)
XLA Modules:
  0.0 89.5 jit_solution(6181663917642703275)
XLA Ops:
  0.6 2.4 %shard_map.86 = (bf16[4,128,512]{2,1,0:T(8,128)(2,1)}, bf16[4,16,512]{2,1,0:T(8,128)(2,1)}, bf16[8,16,512]{2,1,0:T(8,128)(2,1)}) custom-call(s32[1]{0:T(128)} %bitcast.me_ref, s32[2,26]{1,0:T(2,128)} %nb_hbm.1, bf16[2,8,8,512]{3,2,1,0:T(8,128)(2,1)} %x_ref.1, bf16[2,8,8,512]{3,2,1,0:T(8,128)(2,1)} %g_hbm.1, s32[2,8,64]{2,1,0:T(8,128)} %occ_hbm.1), custom_call_target="tpu_custom_call" | custom-call | bytes 524288 | tf_op jit(solution)/shard_map/pallas_call | solution.py:478
  3.0 12.9 %all_to_all.25.near_ref = bf16[4,128,512]{2,1,0:T(8,128)(2,1)S(1)} all-to-all(bf16[4,128,512]{2,1,0:T(8,128)(2,1)} %get-tuple-element.23), channel_id=1, replica_groups={{0,1,2,3},{4,5,6,7},{8,9,10,11},{12,13,14,15},{16,17,18,19},{20,21,22,2..., dimensions={0} | all-to-all | bytes 1048576 | tf_op jit(solution)/shard_map/all_to_all | solution.py:508
  15.9 4.4 %collective-permute-start = (bf16[4,64,512]{2,1,0:T(8,128)(2,1)S(1)}, bf16[4,64,512]{2,1,0:T(8,128)(2,1)S(1)}, u32[]{:S(2)}, u32[]{:S(2)}) collective-permute-start(bf16[4,64,512]{2,1,0:T(8,128)(2,1)S(1)} %get-tuple-element.24), channel_id=1, source_target_pairs={{0,4},{1,5},{4,8},{5,9},{6,2},{7,3},{8,12},{9,13},{10,6},{11,7},{1... | collective-permute-start | bytes 786440 | tf_op jit(solution)/shard_map/ppermute | solution.py:522
  20.3 0.0 copy-start.6
  20.3 7.7 %collective-permute-start.1 = (bf16[2,64,512]{2,1,0:T(8,128)(2,1)S(1)}, bf16[2,64,512]{2,1,0:T(8,128)(2,1)S(1)}, u32[]{:S(2)}, u32[]{:S(2)}) collective-permute-start(bf16[2,64,512]{2,1,0:T(8,128)(2,1)S(1)} %get-tuple-element.25), channel_id=1, source_target_pairs={{2,6},{3,7},{4,0},{5,1},{6,10},{7,11},{8,4},{9,5},{10,14},{11,15},... | collective-permute-start | bytes 393224 | tf_op jit(solution)/shard_map/ppermute | solution.py:522
  28.1 0.0 copy-done.5
  28.1 0.3 copy.9.first_ref
  28.4 0.0 copy-done.6
  28.4 0.0 copy-start.1
  28.4 0.0 copy-start.2
  28.4 0.3 copy.10.second_ref
  28.6 0.4 copy-done.1
  29.1 0.0 copy-done.2
  29.1 0.4 shard_map.85
  29.5 0.5 collective-permute-done.1.shorter_ref
  30.0 0.8 collective-permute-done.longer_ref
  30.8 0.0 copy-done
  30.8 0.0 copy-done.3
  30.8 3.3 %shard_map.88 = (bf16[8,16,512]{2,1,0:T(8,128)(2,1)S(1)}, bf16[4,176,512]{2,1,0:T(8,128)(2,1)S(1)}, f32[4,8,512]{2,1,0:T(8,128)S(1)}) custom-call(s32[1]{0:T(128)} %bitcast.me_ref, s32[2,26]{1,0:T(2,128)S(1)} %get-tuple-element.20.nb_ref, bf16[2,8,8,512]{3,2,1,0:T(8,128)(2,1)S(1)} %copy-done, bf16[8,16,512]{2,1,0:T(8,128)(2,1)S(1)} %copy-done.3, ...), custom_call_target="tpu_custom_call" | custom-call | flops 1073741824 | bytes 524288 | tf_op jit(solution)/shard_map/pallas_call | solution.py:478
  34.1 13.4 %all_to_all.26.near_ref.parts_ref = bf16[4,176,512]{2,1,0:T(8,128)(2,1)S(1)} all-to-all(bf16[4,176,512]{2,1,0:T(8,128)(2,1)S(1)} %get-tuple-element.30), channel_id=1, replica_groups={{0,1,2,3},{4,5,6,7},{8,9,10,11},{12,13,14,15},{16,17,18,19},{20,21,22,2..., dimensions={0} | all-to-all | bytes 1441792 | tf_op jit(solution)/shard_map/all_to_all | solution.py:508
  47.5 0.1 shard_map.91
  47.5 13.4 %all_to_all.27.parts_ref = bf16[8,7,8,128]{3,2,1,0:T(8,128)(2,1)S(1)} all-to-all(bf16[8,7,8,128]{3,2,1,0:T(8,128)(2,1)S(1)} %shard_map.91), channel_id=1, replica_groups=mesh['grp'=8,'dev'=32] {'grp'}, dimensions={0} | all-to-all | bytes 229376 | tf_op jit(solution)/shard_map/all_to_all | solution.py:581
  61.0 10.0 %all_to_all.28.parts_ref = bf16[8,7,8,128]{3,2,1,0:T(8,128)(2,1)S(1)} all-to-all(bf16[8,7,8,128]{3,2,1,0:T(8,128)(2,1)S(1)} %shard_map.92), channel_id=1, replica_groups={{0,4,8,12,16,20,24,28},{1,5,9,13,17,21,25,29},{2,6,10,14,18,22,26,30},{..., dimensions={0} | all-to-all | bytes 229376 | tf_op jit(solution)/shard_map/all_to_all | solution.py:508
  71.0 0.8 shard_map.93
  71.8 5.7 %all-to-all-start.4 = ((bf16[32,7,8,128]{3,2,1,0:T(8,128)(2,1)}), bf16[32,7,8,128]{3,2,1,0:T(8,128)(2,1)S(1)}, u32[]{:S(2)}, u32[]{:S(2)}) async-start(bf16[32,7,8,128]{3,2,1,0:T(8,128)(2,1)} %shard_map.93), calls=%async_computation.4 | async-start | bytes 917504 | tf_op jit(solution)/shard_map/all_to_all | solution.py:508
  77.5 2.2 %collective-permute-start.2 = (bf16[4,32,512]{2,1,0:T(8,128)(2,1)S(1)}, bf16[4,32,512]{2,1,0:T(8,128)(2,1)S(1)}, u32[]{:S(2)}, u32[]{:S(2)}) collective-permute-start(bf16[4,32,512]{2,1,0:T(8,128)(2,1)S(1)} %get-tuple-element.31), channel_id=1, source_target_pairs={{0,4},{1,5},{4,8},{5,9},{6,2},{7,3},{8,12},{9,13},{10,6},{11,7},{1... | collective-permute-start | bytes 393224 | tf_op jit(solution)/shard_map/ppermute | solution.py:522
  79.8 4.6 %collective-permute-start.3 = (bf16[2,32,512]{2,1,0:T(8,128)(2,1)S(1)}, bf16[2,32,512]{2,1,0:T(8,128)(2,1)S(1)}, u32[]{:S(2)}, u32[]{:S(2)}) collective-permute-start(bf16[2,32,512]{2,1,0:T(8,128)(2,1)S(1)} %get-tuple-element.32), channel_id=1, source_target_pairs={{2,6},{3,7},{4,0},{5,1},{6,10},{7,11},{8,4},{9,5},{10,14},{11,15},... | collective-permute-start | bytes 196616 | tf_op jit(solution)/shard_map/ppermute | solution.py:522
  84.3 1.3 %collective-permute-done.3.shorter_ref = bf16[2,32,512]{2,1,0:T(8,128)(2,1)S(1)} collective-permute-done((bf16[2,32,512]{2,1,0:T(8,128)(2,1)S(1)}, bf16[2,32,512]{2,1,0:T(8,128)(2,1)S(1)}, u32[]{:S(2)}, u32[]{:S(2)}) %collective-permute-start.3) | collective-permute-done | bytes 65568 | tf_op jit(solution)/shard_map/ppermute | solution.py:522
  85.6 0.3 collective-permute-done.2.longer_ref
  86.0 2.3 %shard_map.90 = bf16[2,8,8,512]{3,2,1,0:T(8,128)(2,1)} custom-call(s32[1]{0:T(128)} %bitcast.me_ref, s32[2,26]{1,0:T(2,128)S(1)} %get-tuple-element.20.nb_ref, bf16[8,16,512]{2,1,0:T(8,128)(2,1)S(1)} %get-tuple-element.29.grads_ref, f32[128,512]{1,0:T(8,128)S(1)} %get-tuple-element.22.occupied_ref, bf16[4,176,512]{2,1,0:T(8,128)(2,1)S(1)} %all_to_all.26.near_ref.parts_ref, ...), custom_call_target="tpu_custom_call" | custom-call | flops 268435456 | bytes 524288 | tf_op jit(solution)/shard_map/pallas_call | solution.py:478
  88.3 0.0 all-to-all-done.4.parts_ref
  88.3 1.2 %shard_map.94 = (f32[64,1728]{1,0:T(8,128)}, f32[64,1728]{1,0:T(8,128)}) custom-call(bf16[32,7,8,128]{3,2,1,0:T(8,128)(2,1)S(1)} %all-to-all-done.4.parts_ref), custom_call_target="tpu_custom_call" | custom-call | bytes 524288 | tf_op jit(solution)/shard_map/pallas_call | solution.py:478
  (8 shorter events, 0.1 us)
Async XLA Ops:
  15.9 12.2 %copy-start.5 = (bf16[1728,64]{0,1:T(8,128)(2,1)S(1)}, bf16[1728,64]{0,1:T(8,128)(2,1)}, u32[]{:S(2)}) copy-start(bf16[1728,64]{0,1:T(8,128)(2,1)} %param.9) | copy-start | bytes 663556
  15.9 14.9 %collective-permute-start = (bf16[4,64,512]{2,1,0:T(8,128)(2,1)S(1)}, bf16[4,64,512]{2,1,0:T(8,128)(2,1)S(1)}, u32[]{:S(2)}, u32[]{:S(2)}) collective-permute-start(bf16[4,64,512]{2,1,0:T(8,128)(2,1)S(1)} %get-tuple-element.24), channel_id=1, source_target_pairs={{0,4},{1,5},{4,8},{5,9},{6,2},{7,3},{8,12},{9,13},{10,6},{11,7},{1... | collective-permute-start | bytes 786440 | tf_op jit(solution)/shard_map/ppermute | solution.py:522
  20.3 8.0 %copy-start.6 = (bf16[1728,64]{0,1:T(8,128)(2,1)S(1)}, bf16[1728,64]{0,1:T(8,128)(2,1)}, u32[]{:S(2)}) copy-start(bf16[1728,64]{0,1:T(8,128)(2,1)} %param.10) | copy-start | bytes 663556
  20.3 9.7 %collective-permute-start.1 = (bf16[2,64,512]{2,1,0:T(8,128)(2,1)S(1)}, bf16[2,64,512]{2,1,0:T(8,128)(2,1)S(1)}, u32[]{:S(2)}, u32[]{:S(2)}) collective-permute-start(bf16[2,64,512]{2,1,0:T(8,128)(2,1)S(1)} %get-tuple-element.25), channel_id=1, source_target_pairs={{2,6},{3,7},{4,0},{5,1},{6,10},{7,11},{8,4},{9,5},{10,14},{11,15},... | collective-permute-start | bytes 393224 | tf_op jit(solution)/shard_map/ppermute | solution.py:522
  28.4 0.7 copy-start.1
  28.4 0.7 copy-start.2
  29.1 1.7 %copy-start = (bf16[2,8,8,512]{3,2,1,0:T(8,128)(2,1)S(1)}, bf16[2,8,8,512]{3,2,1,0:T(8,128)(2,1)}, u32[]{:S(2)}) copy-start(bf16[2,8,8,512]{3,2,1,0:T(8,128)(2,1)} %x_ref.1) | copy-start | bytes 393220
  29.1 1.7 %copy-start.3 = (bf16[8,16,512]{2,1,0:T(8,128)(2,1)S(1)}, bf16[8,16,512]{2,1,0:T(8,128)(2,1)}, u32[]{:S(2)}) copy-start(bf16[8,16,512]{2,1,0:T(8,128)(2,1)} %get-tuple-element.21.masked_ref) | copy-start | bytes 393220
  29.1 1.7 %copy-start.4 = (bf16[4,16,512]{2,1,0:T(8,128)(2,1)S(1)}, bf16[4,16,512]{2,1,0:T(8,128)(2,1)}, u32[]{:S(2)}) copy-start(bf16[4,16,512]{2,1,0:T(8,128)(2,1)} %get-tuple-element.26.kept_in) | copy-start | bytes 196612
  71.8 16.5 %all-to-all-start.4 = ((bf16[32,7,8,128]{3,2,1,0:T(8,128)(2,1)}), bf16[32,7,8,128]{3,2,1,0:T(8,128)(2,1)S(1)}, u32[]{:S(2)}, u32[]{:S(2)}) async-start(bf16[32,7,8,128]{3,2,1,0:T(8,128)(2,1)} %shard_map.93), calls=%async_computation.4 | async-start | bytes 917504 | tf_op jit(solution)/shard_map/all_to_all | solution.py:508
  77.5 8.4 %collective-permute-start.2 = (bf16[4,32,512]{2,1,0:T(8,128)(2,1)S(1)}, bf16[4,32,512]{2,1,0:T(8,128)(2,1)S(1)}, u32[]{:S(2)}, u32[]{:S(2)}) collective-permute-start(bf16[4,32,512]{2,1,0:T(8,128)(2,1)S(1)} %get-tuple-element.31), channel_id=1, source_target_pairs={{0,4},{1,5},{4,8},{5,9},{6,2},{7,3},{8,12},{9,13},{10,6},{11,7},{1... | collective-permute-start | bytes 393224 | tf_op jit(solution)/shard_map/ppermute | solution.py:522
  79.8 5.9 %collective-permute-start.3 = (bf16[2,32,512]{2,1,0:T(8,128)(2,1)S(1)}, bf16[2,32,512]{2,1,0:T(8,128)(2,1)S(1)}, u32[]{:S(2)}, u32[]{:S(2)}) collective-permute-start(bf16[2,32,512]{2,1,0:T(8,128)(2,1)S(1)} %get-tuple-element.32), channel_id=1, source_target_pairs={{2,6},{3,7},{4,0},{5,1},{6,10},{7,11},{8,4},{9,5},{10,14},{11,15},... | collective-permute-start | bytes 196616 | tf_op jit(solution)/shard_map/ppermute | solution.py:522

commit v9 on v6

--- a/solution.py
+++ b/solution.py
@@ -121,16 +121,18 @@
     copies[0].wait()
     occupied = spread(occ_ref)
     copies[1].wait()
-    copies[2].wait()
     for x in range(EDGE):
         both = []
         for brick in range(2):
-            wide[brick, x * EDGE : (x + 1) * EDGE, :] = x_ref[brick, x].astype(F32)
             at = (2 * x + brick) * EDGE
             piece = g_ref[brick, x].astype(F32) * occupied[at : at + EDGE]
             wide[2 + brick, x * EDGE : (x + 1) * EDGE, :] = piece
             both.append(piece)
         masked_ref[x] = jnp.concatenate(both, axis=0).astype(BF16)
+    copies[2].wait()
+    for brick in range(2):
+        for x in range(EDGE):
+            wide[brick, x * EDGE : (x + 1) * EDGE, :] = x_ref[brick, x].astype(F32)
     copies[3].wait()
     for brick in range(2):
         first = face_values(wide, brick)

time: 90.7 us -> 90.7 us (level)
  no operation moved by 1% of the time
where the time goes in v9:
time: 90.7 us; the launch traced here: 89.7 us
  blocking collectives  49.7 us (55%)
  starting transfers between devices  24.6 us (27%)
  Pallas kernels  10.7 us (12%)
  waiting for transfers between devices  2.94 us (3%)
  local copies, waits for them, and re-layouts  0.98 us (1%)
    all_to_all x3, blocking collectives, swap(): lax.all_to_all(value, AXES, 0, 0, axis_index_groups=members, tiled=True)  36.2 us
    ppermute x4, starting transfers between devices, send_on(): lax.ppermute(value, AXES, [(i, j) for i, j in way if 0 <= j < devices])  18.9 us
    all_to_all x1, blocking collectives, per_device(): sums = lax.all_to_all(sums, 'grp', 0, 0, tiled=True)  13.4 us
    pallas_call x10, Pallas kernels, call(): pl.pallas_call(kernel, out_shape=[jax.ShapeDtypeStruct(shape, kind) for s...  10.7 us
    all_to_all x1, starting transfers between devices, swap(): lax.all_to_all(value, AXES, 0, 0, axis_index_groups=members, tiled=True)  5.7 us
    ppermute x4, waiting for transfers between devices, send_on(): lax.ppermute(value, AXES, [(i, j) for i, j in way if 0 <= j < devices])  2.94 us
  transfers between devices with their start and end apart: 5, of which 4 were waited for; matrix products, arithmetic and copies ran while one was open for 1% of the time, Pallas kernels for 3%

profile of v9, /device:TPU:1, one launch (start us, length us, event | category | flops | bytes accessed | tf_op | source)
XLA Modules:
  0.0 89.7 jit_solution(13147529335717482718)
XLA Ops:
  0.6 2.3 %shard_map.86 = (bf16[4,128,512]{2,1,0:T(8,128)(2,1)}, bf16[4,16,512]{2,1,0:T(8,128)(2,1)}, bf16[8,16,512]{2,1,0:T(8,128)(2,1)}) custom-call(s32[1]{0:T(128)} %bitcast.me_ref, s32[2,26]{1,0:T(2,128)} %nb_hbm.1, bf16[2,8,8,512]{3,2,1,0:T(8,128)(2,1)} %x_ref.1, bf16[2,8,8,512]{3,2,1,0:T(8,128)(2,1)} %g_hbm.1, s32[2,8,64]{2,1,0:T(8,128)} %occ_hbm.1), custom_call_target="tpu_custom_call" | custom-call | bytes 524288 | tf_op jit(solution)/shard_map/pallas_call | solution.py:461
  3.0 12.9 %all_to_all.25.near_ref = bf16[4,128,512]{2,1,0:T(8,128)(2,1)S(1)} all-to-all(bf16[4,128,512]{2,1,0:T(8,128)(2,1)} %get-tuple-element.23), channel_id=1, replica_groups={{0,1,2,3},{4,5,6,7},{8,9,10,11},{12,13,14,15},{16,17,18,19},{20,21,22,2..., dimensions={0} | all-to-all | bytes 1048576 | tf_op jit(solution)/shard_map/all_to_all | solution.py:491
  15.9 4.4 %collective-permute-start = (bf16[4,64,512]{2,1,0:T(8,128)(2,1)S(1)}, bf16[4,64,512]{2,1,0:T(8,128)(2,1)S(1)}, u32[]{:S(2)}, u32[]{:S(2)}) collective-permute-start(bf16[4,64,512]{2,1,0:T(8,128)(2,1)S(1)} %get-tuple-element.24), channel_id=1, source_target_pairs={{0,4},{1,5},{4,8},{5,9},{6,2},{7,3},{8,12},{9,13},{10,6},{11,7},{1... | collective-permute-start | bytes 786440 | tf_op jit(solution)/shard_map/ppermute | solution.py:505
  20.3 0.0 copy-start.6
  20.3 7.8 %collective-permute-start.1 = (bf16[2,64,512]{2,1,0:T(8,128)(2,1)S(1)}, bf16[2,64,512]{2,1,0:T(8,128)(2,1)S(1)}, u32[]{:S(2)}, u32[]{:S(2)}) collective-permute-start(bf16[2,64,512]{2,1,0:T(8,128)(2,1)S(1)} %get-tuple-element.25), channel_id=1, source_target_pairs={{2,6},{3,7},{4,0},{5,1},{6,10},{7,11},{8,4},{9,5},{10,14},{11,15},... | collective-permute-start | bytes 393224 | tf_op jit(solution)/shard_map/ppermute | solution.py:505
  28.0 0.0 copy-done.5
  28.1 0.3 copy.9.first_ref
  28.3 0.0 copy-done.6
  28.3 0.0 copy-start.1
  28.3 0.0 copy-start.2
  28.4 0.3 copy.10.second_ref
  28.6 0.4 copy-done.1
  29.0 0.0 copy-done.2
  29.0 0.4 shard_map.85
  29.5 0.5 collective-permute-done.1.shorter_ref
  30.0 0.8 collective-permute-done.longer_ref
  30.8 0.0 copy-done
  30.8 0.0 copy-done.3
  30.8 3.4 %shard_map.88 = (bf16[8,16,512]{2,1,0:T(8,128)(2,1)S(1)}, bf16[4,176,512]{2,1,0:T(8,128)(2,1)S(1)}, f32[4,8,512]{2,1,0:T(8,128)S(1)}) custom-call(s32[1]{0:T(128)} %bitcast.me_ref, s32[2,26]{1,0:T(2,128)S(1)} %get-tuple-element.20.nb_ref, bf16[2,8,8,512]{3,2,1,0:T(8,128)(2,1)S(1)} %copy-done, bf16[8,16,512]{2,1,0:T(8,128)(2,1)S(1)} %copy-done.3, ...), custom_call_target="tpu_custom_call" | custom-call | flops 1073741824 | bytes 524288 | tf_op jit(solution)/shard_map/pallas_call | solution.py:461
  34.2 13.4 %all_to_all.26.near_ref.parts_ref = bf16[4,176,512]{2,1,0:T(8,128)(2,1)S(1)} all-to-all(bf16[4,176,512]{2,1,0:T(8,128)(2,1)S(1)} %get-tuple-element.30), channel_id=1, replica_groups={{0,1,2,3},{4,5,6,7},{8,9,10,11},{12,13,14,15},{16,17,18,19},{20,21,22,2..., dimensions={0} | all-to-all | bytes 1441792 | tf_op jit(solution)/shard_map/all_to_all | solution.py:491
  47.6 0.1 shard_map.91
  47.6 13.4 %all_to_all.27.parts_ref = bf16[8,7,8,128]{3,2,1,0:T(8,128)(2,1)S(1)} all-to-all(bf16[8,7,8,128]{3,2,1,0:T(8,128)(2,1)S(1)} %shard_map.91), channel_id=1, replica_groups=mesh['grp'=8,'dev'=32] {'grp'}, dimensions={0} | all-to-all | bytes 229376 | tf_op jit(solution)/shard_map/all_to_all | solution.py:564
  61.1 10.0 %all_to_all.28.parts_ref = bf16[8,7,8,128]{3,2,1,0:T(8,128)(2,1)S(1)} all-to-all(bf16[8,7,8,128]{3,2,1,0:T(8,128)(2,1)S(1)} %shard_map.92), channel_id=1, replica_groups={{0,4,8,12,16,20,24,28},{1,5,9,13,17,21,25,29},{2,6,10,14,18,22,26,30},{..., dimensions={0} | all-to-all | bytes 229376 | tf_op jit(solution)/shard_map/all_to_all | solution.py:491
  71.1 0.8 shard_map.93
  71.9 5.7 %all-to-all-start.4 = ((bf16[32,7,8,128]{3,2,1,0:T(8,128)(2,1)}), bf16[32,7,8,128]{3,2,1,0:T(8,128)(2,1)S(1)}, u32[]{:S(2)}, u32[]{:S(2)}) async-start(bf16[32,7,8,128]{3,2,1,0:T(8,128)(2,1)} %shard_map.93), calls=%async_computation.4 | async-start | bytes 917504 | tf_op jit(solution)/shard_map/all_to_all | solution.py:491
  77.6 2.2 %collective-permute-start.2 = (bf16[4,32,512]{2,1,0:T(8,128)(2,1)S(1)}, bf16[4,32,512]{2,1,0:T(8,128)(2,1)S(1)}, u32[]{:S(2)}, u32[]{:S(2)}) collective-permute-start(bf16[4,32,512]{2,1,0:T(8,128)(2,1)S(1)} %get-tuple-element.31), channel_id=1, source_target_pairs={{0,4},{1,5},{4,8},{5,9},{6,2},{7,3},{8,12},{9,13},{10,6},{11,7},{1... | collective-permute-start | bytes 393224 | tf_op jit(solution)/shard_map/ppermute | solution.py:505
  79.8 4.6 %collective-permute-start.3 = (bf16[2,32,512]{2,1,0:T(8,128)(2,1)S(1)}, bf16[2,32,512]{2,1,0:T(8,128)(2,1)S(1)}, u32[]{:S(2)}, u32[]{:S(2)}) collective-permute-start(bf16[2,32,512]{2,1,0:T(8,128)(2,1)S(1)} %get-tuple-element.32), channel_id=1, source_target_pairs={{2,6},{3,7},{4,0},{5,1},{6,10},{7,11},{8,4},{9,5},{10,14},{11,15},... | collective-permute-start | bytes 196616 | tf_op jit(solution)/shard_map/ppermute | solution.py:505
  84.4 1.3 %collective-permute-done.3.shorter_ref = bf16[2,32,512]{2,1,0:T(8,128)(2,1)S(1)} collective-permute-done((bf16[2,32,512]{2,1,0:T(8,128)(2,1)S(1)}, bf16[2,32,512]{2,1,0:T(8,128)(2,1)S(1)}, u32[]{:S(2)}, u32[]{:S(2)}) %collective-permute-start.3) | collective-permute-done | bytes 65568 | tf_op jit(solution)/shard_map/ppermute | solution.py:505
  85.7 0.3 collective-permute-done.2.longer_ref
  86.1 2.4 %shard_map.90 = bf16[2,8,8,512]{3,2,1,0:T(8,128)(2,1)} custom-call(s32[1]{0:T(128)} %bitcast.me_ref, s32[2,26]{1,0:T(2,128)S(1)} %get-tuple-element.20.nb_ref, bf16[8,16,512]{2,1,0:T(8,128)(2,1)S(1)} %get-tuple-element.29.grads_ref, f32[128,512]{1,0:T(8,128)S(1)} %get-tuple-element.22.occupied_ref, bf16[4,176,512]{2,1,0:T(8,128)(2,1)S(1)} %all_to_all.26.near_ref.parts_ref, ...), custom_call_target="tpu_custom_call" | custom-call | flops 268435456 | bytes 524288 | tf_op jit(solution)/shard_map/pallas_call | solution.py:461
  88.4 0.0 all-to-all-done.4.parts_ref
  88.4 1.2 %shard_map.94 = (f32[64,1728]{1,0:T(8,128)}, f32[64,1728]{1,0:T(8,128)}) custom-call(bf16[32,7,8,128]{3,2,1,0:T(8,128)(2,1)S(1)} %all-to-all-done.4.parts_ref), custom_call_target="tpu_custom_call" | custom-call | bytes 524288 | tf_op jit(solution)/shard_map/pallas_call | solution.py:461
  (8 shorter events, 0.1 us)
Async XLA Ops:
  15.8 12.2 %copy-start.5 = (bf16[1728,64]{0,1:T(8,128)(2,1)S(1)}, bf16[1728,64]{0,1:T(8,128)(2,1)}, u32[]{:S(2)}) copy-start(bf16[1728,64]{0,1:T(8,128)(2,1)} %param.9) | copy-start | bytes 663556
  15.9 14.9 %collective-permute-start = (bf16[4,64,512]{2,1,0:T(8,128)(2,1)S(1)}, bf16[4,64,512]{2,1,0:T(8,128)(2,1)S(1)}, u32[]{:S(2)}, u32[]{:S(2)}) collective-permute-start(bf16[4,64,512]{2,1,0:T(8,128)(2,1)S(1)} %get-tuple-element.24), channel_id=1, source_target_pairs={{0,4},{1,5},{4,8},{5,9},{6,2},{7,3},{8,12},{9,13},{10,6},{11,7},{1... | collective-permute-start | bytes 786440 | tf_op jit(solution)/shard_map/ppermute | solution.py:505
  20.3 8.1 %copy-start.6 = (bf16[1728,64]{0,1:T(8,128)(2,1)S(1)}, bf16[1728,64]{0,1:T(8,128)(2,1)}, u32[]{:S(2)}) copy-start(bf16[1728,64]{0,1:T(8,128)(2,1)} %param.10) | copy-start | bytes 663556
  20.3 9.7 %collective-permute-start.1 = (bf16[2,64,512]{2,1,0:T(8,128)(2,1)S(1)}, bf16[2,64,512]{2,1,0:T(8,128)(2,1)S(1)}, u32[]{:S(2)}, u32[]{:S(2)}) collective-permute-start(bf16[2,64,512]{2,1,0:T(8,128)(2,1)S(1)} %get-tuple-element.25), channel_id=1, source_target_pairs={{2,6},{3,7},{4,0},{5,1},{6,10},{7,11},{8,4},{9,5},{10,14},{11,15},... | collective-permute-start | bytes 393224 | tf_op jit(solution)/shard_map/ppermute | solution.py:505
  28.3 0.7 copy-start.1
  28.3 0.7 copy-start.2
  29.0 1.7 %copy-start = (bf16[2,8,8,512]{3,2,1,0:T(8,128)(2,1)S(1)}, bf16[2,8,8,512]{3,2,1,0:T(8,128)(2,1)}, u32[]{:S(2)}) copy-start(bf16[2,8,8,512]{3,2,1,0:T(8,128)(2,1)} %x_ref.1) | copy-start | bytes 393220
  29.0 1.7 %copy-start.3 = (bf16[8,16,512]{2,1,0:T(8,128)(2,1)S(1)}, bf16[8,16,512]{2,1,0:T(8,128)(2,1)}, u32[]{:S(2)}) copy-start(bf16[8,16,512]{2,1,0:T(8,128)(2,1)} %get-tuple-element.21.masked_ref) | copy-start | bytes 393220
  29.0 1.7 %copy-start.4 = (bf16[4,16,512]{2,1,0:T(8,128)(2,1)S(1)}, bf16[4,16,512]{2,1,0:T(8,128)(2,1)}, u32[]{:S(2)}) copy-start(bf16[4,16,512]{2,1,0:T(8,128)(2,1)} %get-tuple-element.26.kept_in) | copy-start | bytes 196612
  71.9 16.5 %all-to-all-start.4 = ((bf16[32,7,8,128]{3,2,1,0:T(8,128)(2,1)}), bf16[32,7,8,128]{3,2,1,0:T(8,128)(2,1)S(1)}, u32[]{:S(2)}, u32[]{:S(2)}) async-start(bf16[32,7,8,128]{3,2,1,0:T(8,128)(2,1)} %shard_map.93), calls=%async_computation.4 | async-start | bytes 917504 | tf_op jit(solution)/shard_map/all_to_all | solution.py:491
  77.6 8.4 %collective-permute-start.2 = (bf16[4,32,512]{2,1,0:T(8,128)(2,1)S(1)}, bf16[4,32,512]{2,1,0:T(8,128)(2,1)S(1)}, u32[]{:S(2)}, u32[]{:S(2)}) collective-permute-start(bf16[4,32,512]{2,1,0:T(8,128)(2,1)S(1)} %get-tuple-element.31), channel_id=1, source_target_pairs={{0,4},{1,5},{4,8},{5,9},{6,2},{7,3},{8,12},{9,13},{10,6},{11,7},{1... | collective-permute-start | bytes 393224 | tf_op jit(solution)/shard_map/ppermute | solution.py:505
  79.8 5.9 %collective-permute-start.3 = (bf16[2,32,512]{2,1,0:T(8,128)(2,1)S(1)}, bf16[2,32,512]{2,1,0:T(8,128)(2,1)S(1)}, u32[]{:S(2)}, u32[]{:S(2)}) collective-permute-start(bf16[2,32,512]{2,1,0:T(8,128)(2,1)S(1)} %get-tuple-element.32), channel_id=1, source_target_pairs={{2,6},{3,7},{4,0},{5,1},{6,10},{7,11},{8,4},{9,5},{10,14},{11,15},... | collective-permute-start | bytes 196616 | tf_op jit(solution)/shard_map/ppermute | solution.py:505
